TPU v7x, 256 devices: a whole 4x4x8 slice. The times are simulated.
256 devices in a mesh: pb: 16 (over z, y_lo), ka: 16 (over y_hi, x, core).
Axes of the slice: x: 4, y: 4 (y_hi: 2, y_lo: 2; y = y_hi * 2 + y_lo), z: 8, core: 2. Of those that a mesh axis runs over, the one named last changes fastest.
Arguments:
- queries: bfloat16 [32768, 512], P('pb'), may hold values from -8 to 8
- point_order: int32 [16, 2048], P('pb'), may hold values from 0 to 2047, each once within a row
- keys: bfloat16 [32, 128, 512], P('ka'), may hold values from -4 to 4
- values: bfloat16 [32, 128, 512], P('ka'), may hold values from -6 to 6
- pair_counts: int32 [16, 16], P('pb'), may hold values from 1 to 31, as said below
- pair_keys: int32 [16, 256], P('pb'), may hold values from 0 to 31, as said below
- out_grad: bfloat16 [256, 128, 512], P('pb'), may hold values from -6 to 6
Outputs:
- attended: bfloat16 [256, 128, 512], P(('pb', 'ka'))
- query_grad: float32 [256, 128, 512], P(('pb', 'ka'))
- key_grad: float32 [32, 128, 512], P('ka', 'pb')
- value_grad: float32 [32, 128, 512], P('ka', 'pb')
Inputs may be any that keep to these rules, and one draw needn't show every extreme that they name: `pair_counts`: every query block has between 1 and 31 pairs, some query block of every slab exactly 31; the counts of a slab add up to 256. `pair_keys`: the key blocks of one query block are distinct and ascending.
All inputs are finite; a program needn't handle non-finite values.
Results may differ from a plain program's by a relative error of at most 0.02.
Values may be sent and summed in bfloat16 or wider, within the bound.
A program may use at most 192 MiB of HBM per device.

v0:
```python
import jax
import jax.numpy as jnp
from jax import lax
from jax.sharding import PartitionSpec as P

H = 8
HD = 64


GROUP = 4
FLOOR = -1e30


def tile_scores(query_tiles, key_tiles):
    query_heads = query_tiles.reshape(query_tiles.shape[0], query_tiles.shape[1], H, HD)
    key_heads = key_tiles.reshape(key_tiles.shape[0], key_tiles.shape[1], H, HD)
    return jnp.einsum(
        "gqhd,gkhd->ghqk", query_heads, key_heads, preferred_element_type=jnp.float32
    ) * HD ** (-0.5)


def slot_groups(query_ids, key_ids, usable):
    slot_total = query_ids.shape[0]
    turn_count = -(-slot_total // GROUP)
    surplus = turn_count * GROUP - slot_total

    def padded(entries, filler):
        return jnp.concatenate([entries, jnp.full((surplus,), filler, entries.dtype)]).reshape(
            turn_count, GROUP
        )

    return (padded(query_ids, 0), padded(key_ids, 0), padded(usable, False))


def row_maxima(query_set, key_panel, groups, target_count):

    def row_advance(running, inputs):
        query_ids, key_ids, usable = inputs
        scores = tile_scores(query_set[query_ids], key_panel[key_ids])
        top_rows = jnp.where(usable[:, None, None], jnp.max(scores, axis=3), FLOOR)
        return (running.at[query_ids].max(top_rows), scores)

    start = jnp.full((target_count, H, query_set.shape[1]), FLOOR, jnp.float32)
    return lax.scan(row_advance, start, groups)


def softmax_sums(value_panel, groups, score_stack, maxima):
    target_count, _, block_rows = maxima.shape
    width = value_panel.shape[2]

    def softmax_advance(running, inputs):
        totals, weighted = running
        query_ids, key_ids, usable, scores = inputs
        probs = jnp.where(
            usable[:, None, None, None], jnp.exp(scores - maxima[query_ids][..., None]), 0.0
        )
        value_heads = value_panel[key_ids].reshape(GROUP, block_rows, H, HD)
        mixed = jnp.einsum(
            "ghqk,gkhd->gqhd",
            probs.astype(jnp.bfloat16),
            value_heads,
            preferred_element_type=jnp.float32,
        )
        totals = totals.at[query_ids].add(jnp.sum(probs, axis=3))
        weighted = weighted.at[query_ids].add(mixed.reshape(GROUP, block_rows, width))
        return ((totals, weighted), None)

    start = (
        jnp.zeros((target_count, H, block_rows), jnp.float32),
        jnp.zeros((target_count, block_rows, width), jnp.float32),
    )
    result, _ = lax.scan(softmax_advance, start, groups + (score_stack,))
    return result


def finish(weighted, totals, maxima, grad_set):
    target_count, block_rows, width = weighted.shape
    scaled = (
        weighted.reshape(target_count, block_rows, H, HD)
        / jnp.transpose(totals, (0, 2, 1))[..., None]
    )
    attended = scaled.reshape(target_count, block_rows, width).astype(jnp.bfloat16)
    log_sum = maxima + jnp.log(totals)
    product = (grad_set.astype(jnp.float32) * attended.astype(jnp.float32)).reshape(
        target_count, block_rows, H, HD
    )
    delta = jnp.transpose(jnp.sum(product, axis=3), (0, 2, 1))
    return (attended, log_sum, delta)


def gradients(query_set, grad_set, key_panel, value_panel, groups, score_stack, log_sum, delta):
    target_count, block_rows, width = query_set.shape
    key_total = key_panel.shape[0]

    def gradients_advance(running, inputs):
        query_grad, key_grad, value_grad = running
        query_ids, key_ids, usable, scores = inputs
        query_heads = query_set[query_ids].reshape(GROUP, block_rows, H, HD)
        key_heads = key_panel[key_ids].reshape(GROUP, block_rows, H, HD)
        grad_heads = grad_set[query_ids].reshape(GROUP, block_rows, H, HD)
        value_heads = value_panel[key_ids].reshape(GROUP, block_rows, H, HD)
        probs = jnp.where(
            usable[:, None, None, None], jnp.exp(scores - log_sum[query_ids][..., None]), 0.0
        )
        value_part = jnp.einsum(
            "ghqk,gqhd->gkhd",
            probs.astype(jnp.bfloat16),
            grad_heads,
            preferred_element_type=jnp.float32,
        )
        prob_grad = jnp.einsum(
            "gqhd,gkhd->ghqk", grad_heads, value_heads, preferred_element_type=jnp.float32
        )
        score_grad = probs * (prob_grad - delta[query_ids][..., None]) * HD ** (-0.5)
        query_part = jnp.einsum(
            "ghqk,gkhd->gqhd",
            score_grad,
            key_heads.astype(jnp.float32),
            preferred_element_type=jnp.float32,
            precision=lax.Precision.HIGHEST,
        )
        key_part = jnp.einsum(
            "ghqk,gqhd->gkhd",
            score_grad,
            query_heads.astype(jnp.float32),
            preferred_element_type=jnp.float32,
            precision=lax.Precision.HIGHEST,
        )
        query_grad = query_grad.at[query_ids].add(query_part.reshape(GROUP, block_rows, width))
        key_grad = key_grad.at[key_ids].add(key_part.reshape(GROUP, block_rows, width))
        value_grad = value_grad.at[key_ids].add(value_part.reshape(GROUP, block_rows, width))
        return ((query_grad, key_grad, value_grad), None)

    start = (
        jnp.zeros((target_count, block_rows, width), jnp.float32),
        jnp.zeros((key_total, block_rows, width), jnp.float32),
        jnp.zeros((key_total, block_rows, width), jnp.float32),
    )
    result, _ = lax.scan(gradients_advance, start, groups + (score_stack,))
    return result


def local(queries, point_order, keys, values, pair_counts, pair_keys, out_grad):
    slab_blocks, block_rows, width = out_grad.shape
    axis_count = lax.axis_size("ka")
    position = lax.axis_index("ka")
    owned = slab_blocks // axis_count
    serial = jnp.take(queries, point_order[0], axis=0).reshape(slab_blocks, block_rows, width)
    key_panel, value_panel = (
        lax.all_gather(keys, "ka", axis=0, tiled=True),
        lax.all_gather(values, "ka", axis=0, tiled=True),
    )
    counts = pair_counts[0]
    listing = pair_keys[0]
    ends = jnp.cumsum(counts)
    starts = ends - counts
    mean_pairs = listing.shape[0] // slab_blocks
    own_grad = lax.dynamic_slice_in_dim(out_grad, position * owned, owned)
    capacity = 2 * mean_pairs - 1
    own_blocks = position * owned + jnp.arange(owned, dtype=jnp.int32)
    local_block = jnp.repeat(jnp.arange(owned, dtype=jnp.int32), capacity)
    offset = jnp.tile(jnp.arange(capacity, dtype=jnp.int32), owned)
    usable = offset < counts[own_blocks][local_block]
    entry = jnp.minimum(starts[own_blocks][local_block] + offset, listing.shape[0] - 1)
    key_ids = listing[entry]
    query_set = lax.dynamic_slice_in_dim(serial, position * owned, owned)
    groups = slot_groups(local_block, key_ids, usable)
    maxima, score_stack = row_maxima(query_set, key_panel, groups, owned)
    totals, weighted = softmax_sums(value_panel, groups, score_stack, maxima)
    attended, log_sum, delta = finish(weighted, totals, maxima, own_grad)
    query_grad, key_grad, value_grad = gradients(
        query_set, own_grad, key_panel, value_panel, groups, score_stack, log_sum, delta
    )
    key_grad, value_grad = (
        lax.psum_scatter(key_grad, "ka", scatter_dimension=0, tiled=True),
        lax.psum_scatter(value_grad, "ka", scatter_dimension=0, tiled=True),
    )
    key_grad, value_grad = (
        lax.psum_scatter(key_grad, "pb", scatter_dimension=1, tiled=True),
        lax.psum_scatter(value_grad, "pb", scatter_dimension=1, tiled=True),
    )
    return (attended, query_grad, key_grad, value_grad)


def solution(mesh):
    placed = (
        P("pb", None),
        P("pb", None),
        P("ka", None, None),
        P("ka", None, None),
        P("pb", None),
        P("pb", None),
        P("pb", None, None),
    )
    return jax.shard_map(
        local,
        mesh=mesh,
        in_specs=placed,
        out_specs=(
            P(("pb", "ka"), None, None),
            P(("pb", "ka"), None, None),
            P("ka", "pb", None),
            P("ka", "pb", None),
        ),
        check_vma=False,
    )
```

profile of v0, /device:TPU:2, one launch (start us, length us, event | category | flops | bytes accessed | tf_op | source)
XLA Modules:
  0.0 893.4 jit_solution(17091614291286306278)
XLA Ops:
  13.1 9.2 %gather_fusion.4 = bf16[2048,512]{1,0:T(8,128)(2,1)} fusion(bf16[2048,512]{1,0:T(8,128)(2,1)S(1)} %copy-done, s32[2048]{0:T(1024)S(1)} %broadcast_clamp_fusion), kind=kCustom, calls=%fused_computation.4 | custom fusion | bytes 4202496 | tf_op jit(solution)/shard_map/jit(_take)/gather | solution.py:148
  26.2 48.4 %all-gather.3.cloned.1.call-done = bf16[32,128,512]{2,1,0:T(8,128)(2,1)} async-done(((bf16[2,128,512]{2,1,0:T(8,128)(2,1)}), bf16[32,128,512]{2,1,0:T(8,128)(2,1)}) %all-gather.3.cloned.1.call-update) | async-done | bytes 4194320 | tf_op jit(solution)/shard_map/all_gather | solution.py:150
  74.6 53.5 %while.40 = (s32[]{:T(128)}, f32[1,8,128]{2,1,0:T(8,128)S(1)}, f32[8,4,8,128,128]{3,4,2,1,0:T(8,128)}, pred[8,4]{1,0:T(8,128)(4,1)S(1)}, bf16[1,128,512]{1,2,0:T...) while((s32[]{:T(128)}, f32[1,8,128]{2,1,0:T(8,128)S(1)}, ...), condition=%wide.region_4.5_spmd, body=%wide.region_1.0_spmd.sunk | while | flops 68686864 | bytes 10195169 | solution.py:44
  128.1 9.3 %all-gather.5.cloned.1.call-done = bf16[32,128,512]{2,1,0:T(8,128)(2,1)} async-done(((bf16[2,128,512]{2,1,0:T(8,128)(2,1)}), bf16[32,128,512]{2,1,0:T(8,128)(2,1)}) %all-gather.5.cloned.1.call-update) | async-done | bytes 4194320 | tf_op jit(solution)/shard_map/all_gather | solution.py:151
  137.4 117.3 %while.41 = (s32[]{:T(128)}, f32[1,8,128]{2,1,0:T(8,128)S(1)}, f32[1,128,512]{2,1,0:T(8,128)S(1)}, pred[8,4]{1,0:T(8,128)(4,1)S(1)}, f32[8,4,8,128,128]{3,4,2,1,...) while((s32[]{:T(128)}, f32[1,8,128]{2,1,0:T(8,128)S(1)}, ...), condition=%wide.region_9.10_spmd, body=%wide.region_5.9_spmd.sunk | while | flops 70517776 | bytes 21574196 | solution.py:72
  256.5 4.3 broadcast.208
  260.8 4.3 broadcast.208.clone
  265.1 255.0 %while.42 = (s32[]{:T(128)}, f32[1,128,512]{2,1,0:T(8,128)S(1)}, f32[32,128,512]{2,1,0:T(8,128)}, f32[32,128,512]{2,1,0:T(8,128)}, s32[8,4]{1,0:T(8,128)}, /*ind...) while((s32[]{:T(128)}, f32[1,128,512]{2,1,0:T(8,128)S(1)}, ...), condition=%wide.region_15.16_spmd, body=%wide.region_11.15_spmd.sunk | while | flops 944505856 | bytes 38027628 | solution.py:139
  283.0 3.3 fusion.82
  293.8 3.2 scatter_fusion.5
  314.9 3.3 fusion.82
  319.8 3.2 scatter_fusion.4
  346.8 3.3 fusion.82
  378.7 3.3 fusion.82
  410.5 3.3 fusion.82
  421.3 3.2 scatter_fusion.5
  442.4 3.3 fusion.82
  474.2 3.3 fusion.82
  506.1 3.3 fusion.82
  517.0 3.2 scatter_fusion.5
  521.5 107.4 %reduce-scatter.5.cloned.1.call-done = f32[2,128,512]{2,1,0:T(8,128)} async-done(((f32[32,128,512]{2,1,0:T(8,128)}), f32[2,128,512]{2,1,0:T(8,128)}) %reduce-scatter.5.cloned.1.call-update) | async-done | bytes 524304 | tf_op jit(solution)/shard_map/reduce_scatter | solution.py:175
  628.9 113.5 %reduce-scatter.9.cloned.1.call-done = f32[2,128,512]{2,1,0:T(8,128)} async-done(((f32[32,128,512]{2,1,0:T(8,128)}), f32[2,128,512]{2,1,0:T(8,128)}) %reduce-scatter.9.cloned.1.call-update) | async-done | bytes 524304 | tf_op jit(solution)/shard_map/reduce_scatter | solution.py:176
  743.3 71.5 %reduce-scatter.7.cloned.1.call-done = f32[2,8,512]{2,1,0:T(8,128)} async-done(((f32[2,128,512]{2,1,0:T(8,128)}), f32[2,8,512]{2,1,0:T(8,128)}) %reduce-scatter.7.cloned.1.call-update) | async-done | bytes 32784 | tf_op jit(solution)/shard_map/reduce_scatter | solution.py:179
  814.8 71.8 %reduce-scatter.11.cloned.1.call-done = f32[2,8,512]{2,1,0:T(8,128)} async-done(((f32[2,128,512]{2,1,0:T(8,128)}), f32[2,8,512]{2,1,0:T(8,128)}) %reduce-scatter.11.cloned.1.call-update) | async-done | bytes 32784 | tf_op jit(solution)/shard_map/reduce_scatter | solution.py:180
  (451 shorter events, 398.6 us)
Async XLA Ops:
  7.2 5.9 copy-start
  7.2 67.4 %all-gather.3.cloned.1.call-start = ((), (), s32[]{:S(2)}) async-start(), calls=%async_computation.4 | async-start | bytes 4456448 | tf_op jit(solution)/shard_map/all_gather | solution.py:150
  7.9 129.5 %all-gather.5.cloned.1.call-start = ((), (), s32[]{:S(2)}) async-start(), calls=%async_computation.5 | async-start | bytes 4456448 | tf_op jit(solution)/shard_map/all_gather | solution.py:151
  8.7 620.2 %reduce-scatter.5.cloned.1.call-start = ((), (), s32[]{:S(2)}) async-start(), calls=%async_computation.6 | async-start | bytes 8912896 | tf_op jit(solution)/shard_map/reduce_scatter | solution.py:175
  13.1 10.2 %copy-start.7 = (s32[1,2048]{1,0:T(1,128)S(1)}, s32[1,2048]{1,0:T(1,128)}, u32[]{:S(2)}) copy-start(s32[1,2048]{1,0:T(1,128)} %param.14) | copy-start | bytes 24580
  13.1 10.3 %copy-start.8 = (s32[1,16]{1,0:T(1,128)S(1)}, s32[1,16]{1,0:T(1,128)}, u32[]{:S(2)}) copy-start(s32[1,16]{1,0:T(1,128)} %param.17) | copy-start | bytes 196
  13.1 11.7 %copy-start.2 = (s32[1,256]{1,0:T(1,128)S(1)}, s32[1,256]{1,0:T(1,128)}, u32[]{:S(2)}) copy-start(s32[1,256]{1,0:T(1,128)} %param.18) | copy-start | bytes 3076
  137.4 5.1 copy-start.9
  152.1 5.1 copy-start.9
  166.7 5.1 copy-start.9
  181.4 5.1 copy-start.9
  196.1 5.1 copy-start.9
  210.7 5.1 copy-start.9
  225.4 5.1 copy-start.9
  240.0 5.1 copy-start.9
  260.8 4.3 copy-start.4
  293.8 3.3 copy-start.5
  421.3 3.2 copy-start.5
  516.9 3.2 copy-start.5
  520.9 221.6 %reduce-scatter.9.cloned.1.call-start = ((), (), s32[]{:S(2)}) async-start(), calls=%async_computation.8 | async-start | bytes 8912896 | tf_op jit(solution)/shard_map/reduce_scatter | solution.py:176
  520.9 221.6 %copy-start.6 = (bf16[1,128,512]{1,2,0:T(8,128)(2,1)S(1)}, bf16[1,128,512]{1,2,0:T(8,128)(2,1)}, u32[]{:S(2)}) copy-start(bf16[1,128,512]{1,2,0:T(8,128)(2,1)} %get-tuple-element.297) | copy-start | bytes 393220
  521.4 365.2 %copy-start.1 = (bf16[2048,512]{1,0:T(8,128)(2,1)S(1)}, bf16[2048,512]{1,0:T(8,128)(2,1)}, u32[]{:S(2)}) copy-start(bf16[2048,512]{1,0:T(8,128)(2,1)} %param.13) | copy-start | bytes 6291460
  521.4 293.4 %reduce-scatter.7.cloned.1.call-start = ((), (), s32[]{:S(2)}) async-start(), calls=%async_computation.7 | async-start | bytes 557056 | tf_op jit(solution)/shard_map/reduce_scatter | solution.py:179
  628.9 257.7 %reduce-scatter.11.cloned.1.call-start = ((), (), s32[]{:S(2)}) async-start(), calls=%async_computation.9 | async-start | bytes 557056 | tf_op jit(solution)/shard_map/reduce_scatter | solution.py:180
  (15 other events, 27.4 us)
Sparse Core Ops, SparseCore 0:
  10.7 63.8 all-gather.2
  77.3 59.9 all-gather.4
  520.3 108.5 reduce-scatter.4
  633.3 109.0 reduce-scatter.8
  745.4 69.3 reduce-scatter.6
  817.9 68.6 reduce-scatter.10
where the time goes:
time: 899 us; the launch traced here: 893 us
  waiting for transfers between devices  424 us (47%)
  local copies, waits for them, and re-layouts  222 us (25%)
  other arithmetic  129 us (14%)
  matrix products  103 us (11%)
  between operations  14.3 us (2%)
    reduce_scatter x1, waiting for transfers between devices, local(): lax.psum_scatter(value_grad, 'ka', scatter_dimension=0, tiled=True)  114 us
    reduce_scatter x1, waiting for transfers between devices, local(): lax.psum_scatter(key_grad, 'ka', scatter_dimension=0, tiled=True)  107 us
    reduce_scatter x1, waiting for transfers between devices, local(): lax.psum_scatter(value_grad, 'pb', scatter_dimension=1, tiled=True)  71.8 us
    reduce_scatter x1, waiting for transfers between devices, local(): lax.psum_scatter(key_grad, 'pb', scatter_dimension=1, tiled=True)  71.5 us
    all_gather x1, waiting for transfers between devices, local(): lax.all_gather(keys, 'ka', axis=0, tiled=True)  48.4 us
    dynamic_slice x16, local copies, waits for them, and re-layouts, softmax_sums(): result, _ = lax.scan(softmax_advance, start, groups + (score_stack,))  40.7 us
    gather x16, local copies, waits for them, and re-layouts, gradients_advance(): value_heads = value_panel[key_ids].reshape(GROUP, block_rows, H, HD)  30.3 us
    gather x16, local copies, waits for them, and re-layouts, softmax_advance(): value_heads = value_panel[key_ids].reshape(GROUP, block_rows, H, HD)  30.1 us
  transfers between devices with their start and end apart: 6, of which 6 were waited for; matrix products, arithmetic and copies ran while one was open for 8% of the time, Pallas kernels for 0%

commit v1 on v0

v1 whole, which is shorter than its diff:
```python
import functools
import math

import jax
import jax.numpy as jnp
from jax import lax
from jax.experimental import pallas as pl
from jax.experimental.pallas import tpu as pltpu
from jax.sharding import PartitionSpec as P

H = 8
HD = 64
D = 512
BS = 128
NP = 16
NX = 4
NY = 2
NM = NX * NY
NC = 4
QS = NM * BS
KS = 4 * BS
PQ = 2 * BS
SCALE = HD ** -0.5
C2 = SCALE * math.log2(math.e)
FAR = 1e30
MESH = pl.DeviceIdType.MESH
BF = jnp.bfloat16
F32 = jnp.float32

NN = (((1,), (0,)), ((), ()))
NT = (((1,), (1,)), ((), ()))


def dot(a, b, dims=NN):
    return lax.dot_general(a, b, dims, preferred_element_type=F32)


def kernel(
    queries,
    order,
    keys,
    values,
    counts,
    listing,
    out_grad,
    att_out,
    qg_out,
    kg_out,
    vg_out,
    qbuf,
    serial,
    og,
    kv,
    use,
    q_t,
    og_t,
    wq_t,
    wog_t,
    probs,
    dps,
    a_keep,
    m_keep,
    d_keep,
    stat_own,
    stat_got,
    aq,
    x1_got,
    x2_got,
    y_keep,
    y_send,
    y_got,
    c_keep,
    c_send,
    c_got,
    z_send,
    z_got,
    load_sem,
    kv_sem,
    stat_sem,
    x1_sem,
    x2_sem,
    y_sem,
    c_sem,
    z_sem,
):
    pb = lax.axis_index("pb")
    ka = lax.axis_index("ka")
    core = lax.rem(ka, 2)
    chip = ka // 2
    xi = lax.rem(chip, NX)
    yi = chip // NX
    xr = lax.rem(xi + 1, NX)
    xl = lax.rem(xi + NX - 1, NX)
    xo = lax.rem(xi + 2, NX)
    yo = 1 - yi

    def at_ka(y, x, c):
        return {"ka": (y * NX + x) * 2 + c}

    right, left = at_ka(yi, xr, core), at_ka(yi, xl, core)
    across = at_ka(yo, xi, core)
    mate = {"ka": chip * 2 + (1 - core)}

    def peer(d):
        return {"ka": lax.rem(chip + d, NM) * 2 + core}

    def slab(d):
        return {"pb": lax.rem(pb + d, NP)}

    def send(src, dst, send_sem, recv_sem, device):
        return pltpu.make_async_remote_copy(
            src_ref=src, dst_ref=dst, send_sem=send_sem, recv_sem=recv_sem,
            device_id=device, device_id_type=MESH,
        )

    barrier = pltpu.get_barrier_semaphore()
    pl.semaphore_signal(barrier, inc=1, device_id=mate, device_id_type=MESH)

    def hello_ka(d, _):
        pl.semaphore_signal(barrier, inc=1, device_id=peer(d), device_id_type=MESH)
        return 0

    def hello_pb(d, _):
        pl.semaphore_signal(barrier, inc=1, device_id=slab(d), device_id_type=MESH)
        return 0

    lax.fori_loop(1, NM, hello_ka, 0)
    lax.fori_loop(1, NP, hello_pb, 0)

    load_q = pltpu.make_async_copy(queries, qbuf, load_sem.at[0])
    load_q.start()
    own2 = pl.ds(2 * core, 2)
    load_k = pltpu.make_async_copy(keys, kv.at[0, own2], load_sem.at[1])
    load_v = pltpu.make_async_copy(values, kv.at[1, own2], load_sem.at[2])
    load_k.start()
    load_v.start()
    load_og = []
    for b in range(NM):
        cp = pltpu.make_async_copy(out_grad.at[2 * b + core], og.at[b], load_sem.at[3 + b])
        cp.start()
        load_og.append(cp)

    cb = jnp.broadcast_to(counts[...].astype(F32), (16, 16))
    i0 = lax.broadcasted_iota(jnp.int32, (16, 16), 0)
    i1 = lax.broadcasted_iota(jnp.int32, (16, 16), 1)
    starts = jnp.sum(jnp.where(i1 < i0, cb, 0.0), axis=1, keepdims=True)
    sizes = jnp.sum(jnp.where(i1 == i0, cb, 0.0), axis=1, keepdims=True)
    slot = lax.broadcasted_iota(jnp.int32, (16, 256), 1).astype(F32)
    inside = jnp.where((slot >= starts) & (slot < starts + sizes), 1.0, 0.0)
    row = lax.broadcasted_iota(jnp.int32, (8, 256), 0) + 4 * chip
    named = jnp.where(jnp.broadcast_to(listing[...], (8, 256)) == row, 1.0, 0.0)
    joined = dot(named.astype(BF), inside.astype(BF), NT)
    e0 = lax.broadcasted_iota(jnp.int32, (16, QS), 0)
    e1 = lax.broadcasted_iota(jnp.int32, (16, QS), 1)
    spread = jnp.where(e0 == 2 * (e1 // BS) + core, 1.0, 0.0)
    use[...] = dot(joined.astype(BF), spread.astype(BF))

    zero_half = jnp.zeros((HD, QS), BF)
    for arr in (wq_t, wog_t):
        arr[HD:, :QS] = zero_half
        arr[:HD, QS:] = zero_half

    load_q.wait()

    def gather(b, _):
        at = pl.multiple_of((2 * b + core) * BS, BS)
        line = order[:, pl.ds(at, BS)]
        column = jnp.broadcast_to(line, (BS, BS)).T
        lanes = lax.broadcasted_iota(jnp.int32, (BS, BS), 1)
        picks = [
            jnp.where(column == lanes + n * BS, 1.0, 0.0).astype(BF) for n in range(16)
        ]
        pick = jnp.concatenate(picks, axis=1)
        serial[pl.ds(pl.multiple_of(b * BS, BS), BS), :] = dot(pick, qbuf[...]).astype(BF)
        return 0

    lax.fori_loop(0, 2, gather, 0)
    pl.semaphore_wait(barrier, 1 + (NM - 1) + (NP - 1))
    send_k = send(keys, kv.at[0, own2], kv_sem.at[0, 0], kv_sem.at[1, 0], mate)
    send_v = send(values, kv.at[1, own2], kv_sem.at[0, 1], kv_sem.at[1, 1], mate)
    send_k.start()
    send_v.start()
    lax.fori_loop(2, NM, gather, 0)
    load_k.wait()
    load_v.wait()
    for cp in load_og:
        cp.wait()
    send_k.wait()
    send_v.wait()

    def lanes_of(hp):
        return pl.ds(pl.multiple_of(hp * 2 * HD, 2 * HD), 2 * HD)

    def first(hp):
        par = lax.rem(hp, 2)
        cols = lanes_of(hp)
        k2 = kv[0, :, :, cols].reshape(KS, 2 * HD)
        v2 = kv[1, :, :, cols].reshape(KS, 2 * HD)
        v2t = v2.T
        q_t[par] = serial[:, cols].T
        og_t[par] = og[:, :, cols].reshape(QS, 2 * HD).T
        zero = jnp.zeros((HD, PQ), BF)

        def step(p, _):
            at = pl.multiple_of(p * PQ, PQ)
            qc = pl.ds(at, PQ)
            usable = use[0:4, qc] > 0.5
            for h in range(2):
                rows = slice(h * HD, (h + 1) * HD)
                cc = pl.ds(pl.multiple_of(h * QS + at, PQ), PQ)
                qh = q_t[par, rows, qc]
                oh = og_t[par, rows, qc]
                qm = jnp.concatenate([qh, zero] if h == 0 else [zero, qh], axis=0)
                om = jnp.concatenate([oh, zero] if h == 0 else [zero, oh], axis=0)
                st = dot(k2, qm)
                m_raw = jnp.full((1, PQ), -FAR, F32)
                for kb in range(4):
                    top = jnp.max(st[kb * BS:(kb + 1) * BS], axis=0, keepdims=True)
                    m_raw = jnp.maximum(m_raw, jnp.where(usable[kb:kb + 1], top, -FAR))
                m = m_raw * C2
                dp = dot(v2, om).astype(BF)
                total = jnp.zeros((1, PQ), F32)
                weighted = jnp.zeros((1, PQ), F32)
                parts = []
                for kb in range(4):
                    off = jnp.where(usable[kb:kb + 1], m, FAR)
                    pr = jnp.exp2(st[kb * BS:(kb + 1) * BS] * C2 - off)
                    total = total + jnp.sum(pr, axis=0, keepdims=True)
                    prb = pr.astype(BF)
                    weighted = weighted + jnp.sum(
                        prb.astype(F32) * dp[kb * BS:(kb + 1) * BS].astype(F32), axis=0, keepdims=True
                    )
                    parts.append(prb)
                prb = jnp.concatenate(parts, axis=0)
                probs[par, :, cc] = prb
                dps[par, :, cc] = dp
                a_keep[par, rows, qc] = dot(v2t[rows, :], prb)
                total = jnp.maximum(total, 0.5)
                r = pl.ds(2 * p + h, 1)
                m_keep[par, r, :] = m
                stat_own[hp, 0, r, :] = m + jnp.log2(total)
                stat_own[hp, 1, r, :] = weighted / total
            return 0

        lax.fori_loop(0, NM // 2, step, 0)

        def share(d, _):
            send(stat_own.at[hp], stat_got.at[hp, d - 1], stat_sem.at[0, hp], stat_sem.at[1, hp], peer(d)).start()
            return 0

        lax.fori_loop(1, NM, share, 0)

    def stat_all(hp):
        return send(stat_got.at[hp], stat_got.at[hp], stat_sem.at[0, hp], stat_sem.at[1, hp], right)

    def second(hp):
        par = lax.rem(hp, 2)
        cols = lanes_of(hp)
        stat_all(hp).wait_recv()
        lse = [stat_own[hp, 0]] + [stat_got[hp, d, 0] for d in range(NM - 1)]
        dlt = [stat_own[hp, 1]] + [stat_got[hp, d, 1] for d in range(NM - 1)]
        top = functools.reduce(jnp.maximum, lse)
        ws = [jnp.exp2(v - top) for v in lse]
        total = functools.reduce(jnp.add, ws)
        delta_all = functools.reduce(jnp.add, [w * v for w, v in zip(ws, dlt)]) / total
        m_keep[par] = jnp.exp2(m_keep[par] - (top + jnp.log2(total)))
        d_keep[...] = delta_all
        k2t = kv[0, :, :, cols].reshape(KS, 2 * HD).T

        def step(p, _):
            at = pl.multiple_of(p * PQ, PQ)
            qc = pl.ds(at, PQ)
            for h in range(2):
                rows = slice(h * HD, (h + 1) * HD)
                cc = pl.ds(pl.multiple_of(h * QS + at, PQ), PQ)
                r = pl.ds(2 * p + h, 1)
                w = m_keep[par, r, :]
                dl = d_keep[r, :]
                ds = (probs[par, :, cc].astype(F32) * (dps[par, :, cc].astype(F32) - dl)).astype(BF)
                dps[par, :, cc] = ds
                dq = (dot(k2t[rows, :], ds) * (w * SCALE)).astype(BF)
                at_ = (a_keep[par, rows, qc] * w).astype(BF)
                for e in range(2):
                    b = 2 * p + e
                    x, y = lax.rem(b, NX), b // NX
                    aq[hp, x, y, 0, rows, :] = at_[:, e * BS:(e + 1) * BS]
                    aq[hp, x, y, 1, rows, :] = dq[:, e * BS:(e + 1) * BS]
                wog_t[rows, cc] = (og_t[par, rows, qc].astype(F32) * w).astype(BF)
                wq_t[rows, cc] = (q_t[par, rows, qc].astype(F32) * (w * SCALE)).astype(BF)
            return 0

        lax.fori_loop(0, NM // 2, step, 0)
        for cp in x1_copies(hp):
            cp.start()
        dk = dot(dps[par], wq_t[...], NT).reshape(2, 2 * BS, 2 * HD)
        dv = dot(probs[par], wog_t[...], NT).reshape(2, 2 * BS, 2 * HD)
        mine = core == 0
        c_keep[hp, 0] = jnp.where(mine, dk[0], dk[1])
        c_keep[hp, 1] = jnp.where(mine, dv[0], dv[1])
        c_send[hp, 0] = jnp.where(mine, dk[1], dk[0]).astype(BF)
        c_send[hp, 1] = jnp.where(mine, dv[1], dv[0]).astype(BF)
        c_copy(hp).start()

    def x1_copies(hp):
        return (
            send(aq.at[hp, xo, 0], x1_got.at[hp, 0], x1_sem.at[0, hp, 0], x1_sem.at[1, hp, 0], right),
            send(aq.at[hp, xo, 1], x1_got.at[hp, 1], x1_sem.at[0, hp, 1], x1_sem.at[1, hp, 1], left),
        )

    def x2_copies(hp):
        return (
            send(aq.at[hp, xr], x2_got.at[hp, 0], x2_sem.at[0, hp, 0], x2_sem.at[1, hp, 0], right),
            send(aq.at[hp, xl], x2_got.at[hp, 1], x2_sem.at[0, hp, 1], x2_sem.at[1, hp, 1], left),
        )

    def y_copy(hp):
        return send(y_send.at[hp], y_got.at[hp], y_sem.at[0, hp], y_sem.at[1, hp], across)

    def c_copy(hp):
        return send(c_send.at[hp], c_got.at[hp], c_sem.at[0, hp], c_sem.at[1, hp], mate)

    def z_all(hp):
        return send(z_got.at[hp], z_got.at[hp], z_sem.at[0, hp], z_sem.at[1, hp], slab(1))

    def relay_x(hp):
        for cp in x1_copies(hp):
            cp.wait_recv()
        aq[hp, xr, 0] = (aq[hp, xr, 0].astype(F32) + x1_got[hp, 0].astype(F32)).astype(BF)
        aq[hp, xl, 1] = (aq[hp, xl, 1].astype(F32) + x1_got[hp, 1].astype(F32)).astype(BF)
        for cp in x2_copies(hp):
            cp.start()

    def relay_c(hp):
        c_copy(hp).wait_recv()
        for a in range(2):
            total = c_keep[hp, a] + c_got[hp, a].astype(F32)
            total = total.reshape(2, NP, 8, 2 * HD).transpose(1, 0, 2, 3)
            z_send[hp, :, a] = total.reshape(NP, 16, 2 * HD).astype(BF)

        def share(d, _):
            send(
                z_send.at[hp, lax.rem(pb + d, NP)], z_got.at[hp, d - 1],
                z_sem.at[0, hp], z_sem.at[1, hp], slab(d),
            ).start()
            return 0

        lax.fori_loop(1, NP, share, 0)

    def relay_y(hp):
        for cp in x2_copies(hp):
            cp.wait_recv()

        def total(y):
            return (
                aq[hp, xi, y].astype(F32)
                + x2_got[hp, 0, y].astype(F32)
                + x2_got[hp, 1, y].astype(F32)
            )

        y_send[hp] = total(yo).astype(BF)
        y_copy(hp).start()
        y_keep[hp] = total(yi)

    def finish(hp):
        cols = lanes_of(hp)
        z_all(hp).wait_recv()
        for a, out in ((0, kg_out), (1, vg_out)):
            total = z_send[hp, pb, a].astype(F32)
            for d in range(NP - 1):
                total = total + z_got[hp, d, a].astype(F32)
            out[:, :, cols] = total.reshape(2, 8, 2 * HD)
        y_copy(hp).wait_recv()
        both = y_keep[hp] + y_got[hp].astype(F32)
        att_out[0, :, cols] = both[0].T.astype(BF)
        qg_out[0, :, cols] = both[1].T
        stat_all(hp).wait_send()
        for cp in x1_copies(hp) + x2_copies(hp):
            cp.wait_send()
        y_copy(hp).wait_send()
        c_copy(hp).wait_send()
        z_all(hp).wait_send()

    def turn(s, _):
        @pl.when(s < NC)
        def _():
            first(s)

        @pl.when((s >= 2) & (s < NC + 2))
        def _():
            relay_x(s - 2)
            relay_c(s - 2)

        @pl.when((s >= 1) & (s < NC + 1))
        def _():
            second(s - 1)

        @pl.when((s >= 2) & (s < NC + 2))
        def _():
            relay_y(s - 2)

        @pl.when(s >= 3)
        def _():
            finish(s - 3)

        return 0

    lax.fori_loop(0, NC + 3, turn, 0)


def local(queries, point_order, keys, values, pair_counts, pair_keys, out_grad):
    anyspace = pl.BlockSpec(memory_space=pl.ANY)
    vmem = pl.BlockSpec(memory_space=pltpu.VMEM)
    dma = pltpu.SemaphoreType.DMA
    w2 = 2 * HD
    return pl.pallas_call(
        kernel,
        out_shape=(
            jax.ShapeDtypeStruct((1, BS, D), BF),
            jax.ShapeDtypeStruct((1, BS, D), F32),
            jax.ShapeDtypeStruct((2, 8, D), F32),
            jax.ShapeDtypeStruct((2, 8, D), F32),
        ),
        in_specs=[anyspace, vmem, anyspace, anyspace, vmem, vmem, anyspace],
        out_specs=(vmem, vmem, vmem, vmem),
        scratch_shapes=[
            pltpu.VMEM((NP * BS, D), BF),
            pltpu.VMEM((QS, D), BF),
            pltpu.VMEM((NM, BS, D), BF),
            pltpu.VMEM((2, 4, BS, D), BF),
            pltpu.VMEM((8, QS), F32),
            pltpu.VMEM((2, w2, QS), BF),
            pltpu.VMEM((2, w2, QS), BF),
            pltpu.VMEM((w2, 2 * QS), BF),
            pltpu.VMEM((w2, 2 * QS), BF),
            pltpu.VMEM((2, KS, 2 * QS), BF),
            pltpu.VMEM((2, KS, 2 * QS), BF),
            pltpu.VMEM((2, w2, QS), F32),
            pltpu.VMEM((2, 8, PQ), F32),
            pltpu.VMEM((8, PQ), F32),
            pltpu.VMEM((NC, 2, 8, PQ), F32),
            pltpu.VMEM((NC, NM - 1, 2, 8, PQ), F32),
            pltpu.VMEM((NC, NX, NY, 2, w2, BS), BF),
            pltpu.VMEM((NC, 2, 2, w2, BS), BF),
            pltpu.VMEM((NC, 2, NY, 2, w2, BS), BF),
            pltpu.VMEM((NC, 2, w2, BS), F32),
            pltpu.VMEM((NC, 2, w2, BS), BF),
            pltpu.VMEM((NC, 2, w2, BS), BF),
            pltpu.VMEM((NC, 2, 2 * BS, w2), F32),
            pltpu.VMEM((NC, 2, 2 * BS, w2), BF),
            pltpu.VMEM((NC, 2, 2 * BS, w2), BF),
            pltpu.VMEM((NC, NP, 2, 16, w2), BF),
            pltpu.VMEM((NC, NP - 1, 2, 16, w2), BF),
            dma((3 + NM,)),
            dma((2, 2)),
            dma((2, NC)),
            dma((2, NC, 2)),
            dma((2, NC, 2)),
            dma((2, NC)),
            dma((2, NC)),
            dma((2, NC)),
        ],
        compiler_params=pltpu.CompilerParams(
            collective_id=0, has_side_effects=True, vmem_limit_bytes=48 * 1024 * 1024
        ),
        name="sparse_attention",
    )(queries, point_order, keys, values, pair_counts, pair_keys, out_grad)


def solution(mesh):
    return jax.shard_map(
        local,
        mesh=mesh,
        in_specs=(
            P("pb", None),
            P("pb", None),
            P("ka", None, None),
            P("ka", None, None),
            P("pb", None),
            P("pb", None),
            P("pb", None, None),
        ),
        out_specs=(
            P(("pb", "ka"), None, None),
            P(("pb", "ka"), None, None),
            P("ka", "pb", None),
            P("ka", "pb", None),
        ),
        check_vma=False,
    )
```

time: 899 us -> 69.3 us (0.08)
  waiting for transfers between devices: 424 us -> 0 us
  local copies, waits for them, and re-layouts: 222 us -> 9.69 us
  other arithmetic: 129 us -> 0 us
  matrix products: 103 us -> 0 us
  Pallas kernels: 0 us -> 58.7 us
  between operations: 14.3 us -> 0.66 us
    reduce_scatter x4 -> x0, waiting for transfers between devices: 364 us -> none  [the longest x1 114 us: local(): lax.psum_scatter(value_grad, 'ka', scatter_dimension=0, tiled=True)]
    gather x92 -> x0, local copies, waits for them, and re-layouts: 123 us -> none  [the longest x16 30.3 us: gradients_advance(): value_heads = value_panel[key_ids].reshape(GROUP, block_rows, H, HD)]
    dot_general x48 -> x0, matrix products: 103 us -> none  [the longest x8 26.1 us: gradients_advance(): jnp.einsum('ghqk,gqhd->gkhd', score_grad, query_heads.astype(jnp.float32)...]
    scatter-add x40 -> x0, other arithmetic: 82.7 us -> none  [the longest x8 25.4 us: gradients_advance(): value_grad.at[key_ids].add(value_part.reshape(GROUP, block_rows, width))]
    pallas_call x0 -> x1, Pallas kernels: none -> 58.7 us  [local(): pl.pallas_call(kernel, out_shape=(jax.ShapeDtypeStruct((1, BS, D), BF), j...]
    all_gather x2 -> x0, waiting for transfers between devices: 57.6 us -> none  [the longest x1 48.4 us: local(): lax.all_gather(keys, 'ka', axis=0, tiled=True)]
    dynamic_slice x19 -> x0, local copies, waits for them, and re-layouts: 42.6 us -> none  [the longest x16 40.7 us: softmax_sums(): result, _ = lax.scan(softmax_advance, start, groups + (score_stack,))]
    reshape x34 -> x0, local copies, waits for them, and re-layouts: 39.5 us -> none  [the longest x8 20.7 us: gradients_advance(): query_part.reshape(GROUP, block_rows, width)]
  transfers between devices with their start and end apart: 6 -> 0, of which waited for: 6 -> 0; matrix products, arithmetic and copies ran while one was open for 8% -> 0% of each run, Pallas kernels for 0% -> 0%
where the time goes in v1:
time: 69.3 us; the launch traced here: 69.1 us
  Pallas kernels  58.7 us (85%)
  local copies, waits for them, and re-layouts  9.69 us (14%)
    pallas_call x1, Pallas kernels, local(): pl.pallas_call(kernel, out_shape=(jax.ShapeDtypeStruct((1, BS, D), BF), j...  58.7 us
    unnamed x18, local copies, waits for them, and re-layouts  9.69 us

profile of v1, /device:TPU:2, one launch (start us, length us, event | category | flops | bytes accessed | tf_op | source)
XLA Modules:
  0.0 69.1 jit_solution(7213241944252905196)
XLA Ops:
  0.6 0.0 copy-start
  0.6 1.6 %copy-done = bf16[2048,512]{1,0:T(8,128)(2,1)S(1)} copy-done((bf16[2048,512]{1,0:T(8,128)(2,1)S(1)}, bf16[2048,512]{1,0:T(8,128)(2,1)}, u32[]{:S(2)}) %copy-start) | copy-done | bytes 2097176
  2.2 0.0 copy-start.1
  2.2 1.6 %copy-done.1 = bf16[16,128,512]{2,1,0:T(8,128)(2,1)S(1)} copy-done((bf16[16,128,512]{2,1,0:T(8,128)(2,1)S(1)}, bf16[16,128,512]{2,1,0:T(8,128)(2,1)}, u32[]{:S(2)}) %copy-start.1) | copy-done | bytes 2097176
  3.8 0.0 copy-start.2
  3.8 0.9 %copy-done.2 = bf16[2,128,512]{2,1,0:T(8,128)(2,1)S(1)} copy-done((bf16[2,128,512]{2,1,0:T(8,128)(2,1)S(1)}, bf16[2,128,512]{2,1,0:T(8,128)(2,1)}, u32[]{:S(2)}) %copy-start.2) | copy-done | bytes 262168
  4.8 0.0 copy-start.3
  4.8 0.9 %copy-done.3 = bf16[2,128,512]{2,1,0:T(8,128)(2,1)S(1)} copy-done((bf16[2,128,512]{2,1,0:T(8,128)(2,1)S(1)}, bf16[2,128,512]{2,1,0:T(8,128)(2,1)}, u32[]{:S(2)}) %copy-start.3) | copy-done | bytes 262168
  5.7 0.0 copy-start.4
  5.7 0.7 %copy-done.4 = s32[1,2048]{1,0:T(1,128)S(1)} copy-done((s32[1,2048]{1,0:T(1,128)S(1)}, s32[1,2048]{1,0:T(1,128)}, u32[]{:S(2)}) %copy-start.4) | copy-done | bytes 8216
  6.4 0.0 copy-start.5
  6.4 0.7 copy-done.5
  7.1 0.0 copy-start.6
  7.1 0.7 copy-done.6
  7.8 58.7 %sparse_attention.1 = (bf16[1,128,512]{2,1,0:T(8,128)(2,1)S(1)}, f32[1,128,512]{2,1,0:T(8,128)S(1)}, f32[2,8,512]{2,1,0:T(8,128)S(1)}, f32[2,8,512]{2,1,0:T(8,128)S(1)}) custom-call(bf16[2048,512]{1,0:T(8,128)(2,1)S(1)} %copy-done, s32[1,2048]{1,0:T(1,128)S(1)} %copy-done.4, bf16[2,128,512]{2,1,0:T(8,128)(2,1)S(1)} %copy-done.2, ...), custom_call_target="tpu_custom_call" | custom-call | tf_op jit(solution)/shard_map/sparse_attention/pallas_call | solution.py:415
  66.5 0.7 copy.15
  67.1 0.7 %copy.16 = f32[1,128,512]{2,1,0:T(8,128)} copy(f32[1,128,512]{2,1,0:T(8,128)S(1)} %get-tuple-element.9) | data formatting | bytes 524288
  67.8 0.6 copy.17
  68.5 0.6 copy.18
Async XLA Ops:
  0.6 1.6 %copy-start = (bf16[2048,512]{1,0:T(8,128)(2,1)S(1)}, bf16[2048,512]{1,0:T(8,128)(2,1)}, u32[]{:S(2)}) copy-start(bf16[2048,512]{1,0:T(8,128)(2,1)} %queries.1) | copy-start | bytes 6291460
  2.2 1.6 %copy-start.1 = (bf16[16,128,512]{2,1,0:T(8,128)(2,1)S(1)}, bf16[16,128,512]{2,1,0:T(8,128)(2,1)}, u32[]{:S(2)}) copy-start(bf16[16,128,512]{2,1,0:T(8,128)(2,1)} %out_grad.1) | copy-start | bytes 6291460
  3.8 0.9 %copy-start.2 = (bf16[2,128,512]{2,1,0:T(8,128)(2,1)S(1)}, bf16[2,128,512]{2,1,0:T(8,128)(2,1)}, u32[]{:S(2)}) copy-start(bf16[2,128,512]{2,1,0:T(8,128)(2,1)} %keys.1) | copy-start | bytes 786436
  4.8 0.9 %copy-start.3 = (bf16[2,128,512]{2,1,0:T(8,128)(2,1)S(1)}, bf16[2,128,512]{2,1,0:T(8,128)(2,1)}, u32[]{:S(2)}) copy-start(bf16[2,128,512]{2,1,0:T(8,128)(2,1)} %values.1) | copy-start | bytes 786436
  5.7 0.7 %copy-start.4 = (s32[1,2048]{1,0:T(1,128)S(1)}, s32[1,2048]{1,0:T(1,128)}, u32[]{:S(2)}) copy-start(s32[1,2048]{1,0:T(1,128)} %order.1) | copy-start | bytes 24580
  6.4 0.7 copy-start.5
  7.1 0.7 copy-start.6

commit v2 on v1

--- a/solution.py
+++ b/solution.py
@@ -48,16 +48,18 @@
     kg_out,
     vg_out,
     qbuf,
+    order_v,
+    counts_v,
+    listing_v,
     serial,
     og,
     kv,
     use,
-    q_t,
+    q_m,
+    og_m,
     og_t,
-    wq_t,
-    wog_t,
     probs,
-    dps,
+    dss,
     a_keep,
     m_keep,
     d_keep,
@@ -127,20 +129,27 @@
     lax.fori_loop(1, NM, hello_ka, 0)
     lax.fori_loop(1, NP, hello_pb, 0)
 
+    own2 = pl.ds(2 * core, 2)
     load_q = pltpu.make_async_copy(queries, qbuf, load_sem.at[0])
-    load_q.start()
-    own2 = pl.ds(2 * core, 2)
-    load_k = pltpu.make_async_copy(keys, kv.at[0, own2], load_sem.at[1])
-    load_v = pltpu.make_async_copy(values, kv.at[1, own2], load_sem.at[2])
-    load_k.start()
-    load_v.start()
-    load_og = []
-    for b in range(NM):
-        cp = pltpu.make_async_copy(out_grad.at[2 * b + core], og.at[b], load_sem.at[3 + b])
+    load_small = [
+        pltpu.make_async_copy(order, order_v, load_sem.at[3]),
+        pltpu.make_async_copy(counts, counts_v, load_sem.at[4]),
+        pltpu.make_async_copy(listing, listing_v, load_sem.at[5]),
+    ]
+    load_kv = [
+        pltpu.make_async_copy(keys, kv.at[0, own2], load_sem.at[1]),
+        pltpu.make_async_copy(values, kv.at[1, own2], load_sem.at[2]),
+    ]
+    load_og = [
+        pltpu.make_async_copy(out_grad.at[2 * b + core], og.at[b], load_sem.at[6 + b])
+        for b in range(NM)
+    ]
+    for cp in load_small + [load_q] + load_kv + load_og:
         cp.start()
-        load_og.append(cp)
-
-    cb = jnp.broadcast_to(counts[...].astype(F32), (16, 16))
+    for cp in load_small:
+        cp.wait()
+
+    cb = jnp.broadcast_to(counts_v[...].astype(F32), (16, 16))
     i0 = lax.broadcasted_iota(jnp.int32, (16, 16), 0)
     i1 = lax.broadcasted_iota(jnp.int32, (16, 16), 1)
     starts = jnp.sum(jnp.where(i1 < i0, cb, 0.0), axis=1, keepdims=True)
@@ -148,101 +157,89 @@
     slot = lax.broadcasted_iota(jnp.int32, (16, 256), 1).astype(F32)
     inside = jnp.where((slot >= starts) & (slot < starts + sizes), 1.0, 0.0)
     row = lax.broadcasted_iota(jnp.int32, (8, 256), 0) + 4 * chip
-    named = jnp.where(jnp.broadcast_to(listing[...], (8, 256)) == row, 1.0, 0.0)
+    named = jnp.where(jnp.broadcast_to(listing_v[...], (8, 256)) == row, 1.0, 0.0)
     joined = dot(named.astype(BF), inside.astype(BF), NT)
     e0 = lax.broadcasted_iota(jnp.int32, (16, QS), 0)
     e1 = lax.broadcasted_iota(jnp.int32, (16, QS), 1)
     spread = jnp.where(e0 == 2 * (e1 // BS) + core, 1.0, 0.0)
     use[...] = dot(joined.astype(BF), spread.astype(BF))
 
-    zero_half = jnp.zeros((HD, QS), BF)
-    for arr in (wq_t, wog_t):
-        arr[HD:, :QS] = zero_half
-        arr[:HD, QS:] = zero_half
-
     load_q.wait()
 
-    def gather(b, _):
-        at = pl.multiple_of((2 * b + core) * BS, BS)
-        line = order[:, pl.ds(at, BS)]
-        column = jnp.broadcast_to(line, (BS, BS)).T
-        lanes = lax.broadcasted_iota(jnp.int32, (BS, BS), 1)
-        picks = [
-            jnp.where(column == lanes + n * BS, 1.0, 0.0).astype(BF) for n in range(16)
-        ]
-        pick = jnp.concatenate(picks, axis=1)
-        serial[pl.ds(pl.multiple_of(b * BS, BS), BS), :] = dot(pick, qbuf[...]).astype(BF)
+    def gather(t, _):
+        picks = []
+        for e in range(4):
+            at = pl.multiple_of((8 * t + 2 * e + core) * BS, BS)
+            column = jnp.broadcast_to(order_v[:, pl.ds(at, BS)], (BS, BS)).T
+            lanes = lax.broadcasted_iota(jnp.int32, (BS, BS), 1)
+            picks.append(jnp.concatenate(
+                [jnp.where(column == lanes + n * BS, 1.0, 0.0).astype(BF) for n in range(16)], axis=1
+            ))
+        pick = jnp.concatenate(picks, axis=0)
+        serial[pl.ds(pl.multiple_of(t * 4 * BS, 4 * BS), 4 * BS), :] = dot(pick, qbuf[...]).astype(BF)
         return 0
 
-    lax.fori_loop(0, 2, gather, 0)
+    lax.fori_loop(0, 1, gather, 0)
     pl.semaphore_wait(barrier, 1 + (NM - 1) + (NP - 1))
     send_k = send(keys, kv.at[0, own2], kv_sem.at[0, 0], kv_sem.at[1, 0], mate)
     send_v = send(values, kv.at[1, own2], kv_sem.at[0, 1], kv_sem.at[1, 1], mate)
     send_k.start()
     send_v.start()
-    lax.fori_loop(2, NM, gather, 0)
-    load_k.wait()
-    load_v.wait()
-    for cp in load_og:
+    lax.fori_loop(1, 2, gather, 0)
+    for cp in load_kv + load_og:
         cp.wait()
     send_k.wait()
     send_v.wait()
 
     def lanes_of(hp):
         return pl.ds(pl.multiple_of(hp * 2 * HD, 2 * HD), 2 * HD)
+
+    def flip(a):
+        unit = jnp.where(
+            lax.broadcasted_iota(jnp.int32, (2 * HD, 2 * HD), 0)
+            == lax.broadcasted_iota(jnp.int32, (2 * HD, 2 * HD), 1), 1.0, 0.0
+        ).astype(BF)
+        return dot(unit, a, NT)
 
     def first(hp):
         par = lax.rem(hp, 2)
         cols = lanes_of(hp)
         k2 = kv[0, :, :, cols].reshape(KS, 2 * HD)
-        v2 = kv[1, :, :, cols].reshape(KS, 2 * HD)
-        v2t = v2.T
-        q_t[par] = serial[:, cols].T
-        og_t[par] = og[:, :, cols].reshape(QS, 2 * HD).T
-        zero = jnp.zeros((HD, PQ), BF)
-
-        def step(p, _):
-            at = pl.multiple_of(p * PQ, PQ)
-            qc = pl.ds(at, PQ)
+        v2t = flip(kv[1, :, :, cols].reshape(KS, 2 * HD)).astype(BF)
+        og_t[...] = flip(og[:, :, cols].reshape(QS, 2 * HD))
+        low = lax.broadcasted_iota(jnp.int32, (QS, 2 * HD), 1) < HD
+        none = jnp.zeros((QS, 2 * HD), BF)
+        for src, dst in ((serial[:, cols], q_m), (og[:, :, cols].reshape(QS, 2 * HD), og_m)):
+            dst[par, :QS] = jnp.where(low, src, none)
+            dst[par, QS:] = jnp.where(low, none, src)
+
+        for p in range(NM // 2):
+            qc = slice(p * PQ, (p + 1) * PQ)
             usable = use[0:4, qc] > 0.5
             for h in range(2):
                 rows = slice(h * HD, (h + 1) * HD)
-                cc = pl.ds(pl.multiple_of(h * QS + at, PQ), PQ)
-                qh = q_t[par, rows, qc]
-                oh = og_t[par, rows, qc]
-                qm = jnp.concatenate([qh, zero] if h == 0 else [zero, qh], axis=0)
-                om = jnp.concatenate([oh, zero] if h == 0 else [zero, oh], axis=0)
-                st = dot(k2, qm)
+                cc = slice(h * QS + p * PQ, h * QS + (p + 1) * PQ)
+                st = dot(k2, q_m[par, cc, :], NT)
                 m_raw = jnp.full((1, PQ), -FAR, F32)
                 for kb in range(4):
                     top = jnp.max(st[kb * BS:(kb + 1) * BS], axis=0, keepdims=True)
                     m_raw = jnp.maximum(m_raw, jnp.where(usable[kb:kb + 1], top, -FAR))
                 m = m_raw * C2
-                dp = dot(v2, om).astype(BF)
-                total = jnp.zeros((1, PQ), F32)
-                weighted = jnp.zeros((1, PQ), F32)
                 parts = []
                 for kb in range(4):
                     off = jnp.where(usable[kb:kb + 1], m, FAR)
-                    pr = jnp.exp2(st[kb * BS:(kb + 1) * BS] * C2 - off)
-                    total = total + jnp.sum(pr, axis=0, keepdims=True)
-                    prb = pr.astype(BF)
-                    weighted = weighted + jnp.sum(
-                        prb.astype(F32) * dp[kb * BS:(kb + 1) * BS].astype(F32), axis=0, keepdims=True
-                    )
-                    parts.append(prb)
-                prb = jnp.concatenate(parts, axis=0)
+                    parts.append(jnp.exp2(st[kb * BS:(kb + 1) * BS] * C2 - off))
+                total = jnp.sum(parts[0] + parts[1] + parts[2] + parts[3], axis=0, keepdims=True)
+                prb = jnp.concatenate([v.astype(BF) for v in parts], axis=0)
                 probs[par, :, cc] = prb
-                dps[par, :, cc] = dp
-                a_keep[par, rows, qc] = dot(v2t[rows, :], prb)
+                a_h = dot(v2t[rows, :], prb)
+                a_keep[par, rows, qc] = a_h
+                weighted = jnp.sum(a_h * og_t[rows, qc], axis=0, keepdims=True)
                 total = jnp.maximum(total, 0.5)
-                r = pl.ds(2 * p + h, 1)
+                r = slice(2 * p + h, 2 * p + h + 1)
                 m_keep[par, r, :] = m
                 stat_own[hp, 0, r, :] = m + jnp.log2(total)
                 stat_own[hp, 1, r, :] = weighted / total
-            return 0
-
-        lax.fori_loop(0, NM // 2, step, 0)
 
         def share(d, _):
             send(stat_own.at[hp], stat_got.at[hp, d - 1], stat_sem.at[0, hp], stat_sem.at[1, hp], peer(d)).start()
@@ -265,35 +262,32 @@
         delta_all = functools.reduce(jnp.add, [w * v for w, v in zip(ws, dlt)]) / total
         m_keep[par] = jnp.exp2(m_keep[par] - (top + jnp.log2(total)))
         d_keep[...] = delta_all
-        k2t = kv[0, :, :, cols].reshape(KS, 2 * HD).T
-
-        def step(p, _):
-            at = pl.multiple_of(p * PQ, PQ)
-            qc = pl.ds(at, PQ)
+        k2t = flip(kv[0, :, :, cols].reshape(KS, 2 * HD)).astype(BF)
+        v2 = kv[1, :, :, cols].reshape(KS, 2 * HD)
+
+        for p in range(NM // 2):
+            qc = slice(p * PQ, (p + 1) * PQ)
             for h in range(2):
                 rows = slice(h * HD, (h + 1) * HD)
-                cc = pl.ds(pl.multiple_of(h * QS + at, PQ), PQ)
-                r = pl.ds(2 * p + h, 1)
+                cc = slice(h * QS + p * PQ, h * QS + (p + 1) * PQ)
+                r = slice(2 * p + h, 2 * p + h + 1)
                 w = m_keep[par, r, :]
-                dl = d_keep[r, :]
-                ds = (probs[par, :, cc].astype(F32) * (dps[par, :, cc].astype(F32) - dl)).astype(BF)
-                dps[par, :, cc] = ds
-                dq = (dot(k2t[rows, :], ds) * (w * SCALE)).astype(BF)
+                dp = dot(v2, og_m[par, cc, :], NT)
+                qf = probs[par, :, cc].astype(F32) * w
+                ds = (qf * (dp - d_keep[r, :])).astype(BF)
+                probs[par, :, cc] = qf.astype(BF)
+                dss[:, cc] = ds
+                dq = (dot(k2t[rows, :], ds) * SCALE).astype(BF)
                 at_ = (a_keep[par, rows, qc] * w).astype(BF)
                 for e in range(2):
                     b = 2 * p + e
-                    x, y = lax.rem(b, NX), b // NX
+                    x, y = b % NX, b // NX
                     aq[hp, x, y, 0, rows, :] = at_[:, e * BS:(e + 1) * BS]
                     aq[hp, x, y, 1, rows, :] = dq[:, e * BS:(e + 1) * BS]
-                wog_t[rows, cc] = (og_t[par, rows, qc].astype(F32) * w).astype(BF)
-                wq_t[rows, cc] = (q_t[par, rows, qc].astype(F32) * (w * SCALE)).astype(BF)
-            return 0
-
-        lax.fori_loop(0, NM // 2, step, 0)
         for cp in x1_copies(hp):
             cp.start()
-        dk = dot(dps[par], wq_t[...], NT).reshape(2, 2 * BS, 2 * HD)
-        dv = dot(probs[par], wog_t[...], NT).reshape(2, 2 * BS, 2 * HD)
+        dk = (dot(dss[...], q_m[par]) * SCALE).reshape(2, 2 * BS, 2 * HD)
+        dv = dot(probs[par], og_m[par]).reshape(2, 2 * BS, 2 * HD)
         mine = core == 0
         c_keep[hp, 0] = jnp.where(mine, dk[0], dk[1])
         c_keep[hp, 1] = jnp.where(mine, dv[0], dv[1])
@@ -420,20 +414,22 @@
             jax.ShapeDtypeStruct((2, 8, D), F32),
             jax.ShapeDtypeStruct((2, 8, D), F32),
         ),
-        in_specs=[anyspace, vmem, anyspace, anyspace, vmem, vmem, anyspace],
+        in_specs=[anyspace] * 7,
         out_specs=(vmem, vmem, vmem, vmem),
         scratch_shapes=[
             pltpu.VMEM((NP * BS, D), BF),
+            pltpu.VMEM((1, NP * BS), jnp.int32),
+            pltpu.VMEM((1, NP), jnp.int32),
+            pltpu.VMEM((1, 256), jnp.int32),
             pltpu.VMEM((QS, D), BF),
             pltpu.VMEM((NM, BS, D), BF),
             pltpu.VMEM((2, 4, BS, D), BF),
             pltpu.VMEM((8, QS), F32),
-            pltpu.VMEM((2, w2, QS), BF),
-            pltpu.VMEM((2, w2, QS), BF),
-            pltpu.VMEM((w2, 2 * QS), BF),
-            pltpu.VMEM((w2, 2 * QS), BF),
+            pltpu.VMEM((2, 2 * QS, w2), BF),
+            pltpu.VMEM((2, 2 * QS, w2), BF),
+            pltpu.VMEM((w2, QS), F32),
             pltpu.VMEM((2, KS, 2 * QS), BF),
-            pltpu.VMEM((2, KS, 2 * QS), BF),
+            pltpu.VMEM((KS, 2 * QS), BF),
             pltpu.VMEM((2, w2, QS), F32),
             pltpu.VMEM((2, 8, PQ), F32),
             pltpu.VMEM((8, PQ), F32),
@@ -450,7 +446,7 @@
             pltpu.VMEM((NC, 2, 2 * BS, w2), BF),
             pltpu.VMEM((NC, NP, 2, 16, w2), BF),
             pltpu.VMEM((NC, NP - 1, 2, 16, w2), BF),
-            dma((3 + NM,)),
+            dma((6 + NM,)),
             dma((2, 2)),
             dma((2, NC)),
             dma((2, NC, 2)),
@@ -460,7 +456,7 @@
             dma((2, NC)),
         ],
         compiler_params=pltpu.CompilerParams(
-            collective_id=0, has_side_effects=True, vmem_limit_bytes=48 * 1024 * 1024
+            collective_id=0, has_side_effects=True, vmem_limit_bytes=60 * 1024 * 1024
         ),
         name="sparse_attention",
     )(queries, point_order, keys, values, pair_counts, pair_keys, out_grad)

time: 69.3 us -> 69.4 us (level)
  Pallas kernels: 58.7 us -> 62.6 us
  local copies, waits for them, and re-layouts: 9.69 us -> 5.99 us
    pallas_call x1, Pallas kernels: 58.7 us -> 62.6 us  [local(): pl.pallas_call(kernel, out_shape=(jax.ShapeDtypeStruct((1, BS, D), BF), j...]
    unnamed x18 -> x4, local copies, waits for them, and re-layouts: 9.69 us -> 5.99 us
where the time goes in v2:
time: 69.4 us; the launch traced here: 69.2 us
  Pallas kernels  62.6 us (90%)
  local copies, waits for them, and re-layouts  5.99 us (9%)
    pallas_call x1, Pallas kernels, local(): pl.pallas_call(kernel, out_shape=(jax.ShapeDtypeStruct((1, BS, D), BF), j...  62.6 us
    unnamed x4, local copies, waits for them, and re-layouts  5.99 us

profile of v2, /device:TPU:2, one launch (start us, length us, event | category | flops | bytes accessed | tf_op | source)
XLA Modules:
  0.0 69.2 jit_solution(6861012668130029713)
XLA Ops:
  0.6 62.6 %sparse_attention.1 = (bf16[1,128,512]{2,1,0:T(8,128)(2,1)}, f32[1,128,512]{2,1,0:T(8,128)}, f32[2,8,512]{2,1,0:T(8,128)}, f32[2,8,512]{2,1,0:T(8,128)}) custom-call(bf16[2048,512]{1,0:T(8,128)(2,1)} %queries.1, s32[1,2048]{1,0:T(1,128)} %order.1, bf16[2,128,512]{2,1,0:T(8,128)(2,1)} %keys.1, bf16[2,128,512]{2,1,0:T(8,128)(2,1)} %values.1, s32[1,16]{1,0:T(1,128)} %counts.1, ...), custom_call_target="tpu_custom_call" | custom-call | tf_op jit(solution)/shard_map/sparse_attention/pallas_call | solution.py:409
  63.2 1.6 %copy.15 = bf16[1,128,512]{2,1,0:T(8,128)(2,1)} copy(bf16[1,128,512]{2,1,0:T(8,128)(2,1)} %get-tuple-element.8) | data formatting | bytes 262144
  64.8 1.7 %copy.16 = f32[1,128,512]{2,1,0:T(8,128)} copy(f32[1,128,512]{2,1,0:T(8,128)} %get-tuple-element.9) | data formatting | bytes 524288
  66.4 1.4 %copy.17 = f32[2,8,512]{2,1,0:T(8,128)} copy(f32[2,8,512]{2,1,0:T(8,128)} %get-tuple-element.10) | data formatting | bytes 65536
  67.8 1.4 %copy.18 = f32[2,8,512]{2,1,0:T(8,128)} copy(f32[2,8,512]{2,1,0:T(8,128)} %get-tuple-element.11) | data formatting | bytes 65536

commit v3 on v2

--- a/solution.py
+++ b/solution.py
@@ -166,7 +166,16 @@
 
     load_q.wait()
 
+    send_k = send(keys, kv.at[0, own2], kv_sem.at[0, 0], kv_sem.at[1, 0], mate)
+    send_v = send(values, kv.at[1, own2], kv_sem.at[0, 1], kv_sem.at[1, 1], mate)
+
     def gather(t, _):
+        @pl.when(t == 1)
+        def _():
+            pl.semaphore_wait(barrier, 1 + (NM - 1) + (NP - 1))
+            send_k.start()
+            send_v.start()
+
         picks = []
         for e in range(4):
             at = pl.multiple_of((8 * t + 2 * e + core) * BS, BS)
@@ -179,13 +188,7 @@
         serial[pl.ds(pl.multiple_of(t * 4 * BS, 4 * BS), 4 * BS), :] = dot(pick, qbuf[...]).astype(BF)
         return 0
 
-    lax.fori_loop(0, 1, gather, 0)
-    pl.semaphore_wait(barrier, 1 + (NM - 1) + (NP - 1))
-    send_k = send(keys, kv.at[0, own2], kv_sem.at[0, 0], kv_sem.at[1, 0], mate)
-    send_v = send(values, kv.at[1, own2], kv_sem.at[0, 1], kv_sem.at[1, 1], mate)
-    send_k.start()
-    send_v.start()
-    lax.fori_loop(1, 2, gather, 0)
+    lax.fori_loop(0, 2, gather, 0)
     for cp in load_kv + load_og:
         cp.wait()
     send_k.wait()
@@ -213,12 +216,13 @@
             dst[par, :QS] = jnp.where(low, src, none)
             dst[par, QS:] = jnp.where(low, none, src)
 
-        for p in range(NM // 2):
-            qc = slice(p * PQ, (p + 1) * PQ)
+        def step(p, _):
+            at = pl.multiple_of(p * PQ, PQ)
+            qc = pl.ds(at, PQ)
             usable = use[0:4, qc] > 0.5
             for h in range(2):
                 rows = slice(h * HD, (h + 1) * HD)
-                cc = slice(h * QS + p * PQ, h * QS + (p + 1) * PQ)
+                cc = pl.ds(pl.multiple_of(h * QS + at, PQ), PQ)
                 st = dot(k2, q_m[par, cc, :], NT)
                 m_raw = jnp.full((1, PQ), -FAR, F32)
                 for kb in range(4):
@@ -236,10 +240,13 @@
                 a_keep[par, rows, qc] = a_h
                 weighted = jnp.sum(a_h * og_t[rows, qc], axis=0, keepdims=True)
                 total = jnp.maximum(total, 0.5)
-                r = slice(2 * p + h, 2 * p + h + 1)
+                r = pl.ds(2 * p + h, 1)
                 m_keep[par, r, :] = m
                 stat_own[hp, 0, r, :] = m + jnp.log2(total)
                 stat_own[hp, 1, r, :] = weighted / total
+            return 0
+
+        lax.fori_loop(0, NM // 2, step, 0)
 
         def share(d, _):
             send(stat_own.at[hp], stat_got.at[hp, d - 1], stat_sem.at[0, hp], stat_sem.at[1, hp], peer(d)).start()
@@ -265,12 +272,13 @@
         k2t = flip(kv[0, :, :, cols].reshape(KS, 2 * HD)).astype(BF)
         v2 = kv[1, :, :, cols].reshape(KS, 2 * HD)
 
-        for p in range(NM // 2):
-            qc = slice(p * PQ, (p + 1) * PQ)
+        def step(p, _):
+            at = pl.multiple_of(p * PQ, PQ)
+            qc = pl.ds(at, PQ)
             for h in range(2):
                 rows = slice(h * HD, (h + 1) * HD)
-                cc = slice(h * QS + p * PQ, h * QS + (p + 1) * PQ)
-                r = slice(2 * p + h, 2 * p + h + 1)
+                cc = pl.ds(pl.multiple_of(h * QS + at, PQ), PQ)
+                r = pl.ds(2 * p + h, 1)
                 w = m_keep[par, r, :]
                 dp = dot(v2, og_m[par, cc, :], NT)
                 qf = probs[par, :, cc].astype(F32) * w
@@ -281,9 +289,12 @@
                 at_ = (a_keep[par, rows, qc] * w).astype(BF)
                 for e in range(2):
                     b = 2 * p + e
-                    x, y = b % NX, b // NX
+                    x, y = lax.rem(b, NX), b // NX
                     aq[hp, x, y, 0, rows, :] = at_[:, e * BS:(e + 1) * BS]
                     aq[hp, x, y, 1, rows, :] = dq[:, e * BS:(e + 1) * BS]
+            return 0
+
+        lax.fori_loop(0, NM // 2, step, 0)
         for cp in x1_copies(hp):
             cp.start()
         dk = (dot(dss[...], q_m[par]) * SCALE).reshape(2, 2 * BS, 2 * HD)
@@ -401,20 +412,30 @@
     lax.fori_loop(0, NC + 3, turn, 0)
 
 
+def write_out(*refs):
+    sems = refs[8]
+    copies = [pltpu.make_async_copy(refs[i], refs[4 + i], sems.at[i]) for i in range(4)]
+    for cp in copies:
+        cp.start()
+    for cp in copies:
+        cp.wait()
+
+
 def local(queries, point_order, keys, values, pair_counts, pair_keys, out_grad):
-    anyspace = pl.BlockSpec(memory_space=pl.ANY)
+    hbm = pl.BlockSpec(memory_space=pl.ANY)
     vmem = pl.BlockSpec(memory_space=pltpu.VMEM)
     dma = pltpu.SemaphoreType.DMA
     w2 = 2 * HD
-    return pl.pallas_call(
+    out_shape = (
+        jax.ShapeDtypeStruct((1, BS, D), BF),
+        jax.ShapeDtypeStruct((1, BS, D), F32),
+        jax.ShapeDtypeStruct((2, 8, D), F32),
+        jax.ShapeDtypeStruct((2, 8, D), F32),
+    )
+    results = pl.pallas_call(
         kernel,
-        out_shape=(
-            jax.ShapeDtypeStruct((1, BS, D), BF),
-            jax.ShapeDtypeStruct((1, BS, D), F32),
-            jax.ShapeDtypeStruct((2, 8, D), F32),
-            jax.ShapeDtypeStruct((2, 8, D), F32),
-        ),
-        in_specs=[anyspace] * 7,
+        out_shape=out_shape,
+        in_specs=[hbm] * 7,
         out_specs=(vmem, vmem, vmem, vmem),
         scratch_shapes=[
             pltpu.VMEM((NP * BS, D), BF),
@@ -460,6 +481,14 @@
         ),
         name="sparse_attention",
     )(queries, point_order, keys, values, pair_counts, pair_keys, out_grad)
+    return pl.pallas_call(
+        write_out,
+        out_shape=out_shape,
+        in_specs=[vmem] * 4,
+        out_specs=(hbm,) * 4,
+        scratch_shapes=[dma((4,))],
+        name="write_out",
+    )(*results)
 
 
 def solution(mesh):

time: 69.4 us -> 68.7 us (0.990)
  local copies, waits for them, and re-layouts: 5.99 us -> 0 us
  Pallas kernels: 62.6 us -> 67.9 us
    unnamed x4 -> x0, local copies, waits for them, and re-layouts: 5.99 us -> none
    pallas_call x1 -> x2, Pallas kernels: 62.6 us -> 67.9 us  [the longest x1 66.2 us: local(): pl.pallas_call(kernel, out_shape=out_shape, in_specs=[hbm] * 7, out_specs...]
where the time goes in v3:
time: 68.7 us; the launch traced here: 68.6 us
  Pallas kernels  67.9 us (99%)
    pallas_call x1, Pallas kernels, local(): pl.pallas_call(kernel, out_shape=out_shape, in_specs=[hbm] * 7, out_specs...  66.2 us
    pallas_call x1, Pallas kernels, local(): pl.pallas_call(write_out, out_shape=out_shape, in_specs=[vmem] * 4, out_s...  1.78 us

profile of v3, /device:TPU:2, one launch (start us, length us, event | category | flops | bytes accessed | tf_op | source)
XLA Modules:
  0.0 68.6 jit_solution(8029435190567973914)
XLA Ops:
  0.6 66.2 %sparse_attention.1 = (bf16[1,128,512]{2,1,0:T(8,128)(2,1)}, f32[1,128,512]{2,1,0:T(8,128)}, f32[2,8,512]{2,1,0:T(8,128)}, f32[2,8,512]{2,1,0:T(8,128)}) custom-call(bf16[2048,512]{1,0:T(8,128)(2,1)} %queries.1, s32[1,2048]{1,0:T(1,128)} %order.1, bf16[2,128,512]{2,1,0:T(8,128)(2,1)} %keys.1, bf16[2,128,512]{2,1,0:T(8,128)(2,1)} %values.1, s32[1,16]{1,0:T(1,128)} %counts.1, ...), custom_call_target="tpu_custom_call" | custom-call | tf_op jit(solution)/shard_map/sparse_attention/pallas_call | solution.py:435
  66.8 1.8 %write_out.1 = (bf16[1,128,512]{2,1,0:T(8,128)(2,1)}, f32[1,128,512]{2,1,0:T(8,128)}, f32[2,8,512]{2,1,0:T(8,128)}, f32[2,8,512]{2,1,0:T(8,128)}) custom-call(bf16[1,128,512]{2,1,0:T(8,128)(2,1)} %get-tuple-element.8.refs_0_, f32[1,128,512]{2,1,0:T(8,128)} %get-tuple-element.9.refs_1_, f32[2,8,512]{2,1,0:T(8,128)} %get-tuple-element.10.refs_2_, ...), custom_call_target="tpu_custom_call" | custom-call | tf_op jit(solution)/shard_map/write_out/pallas_call | solution.py:484

commit v4 on v3

--- a/solution.py
+++ b/solution.py
@@ -29,6 +29,7 @@
 
 NN = (((1,), (0,)), ((), ()))
 NT = (((1,), (1,)), ((), ()))
+TN = (((0,), (0,)), ((), ()))
 
 
 def dot(a, b, dims=NN):
@@ -57,10 +58,10 @@
     use,
     q_m,
     og_m,
-    og_t,
+    k_m,
+    v_m,
     probs,
-    dss,
-    a_keep,
+    dps,
     m_keep,
     d_keep,
     stat_own,
@@ -197,56 +198,48 @@
     def lanes_of(hp):
         return pl.ds(pl.multiple_of(hp * 2 * HD, 2 * HD), 2 * HD)
 
-    def flip(a):
-        unit = jnp.where(
-            lax.broadcasted_iota(jnp.int32, (2 * HD, 2 * HD), 0)
-            == lax.broadcasted_iota(jnp.int32, (2 * HD, 2 * HD), 1), 1.0, 0.0
-        ).astype(BF)
-        return dot(unit, a, NT)
+    def split_heads(src, dst, n):
+        low = lax.broadcasted_iota(jnp.int32, (n, 2 * HD), 1) < HD
+        none = jnp.zeros((n, 2 * HD), BF)
+        dst[:n] = jnp.where(low, src, none)
+        dst[n:] = jnp.where(low, none, src)
 
     def first(hp):
         par = lax.rem(hp, 2)
         cols = lanes_of(hp)
         k2 = kv[0, :, :, cols].reshape(KS, 2 * HD)
-        v2t = flip(kv[1, :, :, cols].reshape(KS, 2 * HD)).astype(BF)
-        og_t[...] = flip(og[:, :, cols].reshape(QS, 2 * HD))
-        low = lax.broadcasted_iota(jnp.int32, (QS, 2 * HD), 1) < HD
-        none = jnp.zeros((QS, 2 * HD), BF)
-        for src, dst in ((serial[:, cols], q_m), (og[:, :, cols].reshape(QS, 2 * HD), og_m)):
-            dst[par, :QS] = jnp.where(low, src, none)
-            dst[par, QS:] = jnp.where(low, none, src)
-
-        def step(p, _):
-            at = pl.multiple_of(p * PQ, PQ)
-            qc = pl.ds(at, PQ)
+        v2 = kv[1, :, :, cols].reshape(KS, 2 * HD)
+        split_heads(serial[:, cols], q_m.at[par], QS)
+        split_heads(og[:, :, cols].reshape(QS, 2 * HD), og_m.at[par], QS)
+
+        for p in range(NM // 2):
+            qc = slice(p * PQ, (p + 1) * PQ)
             usable = use[0:4, qc] > 0.5
             for h in range(2):
-                rows = slice(h * HD, (h + 1) * HD)
-                cc = pl.ds(pl.multiple_of(h * QS + at, PQ), PQ)
+                cc = slice(h * QS + p * PQ, h * QS + (p + 1) * PQ)
                 st = dot(k2, q_m[par, cc, :], NT)
                 m_raw = jnp.full((1, PQ), -FAR, F32)
                 for kb in range(4):
                     top = jnp.max(st[kb * BS:(kb + 1) * BS], axis=0, keepdims=True)
                     m_raw = jnp.maximum(m_raw, jnp.where(usable[kb:kb + 1], top, -FAR))
                 m = m_raw * C2
-                parts = []
+                dp = dot(v2, og_m[par, cc, :], NT)
+                total = jnp.zeros((BS, PQ), F32)
+                weighted = jnp.zeros((BS, PQ), F32)
                 for kb in range(4):
+                    ks = slice(kb * BS, (kb + 1) * BS)
                     off = jnp.where(usable[kb:kb + 1], m, FAR)
-                    parts.append(jnp.exp2(st[kb * BS:(kb + 1) * BS] * C2 - off))
-                total = jnp.sum(parts[0] + parts[1] + parts[2] + parts[3], axis=0, keepdims=True)
-                prb = jnp.concatenate([v.astype(BF) for v in parts], axis=0)
-                probs[par, :, cc] = prb
-                a_h = dot(v2t[rows, :], prb)
-                a_keep[par, rows, qc] = a_h
-                weighted = jnp.sum(a_h * og_t[rows, qc], axis=0, keepdims=True)
-                total = jnp.maximum(total, 0.5)
-                r = pl.ds(2 * p + h, 1)
+                    pr = jnp.exp2(st[ks] * C2 - off)
+                    total = total + pr
+                    weighted = weighted + pr * dp[ks]
+                    probs[par, ks, cc] = pr.astype(BF)
+                dps[par, :, cc] = dp.astype(BF)
+                total = jnp.maximum(jnp.sum(total, axis=0, keepdims=True), 0.5)
+                weighted = jnp.sum(weighted, axis=0, keepdims=True)
+                r = slice(2 * p + h, 2 * p + h + 1)
                 m_keep[par, r, :] = m
                 stat_own[hp, 0, r, :] = m + jnp.log2(total)
                 stat_own[hp, 1, r, :] = weighted / total
-            return 0
-
-        lax.fori_loop(0, NM // 2, step, 0)
 
         def share(d, _):
             send(stat_own.at[hp], stat_got.at[hp, d - 1], stat_sem.at[0, hp], stat_sem.at[1, hp], peer(d)).start()
@@ -269,35 +262,33 @@
         delta_all = functools.reduce(jnp.add, [w * v for w, v in zip(ws, dlt)]) / total
         m_keep[par] = jnp.exp2(m_keep[par] - (top + jnp.log2(total)))
         d_keep[...] = delta_all
-        k2t = flip(kv[0, :, :, cols].reshape(KS, 2 * HD)).astype(BF)
-        v2 = kv[1, :, :, cols].reshape(KS, 2 * HD)
-
-        def step(p, _):
-            at = pl.multiple_of(p * PQ, PQ)
-            qc = pl.ds(at, PQ)
+        split_heads(kv[0, :, :, cols].reshape(KS, 2 * HD), k_m, KS)
+        split_heads(kv[1, :, :, cols].reshape(KS, 2 * HD), v_m, KS)
+
+        for p in range(NM // 2):
+            att = jnp.zeros((PQ, 2 * HD), F32)
+            dq = jnp.zeros((PQ, 2 * HD), F32)
             for h in range(2):
-                rows = slice(h * HD, (h + 1) * HD)
-                cc = pl.ds(pl.multiple_of(h * QS + at, PQ), PQ)
-                r = pl.ds(2 * p + h, 1)
-                w = m_keep[par, r, :]
-                dp = dot(v2, og_m[par, cc, :], NT)
-                qf = probs[par, :, cc].astype(F32) * w
-                ds = (qf * (dp - d_keep[r, :])).astype(BF)
-                probs[par, :, cc] = qf.astype(BF)
-                dss[:, cc] = ds
-                dq = (dot(k2t[rows, :], ds) * SCALE).astype(BF)
-                at_ = (a_keep[par, rows, qc] * w).astype(BF)
-                for e in range(2):
-                    b = 2 * p + e
-                    x, y = lax.rem(b, NX), b // NX
-                    aq[hp, x, y, 0, rows, :] = at_[:, e * BS:(e + 1) * BS]
-                    aq[hp, x, y, 1, rows, :] = dq[:, e * BS:(e + 1) * BS]
-            return 0
-
-        lax.fori_loop(0, NM // 2, step, 0)
+                cc = slice(h * QS + p * PQ, h * QS + (p + 1) * PQ)
+                r = slice(2 * p + h, 2 * p + h + 1)
+                qf = probs[par, :, cc].astype(F32) * m_keep[par, r, :]
+                qb = qf.astype(BF)
+                ds = (qf * (dps[par, :, cc].astype(F32) - d_keep[r, :])).astype(BF)
+                probs[par, :, cc] = qb
+                dps[par, :, cc] = ds
+                hk = slice(h * KS, (h + 1) * KS)
+                att = att + dot(qb, v_m[hk, :], TN)
+                dq = dq + dot(ds, k_m[hk, :], TN)
+            att = att.astype(BF)
+            dq = (dq * SCALE).astype(BF)
+            for e in range(2):
+                b = 2 * p + e
+                x, y = b % NX, b // NX
+                aq[hp, x, y, 0] = att[e * BS:(e + 1) * BS]
+                aq[hp, x, y, 1] = dq[e * BS:(e + 1) * BS]
         for cp in x1_copies(hp):
             cp.start()
-        dk = (dot(dss[...], q_m[par]) * SCALE).reshape(2, 2 * BS, 2 * HD)
+        dk = (dot(dps[par], q_m[par]) * SCALE).reshape(2, 2 * BS, 2 * HD)
         dv = dot(probs[par], og_m[par]).reshape(2, 2 * BS, 2 * HD)
         mine = core == 0
         c_keep[hp, 0] = jnp.where(mine, dk[0], dk[1])
@@ -376,8 +367,8 @@
             out[:, :, cols] = total.reshape(2, 8, 2 * HD)
         y_copy(hp).wait_recv()
         both = y_keep[hp] + y_got[hp].astype(F32)
-        att_out[0, :, cols] = both[0].T.astype(BF)
-        qg_out[0, :, cols] = both[1].T
+        att_out[0, :, cols] = both[0].astype(BF)
+        qg_out[0, :, cols] = both[1]
         stat_all(hp).wait_send()
         for cp in x1_copies(hp) + x2_copies(hp):
             cp.wait_send()
@@ -448,20 +439,20 @@
             pltpu.VMEM((8, QS), F32),
             pltpu.VMEM((2, 2 * QS, w2), BF),
             pltpu.VMEM((2, 2 * QS, w2), BF),
-            pltpu.VMEM((w2, QS), F32),
+            pltpu.VMEM((2 * KS, w2), BF),
+            pltpu.VMEM((2 * KS, w2), BF),
             pltpu.VMEM((2, KS, 2 * QS), BF),
-            pltpu.VMEM((KS, 2 * QS), BF),
-            pltpu.VMEM((2, w2, QS), F32),
+            pltpu.VMEM((2, KS, 2 * QS), BF),
             pltpu.VMEM((2, 8, PQ), F32),
             pltpu.VMEM((8, PQ), F32),
             pltpu.VMEM((NC, 2, 8, PQ), F32),
             pltpu.VMEM((NC, NM - 1, 2, 8, PQ), F32),
-            pltpu.VMEM((NC, NX, NY, 2, w2, BS), BF),
-            pltpu.VMEM((NC, 2, 2, w2, BS), BF),
-            pltpu.VMEM((NC, 2, NY, 2, w2, BS), BF),
-            pltpu.VMEM((NC, 2, w2, BS), F32),
-            pltpu.VMEM((NC, 2, w2, BS), BF),
-            pltpu.VMEM((NC, 2, w2, BS), BF),
+            pltpu.VMEM((NC, NX, NY, 2, BS, w2), BF),
+            pltpu.VMEM((NC, 2, 2, BS, w2), BF),
+            pltpu.VMEM((NC, 2, NY, 2, BS, w2), BF),
+            pltpu.VMEM((NC, 2, BS, w2), F32),
+            pltpu.VMEM((NC, 2, BS, w2), BF),
+            pltpu.VMEM((NC, 2, BS, w2), BF),
             pltpu.VMEM((NC, 2, 2 * BS, w2), F32),
             pltpu.VMEM((NC, 2, 2 * BS, w2), BF),
             pltpu.VMEM((NC, 2, 2 * BS, w2), BF),

time: 68.7 us -> 58.9 us (0.86)
  Pallas kernels: 67.9 us -> 57.6 us
    pallas_call x1, Pallas kernels: 66.2 us -> 55.8 us  [local(): pl.pallas_call(kernel, out_shape=out_shape, in_specs=[hbm] * 7, out_specs...]
where the time goes in v4:
time: 58.9 us; the launch traced here: 58.3 us
  Pallas kernels  57.6 us (98%)
  between operations  0.64 us (1%)
    pallas_call x1, Pallas kernels, local(): pl.pallas_call(kernel, out_shape=out_shape, in_specs=[hbm] * 7, out_specs...  55.8 us
    pallas_call x1, Pallas kernels, local(): pl.pallas_call(write_out, out_shape=out_shape, in_specs=[vmem] * 4, out_s...  1.78 us

profile of v4, /device:TPU:2, one launch (start us, length us, event | category | flops | bytes accessed | tf_op | source)
XLA Modules:
  0.0 58.3 jit_solution(15394810463874600263)
XLA Ops:
  0.6 55.8 %sparse_attention.1 = (bf16[1,128,512]{2,1,0:T(8,128)(2,1)}, f32[1,128,512]{2,1,0:T(8,128)}, f32[2,8,512]{2,1,0:T(8,128)}, f32[2,8,512]{2,1,0:T(8,128)}) custom-call(bf16[2048,512]{1,0:T(8,128)(2,1)} %queries.1, s32[1,2048]{1,0:T(1,128)} %order.1, bf16[2,128,512]{2,1,0:T(8,128)(2,1)} %keys.1, bf16[2,128,512]{2,1,0:T(8,128)(2,1)} %values.1, s32[1,16]{1,0:T(1,128)} %counts.1, ...), custom_call_target="tpu_custom_call" | custom-call | tf_op jit(solution)/shard_map/sparse_attention/pallas_call | solution.py:426
  56.5 1.8 %write_out.1 = (bf16[1,128,512]{2,1,0:T(8,128)(2,1)}, f32[1,128,512]{2,1,0:T(8,128)}, f32[2,8,512]{2,1,0:T(8,128)}, f32[2,8,512]{2,1,0:T(8,128)}) custom-call(bf16[1,128,512]{2,1,0:T(8,128)(2,1)} %get-tuple-element.8.refs_0_, f32[1,128,512]{2,1,0:T(8,128)} %get-tuple-element.9.refs_1_, f32[2,8,512]{2,1,0:T(8,128)} %get-tuple-element.10.refs_2_, ...), custom_call_target="tpu_custom_call" | custom-call | tf_op jit(solution)/shard_map/write_out/pallas_call | solution.py:475

commit v5 on v4

--- a/solution.py
+++ b/solution.py
@@ -52,6 +52,7 @@
     order_v,
     counts_v,
     listing_v,
+    pick,
     serial,
     og,
     kv,
@@ -63,9 +64,9 @@
     probs,
     dps,
     m_keep,
-    d_keep,
     stat_own,
     stat_got,
+    fin_got,
     aq,
     x1_got,
     x2_got,
@@ -80,6 +81,7 @@
     load_sem,
     kv_sem,
     stat_sem,
+    fin_sem,
     x1_sem,
     x2_sem,
     y_sem,
@@ -115,20 +117,6 @@
             src_ref=src, dst_ref=dst, send_sem=send_sem, recv_sem=recv_sem,
             device_id=device, device_id_type=MESH,
         )
-
-    barrier = pltpu.get_barrier_semaphore()
-    pl.semaphore_signal(barrier, inc=1, device_id=mate, device_id_type=MESH)
-
-    def hello_ka(d, _):
-        pl.semaphore_signal(barrier, inc=1, device_id=peer(d), device_id_type=MESH)
-        return 0
-
-    def hello_pb(d, _):
-        pl.semaphore_signal(barrier, inc=1, device_id=slab(d), device_id_type=MESH)
-        return 0
-
-    lax.fori_loop(1, NM, hello_ka, 0)
-    lax.fori_loop(1, NP, hello_pb, 0)
 
     own2 = pl.ds(2 * core, 2)
     load_q = pltpu.make_async_copy(queries, qbuf, load_sem.at[0])
@@ -147,6 +135,21 @@
     ]
     for cp in load_small + [load_q] + load_kv + load_og:
         cp.start()
+
+    barrier = pltpu.get_barrier_semaphore()
+    pl.semaphore_signal(barrier, inc=1, device_id=mate, device_id_type=MESH)
+
+    def hello_ka(d, _):
+        pl.semaphore_signal(barrier, inc=1, device_id=peer(d), device_id_type=MESH)
+        return 0
+
+    def hello_pb(d, _):
+        pl.semaphore_signal(barrier, inc=1, device_id=slab(d), device_id_type=MESH)
+        return 0
+
+    lax.fori_loop(1, NM, hello_ka, 0)
+    lax.fori_loop(1, NP, hello_pb, 0)
+
     for cp in load_small:
         cp.wait()
 
@@ -165,31 +168,33 @@
     spread = jnp.where(e0 == 2 * (e1 // BS) + core, 1.0, 0.0)
     use[...] = dot(joined.astype(BF), spread.astype(BF))
 
+    half = D // 2
+    for b in range(NM):
+        at = pl.multiple_of((2 * b + core) * BS, BS)
+        column = jnp.broadcast_to(order_v[:, pl.ds(at, BS)], (BS, BS)).T
+        lanes = lax.broadcasted_iota(jnp.int32, (BS, BS), 1)
+        for n in range(16):
+            pick[b * BS:(b + 1) * BS, n * BS:(n + 1) * BS] = jnp.where(
+                column == lanes + n * BS, 1.0, 0.0
+            ).astype(BF)
     load_q.wait()
+
+    def gather(c):
+        def part(t, _):
+            rows = pl.ds(pl.multiple_of(t * 4 * BS, 4 * BS), 4 * BS)
+            serial[rows, c * half:(c + 1) * half] = dot(
+                pick[rows, :], qbuf[:, c * half:(c + 1) * half]
+            ).astype(BF)
+            return 0
+
+        lax.fori_loop(0, 2, part, 0)
 
     send_k = send(keys, kv.at[0, own2], kv_sem.at[0, 0], kv_sem.at[1, 0], mate)
     send_v = send(values, kv.at[1, own2], kv_sem.at[0, 1], kv_sem.at[1, 1], mate)
-
-    def gather(t, _):
-        @pl.when(t == 1)
-        def _():
-            pl.semaphore_wait(barrier, 1 + (NM - 1) + (NP - 1))
-            send_k.start()
-            send_v.start()
-
-        picks = []
-        for e in range(4):
-            at = pl.multiple_of((8 * t + 2 * e + core) * BS, BS)
-            column = jnp.broadcast_to(order_v[:, pl.ds(at, BS)], (BS, BS)).T
-            lanes = lax.broadcasted_iota(jnp.int32, (BS, BS), 1)
-            picks.append(jnp.concatenate(
-                [jnp.where(column == lanes + n * BS, 1.0, 0.0).astype(BF) for n in range(16)], axis=1
-            ))
-        pick = jnp.concatenate(picks, axis=0)
-        serial[pl.ds(pl.multiple_of(t * 4 * BS, 4 * BS), 4 * BS), :] = dot(pick, qbuf[...]).astype(BF)
-        return 0
-
-    lax.fori_loop(0, 2, gather, 0)
+    pl.semaphore_wait(barrier, 1 + (NM - 1) + (NP - 1))
+    send_k.start()
+    send_v.start()
+    gather(0)
     for cp in load_kv + load_og:
         cp.wait()
     send_k.wait()
@@ -238,11 +243,17 @@
                 weighted = jnp.sum(weighted, axis=0, keepdims=True)
                 r = slice(2 * p + h, 2 * p + h + 1)
                 m_keep[par, r, :] = m
-                stat_own[hp, 0, r, :] = m + jnp.log2(total)
-                stat_own[hp, 1, r, :] = weighted / total
+                lse = m + jnp.log2(total)
+                delta = weighted / total
+                for e in range(2):
+                    stat_own[hp, 2 * p + e, h:h + 1, :] = lse[:, e * BS:(e + 1) * BS]
+                    stat_own[hp, 2 * p + e, 2 + h:3 + h, :] = delta[:, e * BS:(e + 1) * BS]
 
         def share(d, _):
-            send(stat_own.at[hp], stat_got.at[hp, d - 1], stat_sem.at[0, hp], stat_sem.at[1, hp], peer(d)).start()
+            send(
+                stat_own.at[hp, lax.rem(chip + d, NM)], stat_got.at[hp, d - 1],
+                stat_sem.at[0, hp], stat_sem.at[1, hp], peer(d),
+            ).start()
             return 0
 
         lax.fori_loop(1, NM, share, 0)
@@ -250,85 +261,142 @@
     def stat_all(hp):
         return send(stat_got.at[hp], stat_got.at[hp], stat_sem.at[0, hp], stat_sem.at[1, hp], right)
 
-    def second(hp):
-        par = lax.rem(hp, 2)
-        cols = lanes_of(hp)
+    def fin_all(hp):
+        got = fin_got.at[hp, pl.ds(0, NM - 1)]
+        return send(got, got, fin_sem.at[0, hp], fin_sem.at[1, hp], right)
+
+    def combine(hp):
         stat_all(hp).wait_recv()
-        lse = [stat_own[hp, 0]] + [stat_got[hp, d, 0] for d in range(NM - 1)]
-        dlt = [stat_own[hp, 1]] + [stat_got[hp, d, 1] for d in range(NM - 1)]
+        own = stat_own[hp, chip]
+        parts = [own] + [stat_got[hp, d] for d in range(NM - 1)]
+        lse = [v[0:2] for v in parts]
         top = functools.reduce(jnp.maximum, lse)
         ws = [jnp.exp2(v - top) for v in lse]
         total = functools.reduce(jnp.add, ws)
-        delta_all = functools.reduce(jnp.add, [w * v for w, v in zip(ws, dlt)]) / total
-        m_keep[par] = jnp.exp2(m_keep[par] - (top + jnp.log2(total)))
-        d_keep[...] = delta_all
-        split_heads(kv[0, :, :, cols].reshape(KS, 2 * HD), k_m, KS)
+        delta = functools.reduce(jnp.add, [w * v[2:4] for w, v in zip(ws, parts)]) / total
+        fin_got[hp, NM - 1, 0:2] = top + jnp.log2(total)
+        fin_got[hp, NM - 1, 2:4] = delta
+
+        def share(d, _):
+            send(
+                fin_got.at[hp, NM - 1], fin_got.at[hp, d - 1],
+                fin_sem.at[0, hp], fin_sem.at[1, hp], peer(d),
+            ).start()
+            return 0
+
+        lax.fori_loop(1, NM, share, 0)
+
+    def fin_row(hp, p, row):
+        return jnp.concatenate(
+            [fin_got[hp, lax.rem(chip - (2 * p + e) + 2 * NM - 1, NM), row:row + 1, :] for e in range(2)], axis=1
+        )
+
+    def put(hp, kind, p, block):
+        for e in range(2):
+            b = 2 * p + e
+            aq[hp, kind, b % NX, b // NX] = block[e * BS:(e + 1) * BS]
+
+    def hand_over(hp, kind, grad):
+        grad = grad.reshape(2, 2 * BS, 2 * HD)
+        mine = core == 0
+        c_keep[hp, kind] = jnp.where(mine, grad[0], grad[1])
+        c_send[hp, kind] = jnp.where(mine, grad[1], grad[0]).astype(BF)
+        c_copy(hp, kind).start()
+
+    def second_v(hp):
+        par = lax.rem(hp, 2)
+        cols = lanes_of(hp)
+        fin_all(hp).wait_recv()
         split_heads(kv[1, :, :, cols].reshape(KS, 2 * HD), v_m, KS)
-
         for p in range(NM // 2):
             att = jnp.zeros((PQ, 2 * HD), F32)
+            for h in range(2):
+                cc = slice(h * QS + p * PQ, h * QS + (p + 1) * PQ)
+                r = slice(2 * p + h, 2 * p + h + 1)
+                w = jnp.exp2(m_keep[par, r, :] - fin_row(hp, p, h))
+                qb = (probs[par, :, cc].astype(F32) * w).astype(BF)
+                probs[par, :, cc] = qb
+                att = att + dot(qb, v_m[h * KS:(h + 1) * KS, :], TN)
+            put(hp, 0, p, att.astype(BF))
+        for cp in x1_copies(hp, 0):
+            cp.start()
+
+    def value_part(hp):
+        par = lax.rem(hp, 2)
+        hand_over(hp, 1, dot(probs[par], og_m[par]))
+
+    def second_k(hp):
+        par = lax.rem(hp, 2)
+        cols = lanes_of(hp)
+        split_heads(kv[0, :, :, cols].reshape(KS, 2 * HD), k_m, KS)
+        for p in range(NM // 2):
             dq = jnp.zeros((PQ, 2 * HD), F32)
             for h in range(2):
                 cc = slice(h * QS + p * PQ, h * QS + (p + 1) * PQ)
-                r = slice(2 * p + h, 2 * p + h + 1)
-                qf = probs[par, :, cc].astype(F32) * m_keep[par, r, :]
-                qb = qf.astype(BF)
-                ds = (qf * (dps[par, :, cc].astype(F32) - d_keep[r, :])).astype(BF)
-                probs[par, :, cc] = qb
+                ds = (
+                    probs[par, :, cc].astype(F32) * (dps[par, :, cc].astype(F32) - fin_row(hp, p, 2 + h))
+                ).astype(BF)
                 dps[par, :, cc] = ds
-                hk = slice(h * KS, (h + 1) * KS)
-                att = att + dot(qb, v_m[hk, :], TN)
-                dq = dq + dot(ds, k_m[hk, :], TN)
-            att = att.astype(BF)
-            dq = (dq * SCALE).astype(BF)
-            for e in range(2):
-                b = 2 * p + e
-                x, y = b % NX, b // NX
-                aq[hp, x, y, 0] = att[e * BS:(e + 1) * BS]
-                aq[hp, x, y, 1] = dq[e * BS:(e + 1) * BS]
-        for cp in x1_copies(hp):
+                dq = dq + dot(ds, k_m[h * KS:(h + 1) * KS, :], TN)
+            put(hp, 1, p, (dq * SCALE).astype(BF))
+        for cp in x1_copies(hp, 1):
             cp.start()
-        dk = (dot(dps[par], q_m[par]) * SCALE).reshape(2, 2 * BS, 2 * HD)
-        dv = dot(probs[par], og_m[par]).reshape(2, 2 * BS, 2 * HD)
-        mine = core == 0
-        c_keep[hp, 0] = jnp.where(mine, dk[0], dk[1])
-        c_keep[hp, 1] = jnp.where(mine, dv[0], dv[1])
-        c_send[hp, 0] = jnp.where(mine, dk[1], dk[0]).astype(BF)
-        c_send[hp, 1] = jnp.where(mine, dv[1], dv[0]).astype(BF)
-        c_copy(hp).start()
-
-    def x1_copies(hp):
-        return (
-            send(aq.at[hp, xo, 0], x1_got.at[hp, 0], x1_sem.at[0, hp, 0], x1_sem.at[1, hp, 0], right),
-            send(aq.at[hp, xo, 1], x1_got.at[hp, 1], x1_sem.at[0, hp, 1], x1_sem.at[1, hp, 1], left),
+
+    def key_part(hp):
+        par = lax.rem(hp, 2)
+        hand_over(hp, 0, dot(dps[par], q_m[par]) * SCALE)
+
+    def x1_copies(hp, kind):
+        return tuple(
+            send(
+                aq.at[hp, kind, xo, way], x1_got.at[hp, kind, way],
+                x1_sem.at[0, hp, kind, way], x1_sem.at[1, hp, kind, way], (right, left)[way],
+            ) for way in range(2)
         )
 
-    def x2_copies(hp):
-        return (
-            send(aq.at[hp, xr], x2_got.at[hp, 0], x2_sem.at[0, hp, 0], x2_sem.at[1, hp, 0], right),
-            send(aq.at[hp, xl], x2_got.at[hp, 1], x2_sem.at[0, hp, 1], x2_sem.at[1, hp, 1], left),
+    def x2_copies(hp, kind):
+        return tuple(
+            send(
+                aq.at[hp, kind, (xr, xl)[way]], x2_got.at[hp, kind, way],
+                x2_sem.at[0, hp, kind, way], x2_sem.at[1, hp, kind, way], (right, left)[way],
+            ) for way in range(2)
         )
 
-    def y_copy(hp):
-        return send(y_send.at[hp], y_got.at[hp], y_sem.at[0, hp], y_sem.at[1, hp], across)
-
-    def c_copy(hp):
-        return send(c_send.at[hp], c_got.at[hp], c_sem.at[0, hp], c_sem.at[1, hp], mate)
+    def y_copy(hp, kind):
+        return send(y_send.at[hp, kind], y_got.at[hp, kind], y_sem.at[0, hp, kind], y_sem.at[1, hp, kind], across)
+
+    def c_copy(hp, kind):
+        return send(c_send.at[hp, kind], c_got.at[hp, kind], c_sem.at[0, hp, kind], c_sem.at[1, hp, kind], mate)
 
     def z_all(hp):
         return send(z_got.at[hp], z_got.at[hp], z_sem.at[0, hp], z_sem.at[1, hp], slab(1))
 
-    def relay_x(hp):
-        for cp in x1_copies(hp):
+    def relay_x(hp, kind):
+        for cp in x1_copies(hp, kind):
             cp.wait_recv()
-        aq[hp, xr, 0] = (aq[hp, xr, 0].astype(F32) + x1_got[hp, 0].astype(F32)).astype(BF)
-        aq[hp, xl, 1] = (aq[hp, xl, 1].astype(F32) + x1_got[hp, 1].astype(F32)).astype(BF)
-        for cp in x2_copies(hp):
+        for way, x in ((0, xr), (1, xl)):
+            aq[hp, kind, x, way] = (aq[hp, kind, x, way].astype(F32) + x1_got[hp, kind, way].astype(F32)).astype(BF)
+        for cp in x2_copies(hp, kind):
             cp.start()
 
+    def relay_y(hp, kind):
+        for cp in x2_copies(hp, kind):
+            cp.wait_recv()
+
+        def total(y):
+            return (
+                aq[hp, kind, xi, y].astype(F32)
+                + x2_got[hp, kind, 0, y].astype(F32)
+                + x2_got[hp, kind, 1, y].astype(F32)
+            )
+
+        y_send[hp, kind] = total(yo).astype(BF)
+        y_copy(hp, kind).start()
+        y_keep[hp, kind] = total(yi)
+
     def relay_c(hp):
-        c_copy(hp).wait_recv()
         for a in range(2):
+            c_copy(hp, a).wait_recv()
             total = c_keep[hp, a] + c_got[hp, a].astype(F32)
             total = total.reshape(2, NP, 8, 2 * HD).transpose(1, 0, 2, 3)
             z_send[hp, :, a] = total.reshape(NP, 16, 2 * HD).astype(BF)
@@ -342,38 +410,24 @@
 
         lax.fori_loop(1, NP, share, 0)
 
-    def relay_y(hp):
-        for cp in x2_copies(hp):
-            cp.wait_recv()
-
-        def total(y):
-            return (
-                aq[hp, xi, y].astype(F32)
-                + x2_got[hp, 0, y].astype(F32)
-                + x2_got[hp, 1, y].astype(F32)
-            )
-
-        y_send[hp] = total(yo).astype(BF)
-        y_copy(hp).start()
-        y_keep[hp] = total(yi)
-
     def finish(hp):
         cols = lanes_of(hp)
+        for kind, out in ((0, att_out), (1, qg_out)):
+            y_copy(hp, kind).wait_recv()
+            out[0, :, cols] = (y_keep[hp, kind] + y_got[hp, kind].astype(F32)).astype(out.dtype)
         z_all(hp).wait_recv()
         for a, out in ((0, kg_out), (1, vg_out)):
             total = z_send[hp, pb, a].astype(F32)
             for d in range(NP - 1):
                 total = total + z_got[hp, d, a].astype(F32)
             out[:, :, cols] = total.reshape(2, 8, 2 * HD)
-        y_copy(hp).wait_recv()
-        both = y_keep[hp] + y_got[hp].astype(F32)
-        att_out[0, :, cols] = both[0].astype(BF)
-        qg_out[0, :, cols] = both[1]
         stat_all(hp).wait_send()
-        for cp in x1_copies(hp) + x2_copies(hp):
-            cp.wait_send()
-        y_copy(hp).wait_send()
-        c_copy(hp).wait_send()
+        fin_all(hp).wait_send()
+        for kind in range(2):
+            for cp in x1_copies(hp, kind) + x2_copies(hp, kind):
+                cp.wait_send()
+            y_copy(hp, kind).wait_send()
+            c_copy(hp, kind).wait_send()
         z_all(hp).wait_send()
 
     def turn(s, _):
@@ -381,26 +435,45 @@
         def _():
             first(s)
 
-        @pl.when((s >= 2) & (s < NC + 2))
-        def _():
-            relay_x(s - 2)
+        @pl.when(s == 0)
+        def _():
+            gather(1)
+
+        @pl.when(s >= 2)
+        def _():
+            relay_x(s - 2, 1)
+            relay_y(s - 2, 0)
             relay_c(s - 2)
 
-        @pl.when((s >= 1) & (s < NC + 1))
-        def _():
-            second(s - 1)
-
-        @pl.when((s >= 2) & (s < NC + 2))
-        def _():
-            relay_y(s - 2)
-
-        @pl.when(s >= 3)
-        def _():
-            finish(s - 3)
+        @pl.when((s >= 1) & (s <= NC))
+        def _():
+            second_v(s - 1)
+
+        @pl.when(s >= 2)
+        def _():
+            relay_y(s - 2, 1)
+
+        @pl.when((s >= 1) & (s <= NC))
+        def _():
+            value_part(s - 1)
+
+        @pl.when(s < NC)
+        def _():
+            combine(s)
+
+        @pl.when((s >= 1) & (s <= NC))
+        def _():
+            second_k(s - 1)
+            relay_x(s - 1, 0)
+            key_part(s - 1)
+
+        @pl.when(s >= 2)
+        def _():
+            finish(s - 2)
 
         return 0
 
-    lax.fori_loop(0, NC + 3, turn, 0)
+    lax.fori_loop(0, NC + 2, turn, 0)
 
 
 def write_out(*refs):
@@ -433,6 +506,7 @@
             pltpu.VMEM((1, NP * BS), jnp.int32),
             pltpu.VMEM((1, NP), jnp.int32),
             pltpu.VMEM((1, 256), jnp.int32),
+            pltpu.VMEM((QS, NP * BS), BF),
             pltpu.VMEM((QS, D), BF),
             pltpu.VMEM((NM, BS, D), BF),
             pltpu.VMEM((2, 4, BS, D), BF),
@@ -444,12 +518,12 @@
             pltpu.VMEM((2, KS, 2 * QS), BF),
             pltpu.VMEM((2, KS, 2 * QS), BF),
             pltpu.VMEM((2, 8, PQ), F32),
-            pltpu.VMEM((8, PQ), F32),
-            pltpu.VMEM((NC, 2, 8, PQ), F32),
-            pltpu.VMEM((NC, NM - 1, 2, 8, PQ), F32),
-            pltpu.VMEM((NC, NX, NY, 2, BS, w2), BF),
+            pltpu.VMEM((NC, NM, 4, BS), F32),
+            pltpu.VMEM((NC, NM - 1, 4, BS), F32),
+            pltpu.VMEM((NC, NM, 4, BS), F32),
+            pltpu.VMEM((NC, 2, NX, NY, BS, w2), BF),
             pltpu.VMEM((NC, 2, 2, BS, w2), BF),
-            pltpu.VMEM((NC, 2, NY, 2, BS, w2), BF),
+            pltpu.VMEM((NC, 2, 2, NY, BS, w2), BF),
             pltpu.VMEM((NC, 2, BS, w2), F32),
             pltpu.VMEM((NC, 2, BS, w2), BF),
             pltpu.VMEM((NC, 2, BS, w2), BF),
@@ -461,10 +535,11 @@
             dma((6 + NM,)),
             dma((2, 2)),
             dma((2, NC)),
+            dma((2, NC)),
+            dma((2, NC, 2, 2)),
+            dma((2, NC, 2, 2)),
             dma((2, NC, 2)),
             dma((2, NC, 2)),
-            dma((2, NC)),
-            dma((2, NC)),
             dma((2, NC)),
         ],
         compiler_params=pltpu.CompilerParams(

time: 58.9 us -> 73.3 us (1.24)
  Pallas kernels: 57.6 us -> 72.5 us
    pallas_call x1, Pallas kernels: 55.8 us -> 70.7 us  [local(): pl.pallas_call(kernel, out_shape=out_shape, in_specs=[hbm] * 7, out_specs...]
where the time goes in v5:
time: 73.3 us; the launch traced here: 73.1 us
  Pallas kernels  72.5 us (99%)
    pallas_call x1, Pallas kernels, local(): pl.pallas_call(kernel, out_shape=out_shape, in_specs=[hbm] * 7, out_specs...  70.7 us
    pallas_call x1, Pallas kernels, local(): pl.pallas_call(write_out, out_shape=out_shape, in_specs=[vmem] * 4, out_s...  1.78 us

profile of v5, /device:TPU:2, one launch (start us, length us, event | category | flops | bytes accessed | tf_op | source)
XLA Modules:
  0.0 73.1 jit_solution(15986595460288678274)
XLA Ops:
  0.6 70.7 %sparse_attention.1 = (bf16[1,128,512]{2,1,0:T(8,128)(2,1)}, f32[1,128,512]{2,1,0:T(8,128)}, f32[2,8,512]{2,1,0:T(8,128)}, f32[2,8,512]{2,1,0:T(8,128)}) custom-call(bf16[2048,512]{1,0:T(8,128)(2,1)} %queries.1, s32[1,2048]{1,0:T(1,128)} %order.1, bf16[2,128,512]{2,1,0:T(8,128)(2,1)} %keys.1, bf16[2,128,512]{2,1,0:T(8,128)(2,1)} %values.1, s32[1,16]{1,0:T(1,128)} %counts.1, ...), custom_call_target="tpu_custom_call" | custom-call | tf_op jit(solution)/shard_map/sparse_attention/pallas_call | solution.py:499
  71.3 1.8 %write_out.1 = (bf16[1,128,512]{2,1,0:T(8,128)(2,1)}, f32[1,128,512]{2,1,0:T(8,128)}, f32[2,8,512]{2,1,0:T(8,128)}, f32[2,8,512]{2,1,0:T(8,128)}) custom-call(bf16[1,128,512]{2,1,0:T(8,128)(2,1)} %get-tuple-element.8.refs_0_, f32[1,128,512]{2,1,0:T(8,128)} %get-tuple-element.9.refs_1_, f32[2,8,512]{2,1,0:T(8,128)} %get-tuple-element.10.refs_2_, ...), custom_call_target="tpu_custom_call" | custom-call | tf_op jit(solution)/shard_map/write_out/pallas_call | solution.py:550

commit v6 on v4

--- a/solution.py
+++ b/solution.py
@@ -116,20 +116,6 @@
             device_id=device, device_id_type=MESH,
         )
 
-    barrier = pltpu.get_barrier_semaphore()
-    pl.semaphore_signal(barrier, inc=1, device_id=mate, device_id_type=MESH)
-
-    def hello_ka(d, _):
-        pl.semaphore_signal(barrier, inc=1, device_id=peer(d), device_id_type=MESH)
-        return 0
-
-    def hello_pb(d, _):
-        pl.semaphore_signal(barrier, inc=1, device_id=slab(d), device_id_type=MESH)
-        return 0
-
-    lax.fori_loop(1, NM, hello_ka, 0)
-    lax.fori_loop(1, NP, hello_pb, 0)
-
     own2 = pl.ds(2 * core, 2)
     load_q = pltpu.make_async_copy(queries, qbuf, load_sem.at[0])
     load_small = [
@@ -147,6 +133,21 @@
     ]
     for cp in load_small + [load_q] + load_kv + load_og:
         cp.start()
+
+    barrier = pltpu.get_barrier_semaphore()
+    pl.semaphore_signal(barrier, inc=1, device_id=mate, device_id_type=MESH)
+
+    def hello_ka(d, _):
+        pl.semaphore_signal(barrier, inc=1, device_id=peer(d), device_id_type=MESH)
+        return 0
+
+    def hello_pb(d, _):
+        pl.semaphore_signal(barrier, inc=1, device_id=slab(d), device_id_type=MESH)
+        return 0
+
+    lax.fori_loop(1, NM, hello_ka, 0)
+    lax.fori_loop(1, NP, hello_pb, 0)
+
     for cp in load_small:
         cp.wait()
 
@@ -315,8 +316,8 @@
     def c_copy(hp):
         return send(c_send.at[hp], c_got.at[hp], c_sem.at[0, hp], c_sem.at[1, hp], mate)
 
-    def z_all(hp):
-        return send(z_got.at[hp], z_got.at[hp], z_sem.at[0, hp], z_sem.at[1, hp], slab(1))
+    def z_all(pair):
+        return send(z_got.at[pair], z_got.at[pair], z_sem.at[0, pair], z_sem.at[1, pair], slab(1))
 
     def relay_x(hp):
         for cp in x1_copies(hp):
@@ -328,19 +329,22 @@
 
     def relay_c(hp):
         c_copy(hp).wait_recv()
+        pair = hp // 2
         for a in range(2):
             total = c_keep[hp, a] + c_got[hp, a].astype(F32)
             total = total.reshape(2, NP, 8, 2 * HD).transpose(1, 0, 2, 3)
-            z_send[hp, :, a] = total.reshape(NP, 16, 2 * HD).astype(BF)
+            z_send[pair, :, 2 * lax.rem(hp, 2) + a] = total.reshape(NP, 16, 2 * HD).astype(BF)
 
         def share(d, _):
             send(
-                z_send.at[hp, lax.rem(pb + d, NP)], z_got.at[hp, d - 1],
-                z_sem.at[0, hp], z_sem.at[1, hp], slab(d),
+                z_send.at[pair, lax.rem(pb + d, NP)], z_got.at[pair, d - 1],
+                z_sem.at[0, pair], z_sem.at[1, pair], slab(d),
             ).start()
             return 0
 
-        lax.fori_loop(1, NP, share, 0)
+        @pl.when(lax.rem(hp, 2) == 1)
+        def _():
+            lax.fori_loop(1, NP, share, 0)
 
     def relay_y(hp):
         for cp in x2_copies(hp):
@@ -359,12 +363,6 @@
 
     def finish(hp):
         cols = lanes_of(hp)
-        z_all(hp).wait_recv()
-        for a, out in ((0, kg_out), (1, vg_out)):
-            total = z_send[hp, pb, a].astype(F32)
-            for d in range(NP - 1):
-                total = total + z_got[hp, d, a].astype(F32)
-            out[:, :, cols] = total.reshape(2, 8, 2 * HD)
         y_copy(hp).wait_recv()
         both = y_keep[hp] + y_got[hp].astype(F32)
         att_out[0, :, cols] = both[0].astype(BF)
@@ -374,7 +372,19 @@
             cp.wait_send()
         y_copy(hp).wait_send()
         c_copy(hp).wait_send()
-        z_all(hp).wait_send()
+
+        @pl.when(lax.rem(hp, 2) == 1)
+        def _():
+            pair = hp // 2
+            z_all(pair).wait_recv()
+            for q in range(2):
+                cols = lanes_of(2 * pair + q)
+                for a, out in ((0, kg_out), (1, vg_out)):
+                    total = z_send[pair, pb, 2 * q + a].astype(F32)
+                    for d in range(NP - 1):
+                        total = total + z_got[pair, d, 2 * q + a].astype(F32)
+                    out[:, :, cols] = total.reshape(2, 8, 2 * HD)
+            z_all(pair).wait_send()
 
     def turn(s, _):
         @pl.when(s < NC)
@@ -456,8 +466,8 @@
             pltpu.VMEM((NC, 2, 2 * BS, w2), F32),
             pltpu.VMEM((NC, 2, 2 * BS, w2), BF),
             pltpu.VMEM((NC, 2, 2 * BS, w2), BF),
-            pltpu.VMEM((NC, NP, 2, 16, w2), BF),
-            pltpu.VMEM((NC, NP - 1, 2, 16, w2), BF),
+            pltpu.VMEM((NC // 2, NP, 4, 16, w2), BF),
+            pltpu.VMEM((NC // 2, NP - 1, 4, 16, w2), BF),
             dma((6 + NM,)),
             dma((2, 2)),
             dma((2, NC)),
@@ -465,7 +475,7 @@
             dma((2, NC, 2)),
             dma((2, NC)),
             dma((2, NC)),
-            dma((2, NC)),
+            dma((2, NC // 2)),
         ],
         compiler_params=pltpu.CompilerParams(
             collective_id=0, has_side_effects=True, vmem_limit_bytes=60 * 1024 * 1024

time: 58.9 us -> 59 us (level)
  no operation moved by 1% of the time
where the time goes in v6:
time: 59 us; the launch traced here: 58.6 us
  Pallas kernels  58 us (98%)
  between operations  0.64 us (1%)
    pallas_call x1, Pallas kernels, local(): pl.pallas_call(kernel, out_shape=out_shape, in_specs=[hbm] * 7, out_specs...  56.2 us
    pallas_call x1, Pallas kernels, local(): pl.pallas_call(write_out, out_shape=out_shape, in_specs=[vmem] * 4, out_s...  1.78 us

profile of v6, /device:TPU:2, one launch (start us, length us, event | category | flops | bytes accessed | tf_op | source)
XLA Modules:
  0.0 58.6 jit_solution(1694854538674512335)
XLA Ops:
  0.6 56.2 %sparse_attention.1 = (bf16[1,128,512]{2,1,0:T(8,128)(2,1)}, f32[1,128,512]{2,1,0:T(8,128)}, f32[2,8,512]{2,1,0:T(8,128)}, f32[2,8,512]{2,1,0:T(8,128)}) custom-call(bf16[2048,512]{1,0:T(8,128)(2,1)} %queries.1, s32[1,2048]{1,0:T(1,128)} %order.1, bf16[2,128,512]{2,1,0:T(8,128)(2,1)} %keys.1, bf16[2,128,512]{2,1,0:T(8,128)(2,1)} %values.1, s32[1,16]{1,0:T(1,128)} %counts.1, ...), custom_call_target="tpu_custom_call" | custom-call | tf_op jit(solution)/shard_map/sparse_attention/pallas_call | solution.py:436
  56.9 1.8 %write_out.1 = (bf16[1,128,512]{2,1,0:T(8,128)(2,1)}, f32[1,128,512]{2,1,0:T(8,128)}, f32[2,8,512]{2,1,0:T(8,128)}, f32[2,8,512]{2,1,0:T(8,128)}) custom-call(bf16[1,128,512]{2,1,0:T(8,128)(2,1)} %get-tuple-element.8.refs_0_, f32[1,128,512]{2,1,0:T(8,128)} %get-tuple-element.9.refs_1_, f32[2,8,512]{2,1,0:T(8,128)} %get-tuple-element.10.refs_2_, ...), custom_call_target="tpu_custom_call" | custom-call | tf_op jit(solution)/shard_map/write_out/pallas_call | solution.py:485

commit v7 on v6

--- a/solution.py
+++ b/solution.py
@@ -205,6 +205,10 @@
         dst[:n] = jnp.where(low, src, none)
         dst[n:] = jnp.where(low, none, src)
 
+    def columns(u):
+        p, h = u // 2, u % 2
+        return slice(h * QS + p * PQ, h * QS + (p + 1) * PQ)
+
     def first(hp):
         par = lax.rem(hp, 2)
         cols = lanes_of(hp)
@@ -213,34 +217,42 @@
         split_heads(serial[:, cols], q_m.at[par], QS)
         split_heads(og[:, :, cols].reshape(QS, 2 * HD), og_m.at[par], QS)
 
-        for p in range(NM // 2):
-            qc = slice(p * PQ, (p + 1) * PQ)
-            usable = use[0:4, qc] > 0.5
-            for h in range(2):
-                cc = slice(h * QS + p * PQ, h * QS + (p + 1) * PQ)
-                st = dot(k2, q_m[par, cc, :], NT)
-                m_raw = jnp.full((1, PQ), -FAR, F32)
-                for kb in range(4):
-                    top = jnp.max(st[kb * BS:(kb + 1) * BS], axis=0, keepdims=True)
-                    m_raw = jnp.maximum(m_raw, jnp.where(usable[kb:kb + 1], top, -FAR))
-                m = m_raw * C2
-                dp = dot(v2, og_m[par, cc, :], NT)
-                total = jnp.zeros((BS, PQ), F32)
-                weighted = jnp.zeros((BS, PQ), F32)
-                for kb in range(4):
-                    ks = slice(kb * BS, (kb + 1) * BS)
-                    off = jnp.where(usable[kb:kb + 1], m, FAR)
-                    pr = jnp.exp2(st[ks] * C2 - off)
-                    total = total + pr
-                    weighted = weighted + pr * dp[ks]
-                    probs[par, ks, cc] = pr.astype(BF)
-                dps[par, :, cc] = dp.astype(BF)
-                total = jnp.maximum(jnp.sum(total, axis=0, keepdims=True), 0.5)
-                weighted = jnp.sum(weighted, axis=0, keepdims=True)
-                r = slice(2 * p + h, 2 * p + h + 1)
-                m_keep[par, r, :] = m
-                stat_own[hp, 0, r, :] = m + jnp.log2(total)
-                stat_own[hp, 1, r, :] = weighted / total
+        def products(u):
+            cc = columns(u)
+            return dot(k2, q_m[par, cc, :], NT), dot(v2, og_m[par, cc, :], NT)
+
+        def softmax(u, st, dp):
+            p, h = u // 2, u % 2
+            cc = columns(u)
+            usable = use[0:4, p * PQ:(p + 1) * PQ] > 0.5
+            m_raw = jnp.full((1, PQ), -FAR, F32)
+            for kb in range(4):
+                top = jnp.max(st[kb * BS:(kb + 1) * BS], axis=0, keepdims=True)
+                m_raw = jnp.maximum(m_raw, jnp.where(usable[kb:kb + 1], top, -FAR))
+            m = m_raw * C2
+            total = jnp.zeros((BS, PQ), F32)
+            weighted = jnp.zeros((BS, PQ), F32)
+            for kb in range(4):
+                ks = slice(kb * BS, (kb + 1) * BS)
+                off = jnp.where(usable[kb:kb + 1], m, FAR)
+                pr = jnp.exp2(st[ks] * C2 - off)
+                total = total + pr
+                weighted = weighted + pr * dp[ks]
+                probs[par, ks, cc] = pr.astype(BF)
+            dps[par, :, cc] = dp.astype(BF)
+            total = jnp.maximum(jnp.sum(total, axis=0, keepdims=True), 0.5)
+            weighted = jnp.sum(weighted, axis=0, keepdims=True)
+            r = slice(u, u + 1)
+            m_keep[par, r, :] = m
+            stat_own[hp, 0, r, :] = m + jnp.log2(total)
+            stat_own[hp, 1, r, :] = weighted / total
+
+        ahead = products(0)
+        for u in range(NM):
+            now = ahead
+            if u + 1 < NM:
+                ahead = products(u + 1)
+            softmax(u, *now)
 
         def share(d, _):
             send(stat_own.at[hp], stat_got.at[hp, d - 1], stat_sem.at[0, hp], stat_sem.at[1, hp], peer(d)).start()
@@ -266,20 +278,26 @@
         split_heads(kv[0, :, :, cols].reshape(KS, 2 * HD), k_m, KS)
         split_heads(kv[1, :, :, cols].reshape(KS, 2 * HD), v_m, KS)
 
-        for p in range(NM // 2):
+        for u in range(NM):
+            probs[par, :, columns(u)] = (
+                probs[par, :, columns(u)].astype(F32) * m_keep[par, u:u + 1, :]
+            ).astype(BF)
+        dv = dot(probs[par], og_m[par]).reshape(2, 2 * BS, 2 * HD)
+
+        def scores_grad(u):
+            cc = columns(u)
+            dps[par, :, cc] = (
+                probs[par, :, cc].astype(F32) * (dps[par, :, cc].astype(F32) - d_keep[u:u + 1, :])
+            ).astype(BF)
+
+        def outputs(p):
             att = jnp.zeros((PQ, 2 * HD), F32)
             dq = jnp.zeros((PQ, 2 * HD), F32)
             for h in range(2):
-                cc = slice(h * QS + p * PQ, h * QS + (p + 1) * PQ)
-                r = slice(2 * p + h, 2 * p + h + 1)
-                qf = probs[par, :, cc].astype(F32) * m_keep[par, r, :]
-                qb = qf.astype(BF)
-                ds = (qf * (dps[par, :, cc].astype(F32) - d_keep[r, :])).astype(BF)
-                probs[par, :, cc] = qb
-                dps[par, :, cc] = ds
+                cc = columns(2 * p + h)
                 hk = slice(h * KS, (h + 1) * KS)
-                att = att + dot(qb, v_m[hk, :], TN)
-                dq = dq + dot(ds, k_m[hk, :], TN)
+                att = att + dot(probs[par, :, cc], v_m[hk, :], TN)
+                dq = dq + dot(dps[par, :, cc], k_m[hk, :], TN)
             att = att.astype(BF)
             dq = (dq * SCALE).astype(BF)
             for e in range(2):
@@ -287,10 +305,16 @@
                 x, y = b % NX, b // NX
                 aq[hp, x, y, 0] = att[e * BS:(e + 1) * BS]
                 aq[hp, x, y, 1] = dq[e * BS:(e + 1) * BS]
+
+        for p in range(NM // 2):
+            scores_grad(2 * p)
+            scores_grad(2 * p + 1)
+            if p > 0:
+                outputs(p - 1)
+        outputs(NM // 2 - 1)
         for cp in x1_copies(hp):
             cp.start()
         dk = (dot(dps[par], q_m[par]) * SCALE).reshape(2, 2 * BS, 2 * HD)
-        dv = dot(probs[par], og_m[par]).reshape(2, 2 * BS, 2 * HD)
         mine = core == 0
         c_keep[hp, 0] = jnp.where(mine, dk[0], dk[1])
         c_keep[hp, 1] = jnp.where(mine, dv[0], dv[1])

time: 59 us -> 59 us (level)
  no operation moved by 1% of the time
where the time goes in v7:
time: 59 us; the launch traced here: 58.6 us
  Pallas kernels  58 us (98%)
  between operations  0.64 us (1%)
    pallas_call x1, Pallas kernels, local(): pl.pallas_call(kernel, out_shape=out_shape, in_specs=[hbm] * 7, out_specs...  56.2 us
    pallas_call x1, Pallas kernels, local(): pl.pallas_call(write_out, out_shape=out_shape, in_specs=[vmem] * 4, out_s...  1.78 us

profile of v7, /device:TPU:2, one launch (start us, length us, event | category | flops | bytes accessed | tf_op | source)
XLA Modules:
  0.0 58.6 jit_solution(584402103404000877)
XLA Ops:
  0.6 56.2 %sparse_attention.1 = (bf16[1,128,512]{2,1,0:T(8,128)(2,1)}, f32[1,128,512]{2,1,0:T(8,128)}, f32[2,8,512]{2,1,0:T(8,128)}, f32[2,8,512]{2,1,0:T(8,128)}) custom-call(bf16[2048,512]{1,0:T(8,128)(2,1)} %queries.1, s32[1,2048]{1,0:T(1,128)} %order.1, bf16[2,128,512]{2,1,0:T(8,128)(2,1)} %keys.1, bf16[2,128,512]{2,1,0:T(8,128)(2,1)} %values.1, s32[1,16]{1,0:T(1,128)} %counts.1, ...), custom_call_target="tpu_custom_call" | custom-call | tf_op jit(solution)/shard_map/sparse_attention/pallas_call | solution.py:460
  56.8 1.8 %write_out.1 = (bf16[1,128,512]{2,1,0:T(8,128)(2,1)}, f32[1,128,512]{2,1,0:T(8,128)}, f32[2,8,512]{2,1,0:T(8,128)}, f32[2,8,512]{2,1,0:T(8,128)}) custom-call(bf16[1,128,512]{2,1,0:T(8,128)(2,1)} %get-tuple-element.8.refs_0_, f32[1,128,512]{2,1,0:T(8,128)} %get-tuple-element.9.refs_1_, f32[2,8,512]{2,1,0:T(8,128)} %get-tuple-element.10.refs_2_, ...), custom_call_target="tpu_custom_call" | custom-call | tf_op jit(solution)/shard_map/write_out/pallas_call | solution.py:509

commit v8 on v7

--- a/solution.py
+++ b/solution.py
@@ -415,26 +415,26 @@
         def _():
             first(s)
 
+        @pl.when((s >= 1) & (s < NC + 1))
+        def _():
+            second(s - 1)
+
         @pl.when((s >= 2) & (s < NC + 2))
         def _():
             relay_x(s - 2)
             relay_c(s - 2)
 
-        @pl.when((s >= 1) & (s < NC + 1))
-        def _():
-            second(s - 1)
-
-        @pl.when((s >= 2) & (s < NC + 2))
-        def _():
-            relay_y(s - 2)
-
-        @pl.when(s >= 3)
-        def _():
-            finish(s - 3)
+        @pl.when((s >= 3) & (s < NC + 3))
+        def _():
+            relay_y(s - 3)
+
+        @pl.when(s >= 4)
+        def _():
+            finish(s - 4)
 
         return 0
 
-    lax.fori_loop(0, NC + 3, turn, 0)
+    lax.fori_loop(0, NC + 4, turn, 0)
 
 
 def write_out(*refs):

time: 59 us -> 55.2 us (0.936)
  Pallas kernels: 58 us -> 54.4 us
    pallas_call x1, Pallas kernels: 56.2 us -> 52.7 us  [local(): pl.pallas_call(kernel, out_shape=out_shape, in_specs=[hbm] * 7, out_specs...]
where the time goes in v8:
time: 55.2 us; the launch traced here: 55.1 us
  Pallas kernels  54.4 us (99%)
  between operations  0.64 us (1%)
    pallas_call x1, Pallas kernels, local(): pl.pallas_call(kernel, out_shape=out_shape, in_specs=[hbm] * 7, out_specs...  52.7 us
    pallas_call x1, Pallas kernels, local(): pl.pallas_call(write_out, out_shape=out_shape, in_specs=[vmem] * 4, out_s...  1.78 us

profile of v8, /device:TPU:2, one launch (start us, length us, event | category | flops | bytes accessed | tf_op | source)
XLA Modules:
  0.0 55.1 jit_solution(4096810620017899454)
XLA Ops:
  0.6 52.7 %sparse_attention.1 = (bf16[1,128,512]{2,1,0:T(8,128)(2,1)}, f32[1,128,512]{2,1,0:T(8,128)}, f32[2,8,512]{2,1,0:T(8,128)}, f32[2,8,512]{2,1,0:T(8,128)}) custom-call(bf16[2048,512]{1,0:T(8,128)(2,1)} %queries.1, s32[1,2048]{1,0:T(1,128)} %order.1, bf16[2,128,512]{2,1,0:T(8,128)(2,1)} %keys.1, bf16[2,128,512]{2,1,0:T(8,128)(2,1)} %values.1, s32[1,16]{1,0:T(1,128)} %counts.1, ...), custom_call_target="tpu_custom_call" | custom-call | tf_op jit(solution)/shard_map/sparse_attention/pallas_call | solution.py:460
  53.3 1.8 %write_out.1 = (bf16[1,128,512]{2,1,0:T(8,128)(2,1)}, f32[1,128,512]{2,1,0:T(8,128)}, f32[2,8,512]{2,1,0:T(8,128)}, f32[2,8,512]{2,1,0:T(8,128)}) custom-call(bf16[1,128,512]{2,1,0:T(8,128)(2,1)} %get-tuple-element.8.refs_0_, f32[1,128,512]{2,1,0:T(8,128)} %get-tuple-element.9.refs_1_, f32[2,8,512]{2,1,0:T(8,128)} %get-tuple-element.10.refs_2_, ...), custom_call_target="tpu_custom_call" | custom-call | tf_op jit(solution)/shard_map/write_out/pallas_call | solution.py:509

commit v9 on v8

--- a/solution.py
+++ b/solution.py
@@ -52,6 +52,7 @@
     order_v,
     counts_v,
     listing_v,
+    pick,
     serial,
     og,
     kv,
@@ -63,9 +64,9 @@
     probs,
     dps,
     m_keep,
-    d_keep,
     stat_own,
     stat_got,
+    fin_got,
     aq,
     x1_got,
     x2_got,
@@ -80,6 +81,7 @@
     load_sem,
     kv_sem,
     stat_sem,
+    fin_sem,
     x1_sem,
     x2_sem,
     y_sem,
@@ -166,31 +168,35 @@
     spread = jnp.where(e0 == 2 * (e1 // BS) + core, 1.0, 0.0)
     use[...] = dot(joined.astype(BF), spread.astype(BF))
 
+    half = D // 2
+
+    def mark(b, _):
+        at = pl.multiple_of((2 * b + core) * BS, BS)
+        column = jnp.broadcast_to(order_v[:, pl.ds(at, BS)], (BS, BS)).T
+        lanes = lax.broadcasted_iota(jnp.int32, (BS, BS), 1)
+        rows = pl.ds(pl.multiple_of(b * BS, BS), BS)
+        for n in range(16):
+            pick[rows, n * BS:(n + 1) * BS] = jnp.where(column == lanes + n * BS, 1.0, 0.0).astype(BF)
+        return 0
+
+    lax.fori_loop(0, NM, mark, 0)
     load_q.wait()
+
+    def gather(c):
+        def part(t, _):
+            rows = pl.ds(pl.multiple_of(t * 4 * BS, 4 * BS), 4 * BS)
+            lanes = pl.ds(pl.multiple_of(c * half, half), half)
+            serial[rows, lanes] = dot(pick[rows, :], qbuf[:, lanes]).astype(BF)
+            return 0
+
+        lax.fori_loop(0, 2, part, 0)
 
     send_k = send(keys, kv.at[0, own2], kv_sem.at[0, 0], kv_sem.at[1, 0], mate)
     send_v = send(values, kv.at[1, own2], kv_sem.at[0, 1], kv_sem.at[1, 1], mate)
-
-    def gather(t, _):
-        @pl.when(t == 1)
-        def _():
-            pl.semaphore_wait(barrier, 1 + (NM - 1) + (NP - 1))
-            send_k.start()
-            send_v.start()
-
-        picks = []
-        for e in range(4):
-            at = pl.multiple_of((8 * t + 2 * e + core) * BS, BS)
-            column = jnp.broadcast_to(order_v[:, pl.ds(at, BS)], (BS, BS)).T
-            lanes = lax.broadcasted_iota(jnp.int32, (BS, BS), 1)
-            picks.append(jnp.concatenate(
-                [jnp.where(column == lanes + n * BS, 1.0, 0.0).astype(BF) for n in range(16)], axis=1
-            ))
-        pick = jnp.concatenate(picks, axis=0)
-        serial[pl.ds(pl.multiple_of(t * 4 * BS, 4 * BS), 4 * BS), :] = dot(pick, qbuf[...]).astype(BF)
-        return 0
-
-    lax.fori_loop(0, 2, gather, 0)
+    pl.semaphore_wait(barrier, 1 + (NM - 1) + (NP - 1))
+    send_k.start()
+    send_v.start()
+    gather(0)
     for cp in load_kv + load_og:
         cp.wait()
     send_k.wait()
@@ -244,8 +250,11 @@
             weighted = jnp.sum(weighted, axis=0, keepdims=True)
             r = slice(u, u + 1)
             m_keep[par, r, :] = m
-            stat_own[hp, 0, r, :] = m + jnp.log2(total)
-            stat_own[hp, 1, r, :] = weighted / total
+            lse = m + jnp.log2(total)
+            delta = weighted / total
+            for e in range(2):
+                stat_own[hp, 2 * p + e, h:h + 1, :] = lse[:, e * BS:(e + 1) * BS]
+                stat_own[hp, 2 * p + e, 2 + h:3 + h, :] = delta[:, e * BS:(e + 1) * BS]
 
         ahead = products(0)
         for u in range(NM):
@@ -255,72 +264,95 @@
             softmax(u, *now)
 
         def share(d, _):
-            send(stat_own.at[hp], stat_got.at[hp, d - 1], stat_sem.at[0, hp], stat_sem.at[1, hp], peer(d)).start()
+            send(
+                stat_own.at[hp, lax.rem(chip + d, NM)], stat_got.at[hp, d - 1],
+                stat_sem.at[0, hp], stat_sem.at[1, hp], peer(d),
+            ).start()
             return 0
 
         lax.fori_loop(1, NM, share, 0)
 
     def stat_all(hp):
         return send(stat_got.at[hp], stat_got.at[hp], stat_sem.at[0, hp], stat_sem.at[1, hp], right)
+
+    def fin_all(hp):
+        got = fin_got.at[hp, pl.ds(0, NM - 1)]
+        return send(got, got, fin_sem.at[0, hp], fin_sem.at[1, hp], right)
+
+    def combine(hp):
+        stat_all(hp).wait_recv()
+        own = stat_own[hp, chip]
+        parts = [own] + [stat_got[hp, d] for d in range(NM - 1)]
+        lse = [v[0:2] for v in parts]
+        top = functools.reduce(jnp.maximum, lse)
+        ws = [jnp.exp2(v - top) for v in lse]
+        total = functools.reduce(jnp.add, ws)
+        delta = functools.reduce(jnp.add, [w * v[2:4] for w, v in zip(ws, parts)]) / total
+        fin_got[hp, NM - 1, 0:2] = top + jnp.log2(total)
+        fin_got[hp, NM - 1, 2:4] = delta
+
+        def share(d, _):
+            send(
+                fin_got.at[hp, NM - 1], fin_got.at[hp, d - 1],
+                fin_sem.at[0, hp], fin_sem.at[1, hp], peer(d),
+            ).start()
+            return 0
+
+        lax.fori_loop(1, NM, share, 0)
+
+    def fin_row(hp, p, row):
+        return jnp.concatenate(
+            [fin_got[hp, lax.rem(chip - (2 * p + e) + 2 * NM - 1, NM), row:row + 1, :] for e in range(2)], axis=1
+        )
 
     def second(hp):
         par = lax.rem(hp, 2)
         cols = lanes_of(hp)
-        stat_all(hp).wait_recv()
-        lse = [stat_own[hp, 0]] + [stat_got[hp, d, 0] for d in range(NM - 1)]
-        dlt = [stat_own[hp, 1]] + [stat_got[hp, d, 1] for d in range(NM - 1)]
-        top = functools.reduce(jnp.maximum, lse)
-        ws = [jnp.exp2(v - top) for v in lse]
-        total = functools.reduce(jnp.add, ws)
-        delta_all = functools.reduce(jnp.add, [w * v for w, v in zip(ws, dlt)]) / total
-        m_keep[par] = jnp.exp2(m_keep[par] - (top + jnp.log2(total)))
-        d_keep[...] = delta_all
+        fin_all(hp).wait_recv()
         split_heads(kv[0, :, :, cols].reshape(KS, 2 * HD), k_m, KS)
         split_heads(kv[1, :, :, cols].reshape(KS, 2 * HD), v_m, KS)
 
         for u in range(NM):
-            probs[par, :, columns(u)] = (
-                probs[par, :, columns(u)].astype(F32) * m_keep[par, u:u + 1, :]
-            ).astype(BF)
-        dv = dot(probs[par], og_m[par]).reshape(2, 2 * BS, 2 * HD)
-
-        def scores_grad(u):
-            cc = columns(u)
-            dps[par, :, cc] = (
-                probs[par, :, cc].astype(F32) * (dps[par, :, cc].astype(F32) - d_keep[u:u + 1, :])
-            ).astype(BF)
-
-        def outputs(p):
+            w = jnp.exp2(m_keep[par, u:u + 1, :] - fin_row(hp, u // 2, u % 2))
+            probs[par, :, columns(u)] = (probs[par, :, columns(u)].astype(F32) * w).astype(BF)
+        hand_over(hp, 1, dot(probs[par], og_m[par]))
+
+        @pl.when(hp >= 1)
+        def _():
+            relay_x(hp - 1)
+
+        def query_side(p, x0, y):
             att = jnp.zeros((PQ, 2 * HD), F32)
             dq = jnp.zeros((PQ, 2 * HD), F32)
             for h in range(2):
-                cc = columns(2 * p + h)
+                cc = pl.ds(pl.multiple_of(h * QS + p * PQ, PQ), PQ)
                 hk = slice(h * KS, (h + 1) * KS)
-                att = att + dot(probs[par, :, cc], v_m[hk, :], TN)
-                dq = dq + dot(dps[par, :, cc], k_m[hk, :], TN)
+                qb = probs[par, :, cc]
+                ds = (qb.astype(F32) * (dps[par, :, cc].astype(F32) - fin_row(hp, p, 2 + h))).astype(BF)
+                dps[par, :, cc] = ds
+                att = att + dot(qb, v_m[hk, :], TN)
+                dq = dq + dot(ds, k_m[hk, :], TN)
             att = att.astype(BF)
             dq = (dq * SCALE).astype(BF)
             for e in range(2):
-                b = 2 * p + e
-                x, y = b % NX, b // NX
-                aq[hp, x, y, 0] = att[e * BS:(e + 1) * BS]
-                aq[hp, x, y, 1] = dq[e * BS:(e + 1) * BS]
-
-        for p in range(NM // 2):
-            scores_grad(2 * p)
-            scores_grad(2 * p + 1)
-            if p > 0:
-                outputs(p - 1)
-        outputs(NM // 2 - 1)
+                aq[hp, x0 + e, y, 0] = att[e * BS:(e + 1) * BS]
+                aq[hp, x0 + e, y, 1] = dq[e * BS:(e + 1) * BS]
+
+        far = 1 - xi // 2
+        for y in range(NY):
+            query_side(2 * y + far, 2 * far, y)
         for cp in x1_copies(hp):
             cp.start()
-        dk = (dot(dps[par], q_m[par]) * SCALE).reshape(2, 2 * BS, 2 * HD)
+        for y in range(NY):
+            query_side(2 * y + 1 - far, 2 * (1 - far), y)
+        hand_over(hp, 0, dot(dps[par], q_m[par]) * SCALE)
+
+    def hand_over(hp, kind, grad):
+        grad = grad.reshape(2, 2 * BS, 2 * HD)
         mine = core == 0
-        c_keep[hp, 0] = jnp.where(mine, dk[0], dk[1])
-        c_keep[hp, 1] = jnp.where(mine, dv[0], dv[1])
-        c_send[hp, 0] = jnp.where(mine, dk[1], dk[0]).astype(BF)
-        c_send[hp, 1] = jnp.where(mine, dv[1], dv[0]).astype(BF)
-        c_copy(hp).start()
+        c_keep[hp, kind] = jnp.where(mine, grad[0], grad[1])
+        c_send[hp, kind] = jnp.where(mine, grad[1], grad[0]).astype(BF)
+        c_copy(hp, kind).start()
 
     def x1_copies(hp):
         return (
@@ -337,11 +369,11 @@
     def y_copy(hp):
         return send(y_send.at[hp], y_got.at[hp], y_sem.at[0, hp], y_sem.at[1, hp], across)
 
-    def c_copy(hp):
-        return send(c_send.at[hp], c_got.at[hp], c_sem.at[0, hp], c_sem.at[1, hp], mate)
-
-    def z_all(pair):
-        return send(z_got.at[pair], z_got.at[pair], z_sem.at[0, pair], z_sem.at[1, pair], slab(1))
+    def c_copy(hp, kind):
+        return send(c_send.at[hp, kind], c_got.at[hp, kind], c_sem.at[0, hp, kind], c_sem.at[1, hp, kind], mate)
+
+    def z_all(hp):
+        return send(z_got.at[hp], z_got.at[hp], z_sem.at[0, hp], z_sem.at[1, hp], slab(1))
 
     def relay_x(hp):
         for cp in x1_copies(hp):
@@ -352,23 +384,20 @@
             cp.start()
 
     def relay_c(hp):
-        c_copy(hp).wait_recv()
-        pair = hp // 2
         for a in range(2):
+            c_copy(hp, a).wait_recv()
             total = c_keep[hp, a] + c_got[hp, a].astype(F32)
             total = total.reshape(2, NP, 8, 2 * HD).transpose(1, 0, 2, 3)
-            z_send[pair, :, 2 * lax.rem(hp, 2) + a] = total.reshape(NP, 16, 2 * HD).astype(BF)
+            z_send[hp, :, a] = total.reshape(NP, 16, 2 * HD).astype(BF)
 
         def share(d, _):
             send(
-                z_send.at[pair, lax.rem(pb + d, NP)], z_got.at[pair, d - 1],
-                z_sem.at[0, pair], z_sem.at[1, pair], slab(d),
+                z_send.at[hp, lax.rem(pb + d, NP)], z_got.at[hp, d - 1],
+                z_sem.at[0, hp], z_sem.at[1, hp], slab(d),
             ).start()
             return 0
 
-        @pl.when(lax.rem(hp, 2) == 1)
-        def _():
-            lax.fori_loop(1, NP, share, 0)
+        lax.fori_loop(1, NP, share, 0)
 
     def relay_y(hp):
         for cp in x2_copies(hp):
@@ -391,42 +420,49 @@
         both = y_keep[hp] + y_got[hp].astype(F32)
         att_out[0, :, cols] = both[0].astype(BF)
         qg_out[0, :, cols] = both[1]
+        z_all(hp).wait_recv()
+        for a, out in ((0, kg_out), (1, vg_out)):
+            total = z_send[hp, pb, a].astype(F32)
+            for d in range(NP - 1):
+                total = total + z_got[hp, d, a].astype(F32)
+            out[:, :, cols] = total.reshape(2, 8, 2 * HD)
         stat_all(hp).wait_send()
+        fin_all(hp).wait_send()
         for cp in x1_copies(hp) + x2_copies(hp):
             cp.wait_send()
         y_copy(hp).wait_send()
-        c_copy(hp).wait_send()
-
-        @pl.when(lax.rem(hp, 2) == 1)
-        def _():
-            pair = hp // 2
-            z_all(pair).wait_recv()
-            for q in range(2):
-                cols = lanes_of(2 * pair + q)
-                for a, out in ((0, kg_out), (1, vg_out)):
-                    total = z_send[pair, pb, 2 * q + a].astype(F32)
-                    for d in range(NP - 1):
-                        total = total + z_got[pair, d, 2 * q + a].astype(F32)
-                    out[:, :, cols] = total.reshape(2, 8, 2 * HD)
-            z_all(pair).wait_send()
+        for kind in range(2):
+            c_copy(hp, kind).wait_send()
+        z_all(hp).wait_send()
 
     def turn(s, _):
         @pl.when(s < NC)
         def _():
             first(s)
 
-        @pl.when((s >= 1) & (s < NC + 1))
+        @pl.when(s == 0)
+        def _():
+            gather(1)
+
+        @pl.when((s >= 3) & (s < NC + 3))
+        def _():
+            relay_y(s - 3)
+
+        @pl.when((s >= 1) & (s <= NC))
         def _():
             second(s - 1)
 
+        @pl.when(s == NC + 1)
+        def _():
+            relay_x(NC - 1)
+
         @pl.when((s >= 2) & (s < NC + 2))
         def _():
-            relay_x(s - 2)
             relay_c(s - 2)
 
-        @pl.when((s >= 3) & (s < NC + 3))
-        def _():
-            relay_y(s - 3)
+        @pl.when(s < NC)
+        def _():
+            combine(s)
 
         @pl.when(s >= 4)
         def _():
@@ -467,6 +503,7 @@
             pltpu.VMEM((1, NP * BS), jnp.int32),
             pltpu.VMEM((1, NP), jnp.int32),
             pltpu.VMEM((1, 256), jnp.int32),
+            pltpu.VMEM((QS, NP * BS), BF),
             pltpu.VMEM((QS, D), BF),
             pltpu.VMEM((NM, BS, D), BF),
             pltpu.VMEM((2, 4, BS, D), BF),
@@ -478,9 +515,9 @@
             pltpu.VMEM((2, KS, 2 * QS), BF),
             pltpu.VMEM((2, KS, 2 * QS), BF),
             pltpu.VMEM((2, 8, PQ), F32),
-            pltpu.VMEM((8, PQ), F32),
-            pltpu.VMEM((NC, 2, 8, PQ), F32),
-            pltpu.VMEM((NC, NM - 1, 2, 8, PQ), F32),
+            pltpu.VMEM((NC, NM, 4, BS), F32),
+            pltpu.VMEM((NC, NM - 1, 4, BS), F32),
+            pltpu.VMEM((NC, NM, 4, BS), F32),
             pltpu.VMEM((NC, NX, NY, 2, BS, w2), BF),
             pltpu.VMEM((NC, 2, 2, BS, w2), BF),
             pltpu.VMEM((NC, 2, NY, 2, BS, w2), BF),
@@ -490,16 +527,17 @@
             pltpu.VMEM((NC, 2, 2 * BS, w2), F32),
             pltpu.VMEM((NC, 2, 2 * BS, w2), BF),
             pltpu.VMEM((NC, 2, 2 * BS, w2), BF),
-            pltpu.VMEM((NC // 2, NP, 4, 16, w2), BF),
-            pltpu.VMEM((NC // 2, NP - 1, 4, 16, w2), BF),
+            pltpu.VMEM((NC, NP, 2, 16, w2), BF),
+            pltpu.VMEM((NC, NP - 1, 2, 16, w2), BF),
             dma((6 + NM,)),
             dma((2, 2)),
+            dma((2, NC)),
             dma((2, NC)),
             dma((2, NC, 2)),
             dma((2, NC, 2)),
             dma((2, NC)),
+            dma((2, NC, 2)),
             dma((2, NC)),
-            dma((2, NC // 2)),
         ],
         compiler_params=pltpu.CompilerParams(
             collective_id=0, has_side_effects=True, vmem_limit_bytes=60 * 1024 * 1024

time: 55.2 us -> 70.2 us (1.27)
  Pallas kernels: 54.4 us -> 68.7 us
    pallas_call x1, Pallas kernels: 52.7 us -> 67 us  [local(): pl.pallas_call(kernel, out_shape=out_shape, in_specs=[hbm] * 7, out_specs...]
where the time goes in v9:
time: 70.2 us; the launch traced here: 69.4 us
  Pallas kernels  68.7 us (98%)
    pallas_call x1, Pallas kernels, local(): pl.pallas_call(kernel, out_shape=out_shape, in_specs=[hbm] * 7, out_specs...  67 us
    pallas_call x1, Pallas kernels, local(): pl.pallas_call(write_out, out_shape=out_shape, in_specs=[vmem] * 4, out_s...  1.78 us

profile of v9, /device:TPU:2, one launch (start us, length us, event | category | flops | bytes accessed | tf_op | source)
XLA Modules:
  0.0 69.4 jit_solution(16378063781293139763)
XLA Ops:
  0.6 67.0 %sparse_attention.1 = (bf16[1,128,512]{2,1,0:T(8,128)(2,1)}, f32[1,128,512]{2,1,0:T(8,128)}, f32[2,8,512]{2,1,0:T(8,128)}, f32[2,8,512]{2,1,0:T(8,128)}) custom-call(bf16[2048,512]{1,0:T(8,128)(2,1)} %queries.1, s32[1,2048]{1,0:T(1,128)} %order.1, bf16[2,128,512]{2,1,0:T(8,128)(2,1)} %keys.1, bf16[2,128,512]{2,1,0:T(8,128)(2,1)} %values.1, s32[1,16]{1,0:T(1,128)} %counts.1, ...), custom_call_target="tpu_custom_call" | custom-call | tf_op jit(solution)/shard_map/sparse_attention/pallas_call | solution.py:496
  67.6 1.8 %write_out.1 = (bf16[1,128,512]{2,1,0:T(8,128)(2,1)}, f32[1,128,512]{2,1,0:T(8,128)}, f32[2,8,512]{2,1,0:T(8,128)}, f32[2,8,512]{2,1,0:T(8,128)}) custom-call(bf16[1,128,512]{2,1,0:T(8,128)(2,1)} %get-tuple-element.8.refs_0_, f32[1,128,512]{2,1,0:T(8,128)} %get-tuple-element.9.refs_1_, f32[2,8,512]{2,1,0:T(8,128)} %get-tuple-element.10.refs_2_, ...), custom_call_target="tpu_custom_call" | custom-call | tf_op jit(solution)/shard_map/write_out/pallas_call | solution.py:547

commit v10 on v8

--- a/solution.py
+++ b/solution.py
@@ -282,39 +282,39 @@
             probs[par, :, columns(u)] = (
                 probs[par, :, columns(u)].astype(F32) * m_keep[par, u:u + 1, :]
             ).astype(BF)
-        dv = dot(probs[par], og_m[par]).reshape(2, 2 * BS, 2 * HD)
-
-        def scores_grad(u):
-            cc = columns(u)
-            dps[par, :, cc] = (
-                probs[par, :, cc].astype(F32) * (dps[par, :, cc].astype(F32) - d_keep[u:u + 1, :])
-            ).astype(BF)
-
-        def outputs(p):
+
+        @pl.when(hp >= 1)
+        def _():
+            relay_x(hp - 1)
+
+        def query_side(p, x0, y):
             att = jnp.zeros((PQ, 2 * HD), F32)
             dq = jnp.zeros((PQ, 2 * HD), F32)
             for h in range(2):
-                cc = columns(2 * p + h)
+                cc = pl.ds(pl.multiple_of(h * QS + p * PQ, PQ), PQ)
                 hk = slice(h * KS, (h + 1) * KS)
-                att = att + dot(probs[par, :, cc], v_m[hk, :], TN)
-                dq = dq + dot(dps[par, :, cc], k_m[hk, :], TN)
+                qb = probs[par, :, cc]
+                ds = (
+                    qb.astype(F32) * (dps[par, :, cc].astype(F32) - d_keep[pl.ds(2 * p + h, 1), :])
+                ).astype(BF)
+                dps[par, :, cc] = ds
+                att = att + dot(qb, v_m[hk, :], TN)
+                dq = dq + dot(ds, k_m[hk, :], TN)
             att = att.astype(BF)
             dq = (dq * SCALE).astype(BF)
             for e in range(2):
-                b = 2 * p + e
-                x, y = b % NX, b // NX
-                aq[hp, x, y, 0] = att[e * BS:(e + 1) * BS]
-                aq[hp, x, y, 1] = dq[e * BS:(e + 1) * BS]
-
-        for p in range(NM // 2):
-            scores_grad(2 * p)
-            scores_grad(2 * p + 1)
-            if p > 0:
-                outputs(p - 1)
-        outputs(NM // 2 - 1)
+                aq[hp, x0 + e, y, 0] = att[e * BS:(e + 1) * BS]
+                aq[hp, x0 + e, y, 1] = dq[e * BS:(e + 1) * BS]
+
+        far = 1 - xi // 2
+        for y in range(NY):
+            query_side(2 * y + far, 2 * far, y)
         for cp in x1_copies(hp):
             cp.start()
+        for y in range(NY):
+            query_side(2 * y + 1 - far, 2 * (1 - far), y)
         dk = (dot(dps[par], q_m[par]) * SCALE).reshape(2, 2 * BS, 2 * HD)
+        dv = dot(probs[par], og_m[par]).reshape(2, 2 * BS, 2 * HD)
         mine = core == 0
         c_keep[hp, 0] = jnp.where(mine, dk[0], dk[1])
         c_keep[hp, 1] = jnp.where(mine, dv[0], dv[1])
@@ -415,18 +415,21 @@
         def _():
             first(s)
 
-        @pl.when((s >= 1) & (s < NC + 1))
+        @pl.when((s >= 3) & (s < NC + 3))
+        def _():
+            relay_y(s - 3)
+
+        @pl.when((s >= 1) & (s <= NC))
         def _():
             second(s - 1)
 
+        @pl.when(s == NC + 1)
+        def _():
+            relay_x(NC - 1)
+
         @pl.when((s >= 2) & (s < NC + 2))
         def _():
-            relay_x(s - 2)
             relay_c(s - 2)
-
-        @pl.when((s >= 3) & (s < NC + 3))
-        def _():
-            relay_y(s - 3)
 
         @pl.when(s >= 4)
         def _():

time: 55.2 us -> 58 us (1.051)
  Pallas kernels: 54.4 us -> 57.2 us
    pallas_call x1, Pallas kernels: 52.7 us -> 55.4 us  [local(): pl.pallas_call(kernel, out_shape=out_shape, in_specs=[hbm] * 7, out_specs...]
where the time goes in v10:
time: 58 us; the launch traced here: 57.8 us
  Pallas kernels  57.2 us (99%)
  between operations  0.64 us (1%)
    pallas_call x1, Pallas kernels, local(): pl.pallas_call(kernel, out_shape=out_shape, in_specs=[hbm] * 7, out_specs...  55.4 us
    pallas_call x1, Pallas kernels, local(): pl.pallas_call(write_out, out_shape=out_shape, in_specs=[vmem] * 4, out_s...  1.78 us

profile of v10, /device:TPU:2, one launch (start us, length us, event | category | flops | bytes accessed | tf_op | source)
XLA Modules:
  0.0 57.8 jit_solution(4720224170883467745)
XLA Ops:
  0.6 55.4 %sparse_attention.1 = (bf16[1,128,512]{2,1,0:T(8,128)(2,1)}, f32[1,128,512]{2,1,0:T(8,128)}, f32[2,8,512]{2,1,0:T(8,128)}, f32[2,8,512]{2,1,0:T(8,128)}) custom-call(bf16[2048,512]{1,0:T(8,128)(2,1)} %queries.1, s32[1,2048]{1,0:T(1,128)} %order.1, bf16[2,128,512]{2,1,0:T(8,128)(2,1)} %keys.1, bf16[2,128,512]{2,1,0:T(8,128)(2,1)} %values.1, s32[1,16]{1,0:T(1,128)} %counts.1, ...), custom_call_target="tpu_custom_call" | custom-call | tf_op jit(solution)/shard_map/sparse_attention/pallas_call | solution.py:463
  56.0 1.8 %write_out.1 = (bf16[1,128,512]{2,1,0:T(8,128)(2,1)}, f32[1,128,512]{2,1,0:T(8,128)}, f32[2,8,512]{2,1,0:T(8,128)}, f32[2,8,512]{2,1,0:T(8,128)}) custom-call(bf16[1,128,512]{2,1,0:T(8,128)(2,1)} %get-tuple-element.8.refs_0_, f32[1,128,512]{2,1,0:T(8,128)} %get-tuple-element.9.refs_1_, f32[2,8,512]{2,1,0:T(8,128)} %get-tuple-element.10.refs_2_, ...), custom_call_target="tpu_custom_call" | custom-call | tf_op jit(solution)/shard_map/write_out/pallas_call | solution.py:512

commit v11 on v8

--- a/solution.py
+++ b/solution.py
@@ -205,9 +205,8 @@
         dst[:n] = jnp.where(low, src, none)
         dst[n:] = jnp.where(low, none, src)
 
-    def columns(u):
-        p, h = u // 2, u % 2
-        return slice(h * QS + p * PQ, h * QS + (p + 1) * PQ)
+    def columns(p, h):
+        return pl.ds(pl.multiple_of(h * QS + p * PQ, PQ), PQ)
 
     def first(hp):
         par = lax.rem(hp, 2)
@@ -217,14 +216,11 @@
         split_heads(serial[:, cols], q_m.at[par], QS)
         split_heads(og[:, :, cols].reshape(QS, 2 * HD), og_m.at[par], QS)
 
-        def products(u):
-            cc = columns(u)
-            return dot(k2, q_m[par, cc, :], NT), dot(v2, og_m[par, cc, :], NT)
-
-        def softmax(u, st, dp):
-            p, h = u // 2, u % 2
-            cc = columns(u)
-            usable = use[0:4, p * PQ:(p + 1) * PQ] > 0.5
+        def softmax(p, h):
+            cc = columns(p, h)
+            st = dot(k2, q_m[par, cc, :], NT)
+            dp = dot(v2, og_m[par, cc, :], NT)
+            usable = use[0:4, columns(p, 0)] > 0.5
             m_raw = jnp.full((1, PQ), -FAR, F32)
             for kb in range(4):
                 top = jnp.max(st[kb * BS:(kb + 1) * BS], axis=0, keepdims=True)
@@ -242,17 +238,18 @@
             dps[par, :, cc] = dp.astype(BF)
             total = jnp.maximum(jnp.sum(total, axis=0, keepdims=True), 0.5)
             weighted = jnp.sum(weighted, axis=0, keepdims=True)
-            r = slice(u, u + 1)
+            r = pl.ds(2 * p + h, 1)
             m_keep[par, r, :] = m
             stat_own[hp, 0, r, :] = m + jnp.log2(total)
             stat_own[hp, 1, r, :] = weighted / total
 
-        ahead = products(0)
-        for u in range(NM):
-            now = ahead
-            if u + 1 < NM:
-                ahead = products(u + 1)
-            softmax(u, *now)
+        def steps(y, _):
+            for i in range(2):
+                for h in range(2):
+                    softmax(2 * y + i, h)
+            return 0
+
+        lax.fori_loop(0, NY, steps, 0)
 
         def share(d, _):
             send(stat_own.at[hp], stat_got.at[hp, d - 1], stat_sem.at[0, hp], stat_sem.at[1, hp], peer(d)).start()
@@ -278,43 +275,34 @@
         split_heads(kv[0, :, :, cols].reshape(KS, 2 * HD), k_m, KS)
         split_heads(kv[1, :, :, cols].reshape(KS, 2 * HD), v_m, KS)
 
-        for u in range(NM):
-            probs[par, :, columns(u)] = (
-                probs[par, :, columns(u)].astype(F32) * m_keep[par, u:u + 1, :]
-            ).astype(BF)
-        dv = dot(probs[par], og_m[par]).reshape(2, 2 * BS, 2 * HD)
-
-        def scores_grad(u):
-            cc = columns(u)
-            dps[par, :, cc] = (
-                probs[par, :, cc].astype(F32) * (dps[par, :, cc].astype(F32) - d_keep[u:u + 1, :])
-            ).astype(BF)
-
-        def outputs(p):
-            att = jnp.zeros((PQ, 2 * HD), F32)
-            dq = jnp.zeros((PQ, 2 * HD), F32)
-            for h in range(2):
-                cc = columns(2 * p + h)
-                hk = slice(h * KS, (h + 1) * KS)
-                att = att + dot(probs[par, :, cc], v_m[hk, :], TN)
-                dq = dq + dot(dps[par, :, cc], k_m[hk, :], TN)
-            att = att.astype(BF)
-            dq = (dq * SCALE).astype(BF)
-            for e in range(2):
-                b = 2 * p + e
-                x, y = b % NX, b // NX
-                aq[hp, x, y, 0] = att[e * BS:(e + 1) * BS]
-                aq[hp, x, y, 1] = dq[e * BS:(e + 1) * BS]
-
-        for p in range(NM // 2):
-            scores_grad(2 * p)
-            scores_grad(2 * p + 1)
-            if p > 0:
-                outputs(p - 1)
-        outputs(NM // 2 - 1)
+        def steps(y, _):
+            for i in range(2):
+                p = 2 * y + i
+                att = jnp.zeros((PQ, 2 * HD), F32)
+                dq = jnp.zeros((PQ, 2 * HD), F32)
+                for h in range(2):
+                    cc = columns(p, h)
+                    hk = slice(h * KS, (h + 1) * KS)
+                    r = pl.ds(2 * p + h, 1)
+                    qf = probs[par, :, cc].astype(F32) * m_keep[par, r, :]
+                    qb = qf.astype(BF)
+                    ds = (qf * (dps[par, :, cc].astype(F32) - d_keep[r, :])).astype(BF)
+                    probs[par, :, cc] = qb
+                    dps[par, :, cc] = ds
+                    att = att + dot(qb, v_m[hk, :], TN)
+                    dq = dq + dot(ds, k_m[hk, :], TN)
+                att = att.astype(BF)
+                dq = (dq * SCALE).astype(BF)
+                for e in range(2):
+                    aq[hp, 2 * i + e, y, 0] = att[e * BS:(e + 1) * BS]
+                    aq[hp, 2 * i + e, y, 1] = dq[e * BS:(e + 1) * BS]
+            return 0
+
+        lax.fori_loop(0, NY, steps, 0)
         for cp in x1_copies(hp):
             cp.start()
         dk = (dot(dps[par], q_m[par]) * SCALE).reshape(2, 2 * BS, 2 * HD)
+        dv = dot(probs[par], og_m[par]).reshape(2, 2 * BS, 2 * HD)
         mine = core == 0
         c_keep[hp, 0] = jnp.where(mine, dk[0], dk[1])
         c_keep[hp, 1] = jnp.where(mine, dv[0], dv[1])

time: 55.2 us -> 59 us (1.069)
  the two profiles are of different devices: /device:TPU:2 before, /device:TPU:1 now
where the time goes in v11:
time: 59 us; the launch traced here: 58.8 us
  Pallas kernels  58.2 us (99%)
  between operations  0.64 us (1%)
    pallas_call x1, Pallas kernels, local(): pl.pallas_call(kernel, out_shape=out_shape, in_specs=[hbm] * 7, out_specs...  56.4 us
    pallas_call x1, Pallas kernels, local(): pl.pallas_call(write_out, out_shape=out_shape, in_specs=[vmem] * 4, out_s...  1.78 us

profile of v11, /device:TPU:1, one launch (start us, length us, event | category | flops | bytes accessed | tf_op | source)
XLA Modules:
  0.0 58.8 jit_solution(14996341407406440951)
XLA Ops:
  0.6 56.4 %sparse_attention.1 = (bf16[1,128,512]{2,1,0:T(8,128)(2,1)}, f32[1,128,512]{2,1,0:T(8,128)}, f32[2,8,512]{2,1,0:T(8,128)}, f32[2,8,512]{2,1,0:T(8,128)}) custom-call(bf16[2048,512]{1,0:T(8,128)(2,1)} %queries.1, s32[1,2048]{1,0:T(1,128)} %order.1, bf16[2,128,512]{2,1,0:T(8,128)(2,1)} %keys.1, bf16[2,128,512]{2,1,0:T(8,128)(2,1)} %values.1, s32[1,16]{1,0:T(1,128)} %counts.1, ...), custom_call_target="tpu_custom_call" | custom-call | tf_op jit(solution)/shard_map/sparse_attention/pallas_call | solution.py:448
  57.0 1.8 %write_out.1 = (bf16[1,128,512]{2,1,0:T(8,128)(2,1)}, f32[1,128,512]{2,1,0:T(8,128)}, f32[2,8,512]{2,1,0:T(8,128)}, f32[2,8,512]{2,1,0:T(8,128)}) custom-call(bf16[1,128,512]{2,1,0:T(8,128)(2,1)} %get-tuple-element.8.refs_0_, f32[1,128,512]{2,1,0:T(8,128)} %get-tuple-element.9.refs_1_, f32[2,8,512]{2,1,0:T(8,128)} %get-tuple-element.10.refs_2_, ...), custom_call_target="tpu_custom_call" | custom-call | tf_op jit(solution)/shard_map/write_out/pallas_call | solution.py:497

commit v12 on v8

--- a/solution.py
+++ b/solution.py
@@ -62,7 +62,10 @@
     v_m,
     probs,
     dps,
+    qs,
+    dss,
     m_keep,
+    w_all,
     d_keep,
     stat_own,
     stat_got,
@@ -273,31 +276,25 @@
         ws = [jnp.exp2(v - top) for v in lse]
         total = functools.reduce(jnp.add, ws)
         delta_all = functools.reduce(jnp.add, [w * v for w, v in zip(ws, dlt)]) / total
-        m_keep[par] = jnp.exp2(m_keep[par] - (top + jnp.log2(total)))
+        w_all[...] = jnp.exp2(m_keep[par] - (top + jnp.log2(total)))
         d_keep[...] = delta_all
         split_heads(kv[0, :, :, cols].reshape(KS, 2 * HD), k_m, KS)
         split_heads(kv[1, :, :, cols].reshape(KS, 2 * HD), v_m, KS)
 
-        for u in range(NM):
-            probs[par, :, columns(u)] = (
-                probs[par, :, columns(u)].astype(F32) * m_keep[par, u:u + 1, :]
-            ).astype(BF)
-        dv = dot(probs[par], og_m[par]).reshape(2, 2 * BS, 2 * HD)
-
-        def scores_grad(u):
-            cc = columns(u)
-            dps[par, :, cc] = (
-                probs[par, :, cc].astype(F32) * (dps[par, :, cc].astype(F32) - d_keep[u:u + 1, :])
-            ).astype(BF)
-
-        def outputs(p):
+        for p in range(NM // 2):
             att = jnp.zeros((PQ, 2 * HD), F32)
             dq = jnp.zeros((PQ, 2 * HD), F32)
             for h in range(2):
-                cc = columns(2 * p + h)
+                u = 2 * p + h
+                cc = columns(u)
                 hk = slice(h * KS, (h + 1) * KS)
-                att = att + dot(probs[par, :, cc], v_m[hk, :], TN)
-                dq = dq + dot(dps[par, :, cc], k_m[hk, :], TN)
+                qf = probs[par, :, cc].astype(F32) * w_all[u:u + 1, :]
+                qb = qf.astype(BF)
+                ds = (qf * (dps[par, :, cc].astype(F32) - d_keep[u:u + 1, :])).astype(BF)
+                qs[:, cc] = qb
+                dss[:, cc] = ds
+                att = att + dot(qb, v_m[hk, :], TN)
+                dq = dq + dot(ds, k_m[hk, :], TN)
             att = att.astype(BF)
             dq = (dq * SCALE).astype(BF)
             for e in range(2):
@@ -305,16 +302,10 @@
                 x, y = b % NX, b // NX
                 aq[hp, x, y, 0] = att[e * BS:(e + 1) * BS]
                 aq[hp, x, y, 1] = dq[e * BS:(e + 1) * BS]
-
-        for p in range(NM // 2):
-            scores_grad(2 * p)
-            scores_grad(2 * p + 1)
-            if p > 0:
-                outputs(p - 1)
-        outputs(NM // 2 - 1)
         for cp in x1_copies(hp):
             cp.start()
-        dk = (dot(dps[par], q_m[par]) * SCALE).reshape(2, 2 * BS, 2 * HD)
+        dk = (dot(dss[...], q_m[par]) * SCALE).reshape(2, 2 * BS, 2 * HD)
+        dv = dot(qs[...], og_m[par]).reshape(2, 2 * BS, 2 * HD)
         mine = core == 0
         c_keep[hp, 0] = jnp.where(mine, dk[0], dk[1])
         c_keep[hp, 1] = jnp.where(mine, dv[0], dv[1])
@@ -340,8 +331,8 @@
     def c_copy(hp):
         return send(c_send.at[hp], c_got.at[hp], c_sem.at[0, hp], c_sem.at[1, hp], mate)
 
-    def z_all(pair):
-        return send(z_got.at[pair], z_got.at[pair], z_sem.at[0, pair], z_sem.at[1, pair], slab(1))
+    def z_all(hp):
+        return send(z_got.at[hp], z_got.at[hp], z_sem.at[0, hp], z_sem.at[1, hp], slab(1))
 
     def relay_x(hp):
         for cp in x1_copies(hp):
@@ -353,22 +344,19 @@
 
     def relay_c(hp):
         c_copy(hp).wait_recv()
-        pair = hp // 2
         for a in range(2):
             total = c_keep[hp, a] + c_got[hp, a].astype(F32)
             total = total.reshape(2, NP, 8, 2 * HD).transpose(1, 0, 2, 3)
-            z_send[pair, :, 2 * lax.rem(hp, 2) + a] = total.reshape(NP, 16, 2 * HD).astype(BF)
+            z_send[hp, :, a] = total.reshape(NP, 16, 2 * HD).astype(BF)
 
         def share(d, _):
             send(
-                z_send.at[pair, lax.rem(pb + d, NP)], z_got.at[pair, d - 1],
-                z_sem.at[0, pair], z_sem.at[1, pair], slab(d),
+                z_send.at[hp, lax.rem(pb + d, NP)], z_got.at[hp, d - 1],
+                z_sem.at[0, hp], z_sem.at[1, hp], slab(d),
             ).start()
             return 0
 
-        @pl.when(lax.rem(hp, 2) == 1)
-        def _():
-            lax.fori_loop(1, NP, share, 0)
+        lax.fori_loop(1, NP, share, 0)
 
     def relay_y(hp):
         for cp in x2_copies(hp):
@@ -387,6 +375,12 @@
 
     def finish(hp):
         cols = lanes_of(hp)
+        z_all(hp).wait_recv()
+        for a, out in ((0, kg_out), (1, vg_out)):
+            total = z_send[hp, pb, a].astype(F32)
+            for d in range(NP - 1):
+                total = total + z_got[hp, d, a].astype(F32)
+            out[:, :, cols] = total.reshape(2, 8, 2 * HD)
         y_copy(hp).wait_recv()
         both = y_keep[hp] + y_got[hp].astype(F32)
         att_out[0, :, cols] = both[0].astype(BF)
@@ -396,19 +390,7 @@
             cp.wait_send()
         y_copy(hp).wait_send()
         c_copy(hp).wait_send()
-
-        @pl.when(lax.rem(hp, 2) == 1)
-        def _():
-            pair = hp // 2
-            z_all(pair).wait_recv()
-            for q in range(2):
-                cols = lanes_of(2 * pair + q)
-                for a, out in ((0, kg_out), (1, vg_out)):
-                    total = z_send[pair, pb, 2 * q + a].astype(F32)
-                    for d in range(NP - 1):
-                        total = total + z_got[pair, d, 2 * q + a].astype(F32)
-                    out[:, :, cols] = total.reshape(2, 8, 2 * HD)
-            z_all(pair).wait_send()
+        z_all(hp).wait_send()
 
     def turn(s, _):
         @pl.when(s < NC)
@@ -477,7 +459,10 @@
             pltpu.VMEM((2 * KS, w2), BF),
             pltpu.VMEM((2, KS, 2 * QS), BF),
             pltpu.VMEM((2, KS, 2 * QS), BF),
+            pltpu.VMEM((KS, 2 * QS), BF),
+            pltpu.VMEM((KS, 2 * QS), BF),
             pltpu.VMEM((2, 8, PQ), F32),
+            pltpu.VMEM((8, PQ), F32),
             pltpu.VMEM((8, PQ), F32),
             pltpu.VMEM((NC, 2, 8, PQ), F32),
             pltpu.VMEM((NC, NM - 1, 2, 8, PQ), F32),
@@ -490,8 +475,8 @@
             pltpu.VMEM((NC, 2, 2 * BS, w2), F32),
             pltpu.VMEM((NC, 2, 2 * BS, w2), BF),
             pltpu.VMEM((NC, 2, 2 * BS, w2), BF),
-            pltpu.VMEM((NC // 2, NP, 4, 16, w2), BF),
-            pltpu.VMEM((NC // 2, NP - 1, 4, 16, w2), BF),
+            pltpu.VMEM((NC, NP, 2, 16, w2), BF),
+            pltpu.VMEM((NC, NP - 1, 2, 16, w2), BF),
             dma((6 + NM,)),
             dma((2, 2)),
             dma((2, NC)),
@@ -499,7 +484,7 @@
             dma((2, NC, 2)),
             dma((2, NC)),
             dma((2, NC)),
-            dma((2, NC // 2)),
+            dma((2, NC)),
         ],
         compiler_params=pltpu.CompilerParams(
             collective_id=0, has_side_effects=True, vmem_limit_bytes=60 * 1024 * 1024

time: 55.2 us -> 55.2 us (level)
  no operation moved by 1% of the time
where the time goes in v12:
time: 55.2 us; the launch traced here: 55.1 us
  Pallas kernels  54.4 us (99%)
  between operations  0.64 us (1%)
    pallas_call x1, Pallas kernels, local(): pl.pallas_call(kernel, out_shape=out_shape, in_specs=[hbm] * 7, out_specs...  52.6 us
    pallas_call x1, Pallas kernels, local(): pl.pallas_call(write_out, out_shape=out_shape, in_specs=[vmem] * 4, out_s...  1.78 us

profile of v12, /device:TPU:2, one launch (start us, length us, event | category | flops | bytes accessed | tf_op | source)
XLA Modules:
  0.0 55.1 jit_solution(7682977587796274771)
XLA Ops:
  0.6 52.6 %sparse_attention.1 = (bf16[1,128,512]{2,1,0:T(8,128)(2,1)}, f32[1,128,512]{2,1,0:T(8,128)}, f32[2,8,512]{2,1,0:T(8,128)}, f32[2,8,512]{2,1,0:T(8,128)}) custom-call(bf16[2048,512]{1,0:T(8,128)(2,1)} %queries.1, s32[1,2048]{1,0:T(1,128)} %order.1, bf16[2,128,512]{2,1,0:T(8,128)(2,1)} %keys.1, bf16[2,128,512]{2,1,0:T(8,128)(2,1)} %values.1, s32[1,16]{1,0:T(1,128)} %counts.1, ...), custom_call_target="tpu_custom_call" | custom-call | tf_op jit(solution)/shard_map/sparse_attention/pallas_call | solution.py:442
  53.3 1.8 %write_out.1 = (bf16[1,128,512]{2,1,0:T(8,128)(2,1)}, f32[1,128,512]{2,1,0:T(8,128)}, f32[2,8,512]{2,1,0:T(8,128)}, f32[2,8,512]{2,1,0:T(8,128)}) custom-call(bf16[1,128,512]{2,1,0:T(8,128)(2,1)} %get-tuple-element.8.refs_0_, f32[1,128,512]{2,1,0:T(8,128)} %get-tuple-element.9.refs_1_, f32[2,8,512]{2,1,0:T(8,128)} %get-tuple-element.10.refs_2_, ...), custom_call_target="tpu_custom_call" | custom-call | tf_op jit(solution)/shard_map/write_out/pallas_call | solution.py:494

commit v13 on v12

--- a/solution.py
+++ b/solution.py
@@ -71,6 +71,7 @@
     stat_got,
     aq,
     x1_got,
+    near_got,
     x2_got,
     y_keep,
     y_send,
@@ -84,6 +85,7 @@
     kv_sem,
     stat_sem,
     x1_sem,
+    near_sem,
     x2_sem,
     y_sem,
     c_sem,
@@ -302,7 +304,7 @@
                 x, y = b % NX, b // NX
                 aq[hp, x, y, 0] = att[e * BS:(e + 1) * BS]
                 aq[hp, x, y, 1] = dq[e * BS:(e + 1) * BS]
-        for cp in x1_copies(hp):
+        for cp in x1_copies(hp, 0) + x1_copies(hp, 1) + near_copies(hp):
             cp.start()
         dk = (dot(dss[...], q_m[par]) * SCALE).reshape(2, 2 * BS, 2 * HD)
         dv = dot(qs[...], og_m[par]).reshape(2, 2 * BS, 2 * HD)
@@ -313,20 +315,32 @@
         c_send[hp, 1] = jnp.where(mine, dv[1], dv[0]).astype(BF)
         c_copy(hp).start()
 
-    def x1_copies(hp):
-        return (
-            send(aq.at[hp, xo, 0], x1_got.at[hp, 0], x1_sem.at[0, hp, 0], x1_sem.at[1, hp, 0], right),
-            send(aq.at[hp, xo, 1], x1_got.at[hp, 1], x1_sem.at[0, hp, 1], x1_sem.at[1, hp, 1], left),
+    def x1_copies(hp, kind):
+        return tuple(
+            send(
+                aq.at[hp, xo, way, kind], x1_got.at[hp, way, kind],
+                x1_sem.at[0, hp, way, kind], x1_sem.at[1, hp, way, kind], (right, left)[way],
+            ) for way in range(2)
         )
 
-    def x2_copies(hp):
-        return (
-            send(aq.at[hp, xr], x2_got.at[hp, 0], x2_sem.at[0, hp, 0], x2_sem.at[1, hp, 0], right),
-            send(aq.at[hp, xl], x2_got.at[hp, 1], x2_sem.at[0, hp, 1], x2_sem.at[1, hp, 1], left),
+    def near_copies(hp):
+        return tuple(
+            send(
+                aq.at[hp, (xr, xl)[way], 1 - way], near_got.at[hp, way],
+                near_sem.at[0, hp, way], near_sem.at[1, hp, way], (right, left)[way],
+            ) for way in range(2)
         )
 
-    def y_copy(hp):
-        return send(y_send.at[hp], y_got.at[hp], y_sem.at[0, hp], y_sem.at[1, hp], across)
+    def x2_copies(hp, kind):
+        return tuple(
+            send(
+                aq.at[hp, (xr, xl)[way], way, kind], x2_got.at[hp, way, kind],
+                x2_sem.at[0, hp, way, kind], x2_sem.at[1, hp, way, kind], (right, left)[way],
+            ) for way in range(2)
+        )
+
+    def y_copy(hp, kind):
+        return send(y_send.at[hp, kind], y_got.at[hp, kind], y_sem.at[0, hp, kind], y_sem.at[1, hp, kind], across)
 
     def c_copy(hp):
         return send(c_send.at[hp], c_got.at[hp], c_sem.at[0, hp], c_sem.at[1, hp], mate)
@@ -335,12 +349,15 @@
         return send(z_got.at[hp], z_got.at[hp], z_sem.at[0, hp], z_sem.at[1, hp], slab(1))
 
     def relay_x(hp):
-        for cp in x1_copies(hp):
-            cp.wait_recv()
-        aq[hp, xr, 0] = (aq[hp, xr, 0].astype(F32) + x1_got[hp, 0].astype(F32)).astype(BF)
-        aq[hp, xl, 1] = (aq[hp, xl, 1].astype(F32) + x1_got[hp, 1].astype(F32)).astype(BF)
-        for cp in x2_copies(hp):
-            cp.start()
+        for kind in range(2):
+            for cp in x1_copies(hp, kind):
+                cp.wait_recv()
+            for way, x in ((0, xr), (1, xl)):
+                aq[hp, x, way, kind] = (
+                    aq[hp, x, way, kind].astype(F32) + x1_got[hp, way, kind].astype(F32)
+                ).astype(BF)
+            for cp in x2_copies(hp, kind):
+                cp.start()
 
     def relay_c(hp):
         c_copy(hp).wait_recv()
@@ -359,19 +376,21 @@
         lax.fori_loop(1, NP, share, 0)
 
     def relay_y(hp):
-        for cp in x2_copies(hp):
+        for cp in near_copies(hp):
             cp.wait_recv()
-
-        def total(y):
-            return (
-                aq[hp, xi, y].astype(F32)
-                + x2_got[hp, 0, y].astype(F32)
-                + x2_got[hp, 1, y].astype(F32)
+        low = yi == 0
+        for kind in range(2):
+            for cp in x2_copies(hp, kind):
+                cp.wait_recv()
+            t0, t1 = (
+                aq[hp, xi, y, kind].astype(F32)
+                + x2_got[hp, y, kind].astype(F32)
+                + near_got[hp, 1 - y, kind].astype(F32)
+                for y in range(NY)
             )
-
-        y_send[hp] = total(yo).astype(BF)
-        y_copy(hp).start()
-        y_keep[hp] = total(yi)
+            y_send[hp, kind] = jnp.where(low, t1, t0).astype(BF)
+            y_copy(hp, kind).start()
+            y_keep[hp, kind] = jnp.where(low, t0, t1)
 
     def finish(hp):
         cols = lanes_of(hp)
@@ -381,14 +400,16 @@
             for d in range(NP - 1):
                 total = total + z_got[hp, d, a].astype(F32)
             out[:, :, cols] = total.reshape(2, 8, 2 * HD)
-        y_copy(hp).wait_recv()
-        both = y_keep[hp] + y_got[hp].astype(F32)
-        att_out[0, :, cols] = both[0].astype(BF)
-        qg_out[0, :, cols] = both[1]
+        for kind, out in ((0, att_out), (1, qg_out)):
+            y_copy(hp, kind).wait_recv()
+            out[0, :, cols] = (y_keep[hp, kind] + y_got[hp, kind].astype(F32)).astype(out.dtype)
         stat_all(hp).wait_send()
-        for cp in x1_copies(hp) + x2_copies(hp):
+        for kind in range(2):
+            for cp in x1_copies(hp, kind) + x2_copies(hp, kind):
+                cp.wait_send()
+            y_copy(hp, kind).wait_send()
+        for cp in near_copies(hp):
             cp.wait_send()
-        y_copy(hp).wait_send()
         c_copy(hp).wait_send()
         z_all(hp).wait_send()
 
@@ -404,11 +425,14 @@
         @pl.when((s >= 2) & (s < NC + 2))
         def _():
             relay_x(s - 2)
+
+        @pl.when((s >= 3) & (s < NC + 3))
+        def _():
+            relay_y(s - 3)
+
+        @pl.when((s >= 2) & (s < NC + 2))
+        def _():
             relay_c(s - 2)
-
-        @pl.when((s >= 3) & (s < NC + 3))
-        def _():
-            relay_y(s - 3)
 
         @pl.when(s >= 4)
         def _():
@@ -468,7 +492,8 @@
             pltpu.VMEM((NC, NM - 1, 2, 8, PQ), F32),
             pltpu.VMEM((NC, NX, NY, 2, BS, w2), BF),
             pltpu.VMEM((NC, 2, 2, BS, w2), BF),
-            pltpu.VMEM((NC, 2, NY, 2, BS, w2), BF),
+            pltpu.VMEM((NC, 2, 2, BS, w2), BF),
+            pltpu.VMEM((NC, 2, 2, BS, w2), BF),
             pltpu.VMEM((NC, 2, BS, w2), F32),
             pltpu.VMEM((NC, 2, BS, w2), BF),
             pltpu.VMEM((NC, 2, BS, w2), BF),
@@ -480,9 +505,10 @@
             dma((6 + NM,)),
             dma((2, 2)),
             dma((2, NC)),
+            dma((2, NC, 2, 2)),
             dma((2, NC, 2)),
+            dma((2, NC, 2, 2)),
             dma((2, NC, 2)),
-            dma((2, NC)),
             dma((2, NC)),
             dma((2, NC)),
         ],

time: 55.2 us -> 54.2 us (0.982)
  Pallas kernels: 54.4 us -> 52.9 us
    pallas_call x1, Pallas kernels: 52.6 us -> 51.1 us  [local(): pl.pallas_call(kernel, out_shape=out_shape, in_specs=[hbm] * 7, out_specs...]
where the time goes in v13:
time: 54.2 us; the launch traced here: 53.5 us
  Pallas kernels  52.9 us (98%)
  between operations  0.64 us (1%)
    pallas_call x1, Pallas kernels, local(): pl.pallas_call(kernel, out_shape=out_shape, in_specs=[hbm] * 7, out_specs...  51.1 us
    pallas_call x1, Pallas kernels, local(): pl.pallas_call(write_out, out_shape=out_shape, in_specs=[vmem] * 4, out_s...  1.78 us

profile of v13, /device:TPU:2, one launch (start us, length us, event | category | flops | bytes accessed | tf_op | source)
XLA Modules:
  0.0 53.5 jit_solution(8844705371181047322)
XLA Ops:
  0.6 51.1 %sparse_attention.1 = (bf16[1,128,512]{2,1,0:T(8,128)(2,1)}, f32[1,128,512]{2,1,0:T(8,128)}, f32[2,8,512]{2,1,0:T(8,128)}, f32[2,8,512]{2,1,0:T(8,128)}) custom-call(bf16[2048,512]{1,0:T(8,128)(2,1)} %queries.1, s32[1,2048]{1,0:T(1,128)} %order.1, bf16[2,128,512]{2,1,0:T(8,128)(2,1)} %keys.1, bf16[2,128,512]{2,1,0:T(8,128)(2,1)} %values.1, s32[1,16]{1,0:T(1,128)} %counts.1, ...), custom_call_target="tpu_custom_call" | custom-call | tf_op jit(solution)/shard_map/sparse_attention/pallas_call | solution.py:466
  51.7 1.8 %write_out.1 = (bf16[1,128,512]{2,1,0:T(8,128)(2,1)}, f32[1,128,512]{2,1,0:T(8,128)}, f32[2,8,512]{2,1,0:T(8,128)}, f32[2,8,512]{2,1,0:T(8,128)}) custom-call(bf16[1,128,512]{2,1,0:T(8,128)(2,1)} %get-tuple-element.8.refs_0_, f32[1,128,512]{2,1,0:T(8,128)} %get-tuple-element.9.refs_1_, f32[2,8,512]{2,1,0:T(8,128)} %get-tuple-element.10.refs_2_, ...), custom_call_target="tpu_custom_call" | custom-call | tf_op jit(solution)/shard_map/write_out/pallas_call | solution.py:520

commit v14 on v13

--- a/solution.py
+++ b/solution.py
@@ -271,6 +271,8 @@
     def second(hp):
         par = lax.rem(hp, 2)
         cols = lanes_of(hp)
+        split_heads(kv[0, :, :, cols].reshape(KS, 2 * HD), k_m, KS)
+        split_heads(kv[1, :, :, cols].reshape(KS, 2 * HD), v_m, KS)
         stat_all(hp).wait_recv()
         lse = [stat_own[hp, 0]] + [stat_got[hp, d, 0] for d in range(NM - 1)]
         dlt = [stat_own[hp, 1]] + [stat_got[hp, d, 1] for d in range(NM - 1)]
@@ -280,8 +282,6 @@
         delta_all = functools.reduce(jnp.add, [w * v for w, v in zip(ws, dlt)]) / total
         w_all[...] = jnp.exp2(m_keep[par] - (top + jnp.log2(total)))
         d_keep[...] = delta_all
-        split_heads(kv[0, :, :, cols].reshape(KS, 2 * HD), k_m, KS)
-        split_heads(kv[1, :, :, cols].reshape(KS, 2 * HD), v_m, KS)
 
         for p in range(NM // 2):
             att = jnp.zeros((PQ, 2 * HD), F32)
@@ -424,15 +424,15 @@
 
         @pl.when((s >= 2) & (s < NC + 2))
         def _():
+            relay_c(s - 2)
+
+        @pl.when((s >= 2) & (s < NC + 2))
+        def _():
             relay_x(s - 2)
 
         @pl.when((s >= 3) & (s < NC + 3))
         def _():
             relay_y(s - 3)
-
-        @pl.when((s >= 2) & (s < NC + 2))
-        def _():
-            relay_c(s - 2)
 
         @pl.when(s >= 4)
         def _():

time: 54.2 us -> 54.4 us (level)
  the two profiles are of different devices: /device:TPU:2 before, /device:TPU:1 now
where the time goes in v14:
time: 54.4 us; the launch traced here: 54.2 us
  Pallas kernels  53.6 us (99%)
  between operations  0.64 us (1%)
    pallas_call x1, Pallas kernels, local(): pl.pallas_call(kernel, out_shape=out_shape, in_specs=[hbm] * 7, out_specs...  51.8 us
    pallas_call x1, Pallas kernels, local(): pl.pallas_call(write_out, out_shape=out_shape, in_specs=[vmem] * 4, out_s...  1.78 us

profile of v14, /device:TPU:1, one launch (start us, length us, event | category | flops | bytes accessed | tf_op | source)
XLA Modules:
  0.0 54.2 jit_solution(9436628002003354819)
XLA Ops:
  0.6 51.8 %sparse_attention.1 = (bf16[1,128,512]{2,1,0:T(8,128)(2,1)}, f32[1,128,512]{2,1,0:T(8,128)}, f32[2,8,512]{2,1,0:T(8,128)}, f32[2,8,512]{2,1,0:T(8,128)}) custom-call(bf16[2048,512]{1,0:T(8,128)(2,1)} %queries.1, s32[1,2048]{1,0:T(1,128)} %order.1, bf16[2,128,512]{2,1,0:T(8,128)(2,1)} %keys.1, bf16[2,128,512]{2,1,0:T(8,128)(2,1)} %values.1, s32[1,16]{1,0:T(1,128)} %counts.1, ...), custom_call_target="tpu_custom_call" | custom-call | tf_op jit(solution)/shard_map/sparse_attention/pallas_call | solution.py:466
  52.5 1.8 %write_out.1 = (bf16[1,128,512]{2,1,0:T(8,128)(2,1)}, f32[1,128,512]{2,1,0:T(8,128)}, f32[2,8,512]{2,1,0:T(8,128)}, f32[2,8,512]{2,1,0:T(8,128)}) custom-call(bf16[1,128,512]{2,1,0:T(8,128)(2,1)} %get-tuple-element.8.refs_0_, f32[1,128,512]{2,1,0:T(8,128)} %get-tuple-element.9.refs_1_, f32[2,8,512]{2,1,0:T(8,128)} %get-tuple-element.10.refs_2_, ...), custom_call_target="tpu_custom_call" | custom-call | tf_op jit(solution)/shard_map/write_out/pallas_call | solution.py:520

commit v15 on v14

--- a/solution.py
+++ b/solution.py
@@ -215,7 +215,7 @@
         return slice(h * QS + p * PQ, h * QS + (p + 1) * PQ)
 
     def first(hp):
-        par = lax.rem(hp, 2)
+        par = lax.rem(hp, 3)
         cols = lanes_of(hp)
         k2 = kv[0, :, :, cols].reshape(KS, 2 * HD)
         v2 = kv[1, :, :, cols].reshape(KS, 2 * HD)
@@ -269,7 +269,7 @@
         return send(stat_got.at[hp], stat_got.at[hp], stat_sem.at[0, hp], stat_sem.at[1, hp], right)
 
     def second(hp):
-        par = lax.rem(hp, 2)
+        par = lax.rem(hp, 3)
         cols = lanes_of(hp)
         split_heads(kv[0, :, :, cols].reshape(KS, 2 * HD), k_m, KS)
         split_heads(kv[1, :, :, cols].reshape(KS, 2 * HD), v_m, KS)
@@ -418,29 +418,26 @@
         def _():
             first(s)
 
-        @pl.when((s >= 1) & (s < NC + 1))
-        def _():
-            second(s - 1)
-
         @pl.when((s >= 2) & (s < NC + 2))
         def _():
-            relay_c(s - 2)
-
-        @pl.when((s >= 2) & (s < NC + 2))
-        def _():
-            relay_x(s - 2)
+            second(s - 2)
 
         @pl.when((s >= 3) & (s < NC + 3))
         def _():
-            relay_y(s - 3)
-
-        @pl.when(s >= 4)
+            relay_c(s - 3)
+            relay_x(s - 3)
+
+        @pl.when((s >= 4) & (s < NC + 4))
         def _():
-            finish(s - 4)
+            relay_y(s - 4)
+
+        @pl.when(s >= 5)
+        def _():
+            finish(s - 5)
 
         return 0
 
-    lax.fori_loop(0, NC + 4, turn, 0)
+    lax.fori_loop(0, NC + 5, turn, 0)
 
 
 def write_out(*refs):
@@ -477,15 +474,15 @@
             pltpu.VMEM((NM, BS, D), BF),
             pltpu.VMEM((2, 4, BS, D), BF),
             pltpu.VMEM((8, QS), F32),
-            pltpu.VMEM((2, 2 * QS, w2), BF),
-            pltpu.VMEM((2, 2 * QS, w2), BF),
+            pltpu.VMEM((3, 2 * QS, w2), BF),
+            pltpu.VMEM((3, 2 * QS, w2), BF),
             pltpu.VMEM((2 * KS, w2), BF),
             pltpu.VMEM((2 * KS, w2), BF),
-            pltpu.VMEM((2, KS, 2 * QS), BF),
-            pltpu.VMEM((2, KS, 2 * QS), BF),
+            pltpu.VMEM((3, KS, 2 * QS), BF),
+            pltpu.VMEM((3, KS, 2 * QS), BF),
             pltpu.VMEM((KS, 2 * QS), BF),
             pltpu.VMEM((KS, 2 * QS), BF),
-            pltpu.VMEM((2, 8, PQ), F32),
+            pltpu.VMEM((3, 8, PQ), F32),
             pltpu.VMEM((8, PQ), F32),
             pltpu.VMEM((8, PQ), F32),
             pltpu.VMEM((NC, 2, 8, PQ), F32),

time: 54.4 us -> 51.8 us (0.952)
  the two profiles are of different devices: /device:TPU:1 before, /device:TPU:2 now
where the time goes in v15:
time: 51.8 us; the launch traced here: 50.8 us
  Pallas kernels  50.2 us (97%)
  between operations  0.64 us (1%)
    pallas_call x1, Pallas kernels, local(): pl.pallas_call(kernel, out_shape=out_shape, in_specs=[hbm] * 7, out_specs...  48.4 us
    pallas_call x1, Pallas kernels, local(): pl.pallas_call(write_out, out_shape=out_shape, in_specs=[vmem] * 4, out_s...  1.78 us

profile of v15, /device:TPU:2, one launch (start us, length us, event | category | flops | bytes accessed | tf_op | source)
XLA Modules:
  0.0 50.8 jit_solution(10599156452938811588)
XLA Ops:
  0.6 48.4 %sparse_attention.1 = (bf16[1,128,512]{2,1,0:T(8,128)(2,1)}, f32[1,128,512]{2,1,0:T(8,128)}, f32[2,8,512]{2,1,0:T(8,128)}, f32[2,8,512]{2,1,0:T(8,128)}) custom-call(bf16[2048,512]{1,0:T(8,128)(2,1)} %queries.1, s32[1,2048]{1,0:T(1,128)} %order.1, bf16[2,128,512]{2,1,0:T(8,128)(2,1)} %keys.1, bf16[2,128,512]{2,1,0:T(8,128)(2,1)} %values.1, s32[1,16]{1,0:T(1,128)} %counts.1, ...), custom_call_target="tpu_custom_call" | custom-call | tf_op jit(solution)/shard_map/sparse_attention/pallas_call | solution.py:463
  49.0 1.8 %write_out.1 = (bf16[1,128,512]{2,1,0:T(8,128)(2,1)}, f32[1,128,512]{2,1,0:T(8,128)}, f32[2,8,512]{2,1,0:T(8,128)}, f32[2,8,512]{2,1,0:T(8,128)}) custom-call(bf16[1,128,512]{2,1,0:T(8,128)(2,1)} %get-tuple-element.8.refs_0_, f32[1,128,512]{2,1,0:T(8,128)} %get-tuple-element.9.refs_1_, f32[2,8,512]{2,1,0:T(8,128)} %get-tuple-element.10.refs_2_, ...), custom_call_target="tpu_custom_call" | custom-call | tf_op jit(solution)/shard_map/write_out/pallas_call | solution.py:517

commit v16 on v15

--- a/solution.py
+++ b/solution.py
@@ -215,7 +215,7 @@
         return slice(h * QS + p * PQ, h * QS + (p + 1) * PQ)
 
     def first(hp):
-        par = lax.rem(hp, 3)
+        par = hp
         cols = lanes_of(hp)
         k2 = kv[0, :, :, cols].reshape(KS, 2 * HD)
         v2 = kv[1, :, :, cols].reshape(KS, 2 * HD)
@@ -269,7 +269,7 @@
         return send(stat_got.at[hp], stat_got.at[hp], stat_sem.at[0, hp], stat_sem.at[1, hp], right)
 
     def second(hp):
-        par = lax.rem(hp, 3)
+        par = hp
         cols = lanes_of(hp)
         split_heads(kv[0, :, :, cols].reshape(KS, 2 * HD), k_m, KS)
         split_heads(kv[1, :, :, cols].reshape(KS, 2 * HD), v_m, KS)
@@ -418,26 +418,26 @@
         def _():
             first(s)
 
-        @pl.when((s >= 2) & (s < NC + 2))
-        def _():
-            second(s - 2)
-
         @pl.when((s >= 3) & (s < NC + 3))
         def _():
-            relay_c(s - 3)
-            relay_x(s - 3)
+            second(s - 3)
 
         @pl.when((s >= 4) & (s < NC + 4))
         def _():
-            relay_y(s - 4)
-
-        @pl.when(s >= 5)
+            relay_c(s - 4)
+            relay_x(s - 4)
+
+        @pl.when((s >= 5) & (s < NC + 5))
         def _():
-            finish(s - 5)
+            relay_y(s - 5)
+
+        @pl.when(s >= 6)
+        def _():
+            finish(s - 6)
 
         return 0
 
-    lax.fori_loop(0, NC + 5, turn, 0)
+    lax.fori_loop(0, NC + 6, turn, 0)
 
 
 def write_out(*refs):
@@ -474,15 +474,15 @@
             pltpu.VMEM((NM, BS, D), BF),
             pltpu.VMEM((2, 4, BS, D), BF),
             pltpu.VMEM((8, QS), F32),
-            pltpu.VMEM((3, 2 * QS, w2), BF),
-            pltpu.VMEM((3, 2 * QS, w2), BF),
+            pltpu.VMEM((NC, 2 * QS, w2), BF),
+            pltpu.VMEM((NC, 2 * QS, w2), BF),
             pltpu.VMEM((2 * KS, w2), BF),
             pltpu.VMEM((2 * KS, w2), BF),
-            pltpu.VMEM((3, KS, 2 * QS), BF),
-            pltpu.VMEM((3, KS, 2 * QS), BF),
+            pltpu.VMEM((NC, KS, 2 * QS), BF),
+            pltpu.VMEM((NC, KS, 2 * QS), BF),
             pltpu.VMEM((KS, 2 * QS), BF),
             pltpu.VMEM((KS, 2 * QS), BF),
-            pltpu.VMEM((3, 8, PQ), F32),
+            pltpu.VMEM((NC, 8, PQ), F32),
             pltpu.VMEM((8, PQ), F32),
             pltpu.VMEM((8, PQ), F32),
             pltpu.VMEM((NC, 2, 8, PQ), F32),

time: 51.8 us -> 52.8 us (1.019)
  the two profiles are of different devices: /device:TPU:2 before, /device:TPU:1 now
where the time goes in v16:
time: 52.8 us; the launch traced here: 52.7 us
  Pallas kernels  52 us (98%)
  between operations  0.64 us (1%)
    pallas_call x1, Pallas kernels, local(): pl.pallas_call(kernel, out_shape=out_shape, in_specs=[hbm] * 7, out_specs...  50.2 us
    pallas_call x1, Pallas kernels, local(): pl.pallas_call(write_out, out_shape=out_shape, in_specs=[vmem] * 4, out_s...  1.78 us

profile of v16, /device:TPU:1, one launch (start us, length us, event | category | flops | bytes accessed | tf_op | source)
XLA Modules:
  0.0 52.7 jit_solution(2858931086952460162)
XLA Ops:
  0.6 50.2 %sparse_attention.1 = (bf16[1,128,512]{2,1,0:T(8,128)(2,1)}, f32[1,128,512]{2,1,0:T(8,128)}, f32[2,8,512]{2,1,0:T(8,128)}, f32[2,8,512]{2,1,0:T(8,128)}) custom-call(bf16[2048,512]{1,0:T(8,128)(2,1)} %queries.1, s32[1,2048]{1,0:T(1,128)} %order.1, bf16[2,128,512]{2,1,0:T(8,128)(2,1)} %keys.1, bf16[2,128,512]{2,1,0:T(8,128)(2,1)} %values.1, s32[1,16]{1,0:T(1,128)} %counts.1, ...), custom_call_target="tpu_custom_call" | custom-call | tf_op jit(solution)/shard_map/sparse_attention/pallas_call | solution.py:463
  50.9 1.8 %write_out.1 = (bf16[1,128,512]{2,1,0:T(8,128)(2,1)}, f32[1,128,512]{2,1,0:T(8,128)}, f32[2,8,512]{2,1,0:T(8,128)}, f32[2,8,512]{2,1,0:T(8,128)}) custom-call(bf16[1,128,512]{2,1,0:T(8,128)(2,1)} %get-tuple-element.8.refs_0_, f32[1,128,512]{2,1,0:T(8,128)} %get-tuple-element.9.refs_1_, f32[2,8,512]{2,1,0:T(8,128)} %get-tuple-element.10.refs_2_, ...), custom_call_target="tpu_custom_call" | custom-call | tf_op jit(solution)/shard_map/write_out/pallas_call | solution.py:517
